TPU v7x, 32 devices: a whole 2x2x4 slice. The times are simulated.
32 devices in a mesh: gx: 4 (over y, core), gy: 8 (over z, x).
Axes of the slice: x: 2, y: 2, z: 4, core: 2. Of those that a mesh axis runs over, the one named last changes fastest.
Arguments:
- reference_image: bfloat16 [64, 64, 1024], P(None, 'gx', 'gy'), may hold values from -8 to 8
- deformed_image: bfloat16 [64, 64, 1024], P(None, 'gx', 'gy'), may hold values from -8 to 8
- route: int32 [4, 8, 32, 1], P('gx', 'gy'), may hold values from 0 to 4; in each aligned block of 32 rows (0 to 31, 32 to 63, ..., all dimensions but the last counted through in order) at most 8 rows name the same one
- within: int32 [4, 8, 32], P('gx', 'gy'), may hold values from 0 to 7
- xshift: int32 [4, 8, 32], P('gx', 'gy'), may hold values from 0 to 2
- fractions: int32 [4, 8, 32, 3], P('gx', 'gy'), may hold values from 0 to 15
Outputs:
- increment: float32 [3, 5, 4, 64], P(None, None, 'gx', 'gy')
- mismatch: float32 [64, 64, 1024], P(None, 'gx', 'gy')
Inputs may be any that keep to these rules, and one draw needn't show every extreme that they name: `route`: among the 32 rows of one device (aligned blocks of rows along the first three dimensions taken together) no value occurs more than 8 times, and some value occurs exactly 8 times.
All inputs are finite; a program needn't handle non-finite values.
Results may differ from a plain program's by a relative error of at most 0.0006.
Values may be sent and summed in bfloat16 or wider, within the bound.
No kernel may reach another device: no remote copies, remote signals or barrier semaphores. Data moves between devices by JAX's collectives and lax.ppermute only.
A program may use at most 64 MiB of HBM per device.

v0:
```python
import jax
import jax.numpy as jnp
from jax import lax
from jax.sharding import PartitionSpec as P

EDGE = 16
EZ = 4
EXD = 1
EYD = 8
SPAN = 2
ITERS = 3
NEL = 32
VOL = 4096


LAMBDA = 0.05


def from_behind(array, axis, by):
    size = lax.axis_size(axis)
    pairs = [(i, i + by) for i in range(size) if 0 <= i + by < size]
    return lax.ppermute(array, axis, pairs)


def padded_2(block, sides, width):
    for axis, dim in sides:
        count = lax.axis_size(axis)
        forward = [(i, i + 1) for i in range(count - 1)]
        backward = [(target, source) for source, target in forward]
        low = lax.ppermute(
            lax.slice_in_dim(block, block.shape[dim] - width, None, axis=dim), axis, forward
        )
        high = lax.ppermute(lax.slice_in_dim(block, 0, width, axis=dim), axis, backward)
        block = jnp.concatenate([low, block, high], axis=dim)
    return block


def passed_along(block, axis, distance):
    devices = range(lax.axis_size(axis))
    route = [((i - distance) % len(devices), i) for i in devices]
    return lax.ppermute(block, axis, route)


def hat_positions(brick_edge, trailing):
    positions = (jnp.arange(brick_edge, dtype=jnp.float32) + 0.5) / brick_edge
    return positions.reshape((brick_edge,) + (1,) * trailing)


def spread_along(node_values, which_axis, brick_edge):
    node_count = node_values.shape[which_axis] - 1
    positions = hat_positions(brick_edge, node_values.ndim - which_axis - 1)
    lower_part = jnp.expand_dims(
        lax.slice_in_dim(node_values, 0, node_count, axis=which_axis), which_axis + 1
    )
    upper_part = jnp.expand_dims(
        lax.slice_in_dim(node_values, 1, node_count + 1, axis=which_axis), which_axis + 1
    )
    blended = lower_part * (1.0 - positions) + upper_part * positions
    new_shape = (
        node_values.shape[:which_axis]
        + (node_count * brick_edge,)
        + node_values.shape[which_axis + 1 :]
    )
    return blended.reshape(new_shape)


def collect_along(voxel_values, which_axis, brick_edge):
    node_count = voxel_values.shape[which_axis] // brick_edge
    positions = hat_positions(brick_edge, voxel_values.ndim - which_axis - 1)
    blocks = voxel_values.reshape(
        voxel_values.shape[:which_axis]
        + (node_count, brick_edge)
        + voxel_values.shape[which_axis + 1 :]
    )
    lower_part = jnp.sum(blocks * (1.0 - positions), axis=which_axis + 1)
    upper_part = jnp.sum(blocks * positions, axis=which_axis + 1)
    zero_cap = jnp.zeros_like(lax.slice_in_dim(lower_part, 0, 1, axis=which_axis))
    return jnp.concatenate([lower_part, zero_cap], which_axis) + jnp.concatenate(
        [zero_cap, upper_part], which_axis
    )


def clamp_shift(bricks, stride):
    advanced = jnp.concatenate([bricks[:, stride:], bricks[:, -stride:]], axis=1)
    places = jnp.arange(bricks.shape[1], dtype=jnp.int32)
    at_rim = places // stride % EDGE == EDGE - 1
    return jnp.where(at_rim[None, :], bricks, advanced)


def warp_bricks(bricks, fractions):
    weights = fractions.astype(jnp.float32) / EDGE
    blended = bricks
    for column, stride in ((2, 1), (1, EDGE), (0, EDGE * EDGE)):
        portion = weights[:, column : column + 1]
        blended = (1.0 - portion) * blended + portion * clamp_shift(blended, stride)
    return blended


def local_bricks(image, depth_count, width_count, height_count):
    shaped = image.reshape(depth_count, EDGE, width_count, EDGE, height_count, EDGE)
    return shaped.transpose(0, 2, 4, 1, 3, 5).reshape(depth_count * width_count * height_count, VOL)


def settle_faces(partial_value):
    upper_rim = partial_value[:, :, -1, :]
    arrived = from_behind(upper_rim, "gx", 1)
    interior = partial_value[:, :, :-1, :].at[:, :, 0, :].add(arrived)
    side_rim = interior[:, :, :, -1]
    arrived_side = from_behind(side_rim, "gy", 1)
    return interior[:, :, :, :-1].at[:, :, :, 0].add(arrived_side)


def reach_faces(unknown):
    next_row = from_behind(unknown, "gx", -1)
    wider = jnp.concatenate([unknown, next_row], axis=2)
    next_column = from_behind(wider[:, :, :, :1], "gy", -1)
    return jnp.concatenate([wider, next_column], axis=3)


def restrict(voxel_terms):
    partial_value = collect_along(
        collect_along(collect_along(voxel_terms, 1, EDGE), 2, EDGE), 3, EDGE
    )
    return settle_faces(partial_value) / VOL


def squared(vector):
    return lax.psum(jnp.sum(vector * vector), ("gx", "gy"))


def body(reference_image, deformed_image, route, within, xshift, fractions):
    column_x = lax.axis_index("gx")
    width_devices = lax.axis_size("gx")
    offsets = route.reshape(NEL) - SPAN
    within_rows = within.reshape(NEL)
    shift_rows = xshift.reshape(NEL)
    weights_rows = fractions.reshape(NEL, 3)
    element = jnp.arange(NEL, dtype=jnp.int32)
    depth_rows = element // (EXD * EYD)
    across = element // EYD % EXD
    global_x = column_x * EXD + across
    source_x = jnp.clip(global_x + shift_rows - 1, 0, EXD * width_devices - 1)
    local_x = source_x - column_x * EXD + 1
    source_index = (depth_rows * (EXD + 2) + local_x) * EYD + within_rows
    extended = padded_2(deformed_image, (("gx", 1),), EDGE)
    wide_rows = local_bricks(extended, EZ, EXD + 2, EYD)
    fetched = jnp.take(wide_rows, source_index, axis=0)
    for distance in range(-SPAN, SPAN + 1):
        if distance != 0:
            window = passed_along(wide_rows, "gy", -distance)
            picked = jnp.take(window, source_index, axis=0)
            fetched = jnp.where((offsets == distance)[:, None], picked, fetched)
    warped = warp_bricks(fetched.astype(jnp.float32), weights_rows)
    reference_rows = local_bricks(reference_image, EZ, EXD, EYD)
    mismatch_rows = reference_rows.astype(jnp.float32) - warped
    mismatch = (
        mismatch_rows.reshape(EZ, EXD, EYD, EDGE, EDGE, EDGE)
        .transpose(0, 3, 1, 4, 2, 5)
        .reshape(reference_image.shape)
    )
    padded = padded_2(reference_image, (("gx", 1), ("gy", 2)), 1)
    padded = jnp.pad(padded, ((1, 1), (0, 0), (0, 0)))
    middle = padded[1:-1].astype(jnp.float32)
    along_z = (
        padded[2:, 1:-1, 1:-1].astype(jnp.float32) - padded[:-2, 1:-1, 1:-1].astype(jnp.float32)
    ) * 0.5
    along_x = (middle[:, 2:, 1:-1] - middle[:, :-2, 1:-1]) * 0.5
    along_y = (middle[:, 1:-1, 2:] - middle[:, 1:-1, :-2]) * 0.5
    gradient = jnp.stack([along_z, along_x, along_y]).astype(jnp.bfloat16)
    residual = restrict(gradient.astype(jnp.float32) * mismatch[None])
    increment = jnp.zeros_like(residual)
    direction = residual
    norm_now = squared(residual)
    for iteration in range(ITERS):
        node_values = reach_faces(direction)
        displaced = spread_along(spread_along(spread_along(node_values, 3, EDGE), 2, EDGE), 1, EDGE)
        normal_part = jnp.sum(gradient.astype(jnp.float32) * displaced, axis=0)
        curved = restrict(gradient.astype(jnp.float32) * normal_part[None]) + LAMBDA * direction
        step_size = norm_now / lax.psum(jnp.sum(direction * curved), ("gx", "gy"))
        increment = increment + step_size * direction
        if iteration + 1 < ITERS:
            residual = residual - step_size * curved
            norm_next = squared(residual)
            direction = residual + norm_next / norm_now * direction
            norm_now = norm_next
    return (increment, mismatch)


def solution(mesh):
    placed = (
        P(None, "gx", "gy"),
        P(None, "gx", "gy"),
        P("gx", "gy", None, None),
        P("gx", "gy", None),
        P("gx", "gy", None),
        P("gx", "gy", None, None),
    )
    return jax.shard_map(
        body,
        mesh=mesh,
        in_specs=placed,
        out_specs=(P(None, None, "gx", "gy"), P(None, "gx", "gy")),
        check_vma=False,
    )
```

profile of v0, /device:TPU:0, one launch (start us, length us, event | category | flops | bytes accessed | tf_op | source)
XLA Modules:
  0.0 444.6 jit_solution(454483370333902962)
XLA Ops:
  5.3 5.2 %collective-permute-start = (bf16[64,1,128]{2,1,0:T(2,128)(2,1)S(1)}, bf16[64,1,128]{2,1,0:T(2,128)(2,1)S(1)}, u32[]{:S(2)}, u32[]{:S(2)}) collective-permute-start(bf16[64,1,128]{2,1,0:T(2,128)(2,1)S(1)} %get-tuple-element.145), channel_id=1, source_target_pairs={{0,8},{8,16},{16,24},{1,9},{9,17},{17,25},{2,10},{10,18},{18,26},{... | collective-permute-start | bytes 49160 | tf_op jit(solution)/shard_map/ppermute | solution.py:30
  18.4 5.7 %reshape.640 = bf16[4,16,3,16,8,16]{5,4,3,2,1,0:T(8,128)(2,1)} reshape(bf16[64,48,128]{2,1,0:T(8,128)(2,1)S(1)} %pad_maximum_fusion.2) | data formatting | bytes 1572864 | tf_op jit(solution)/shard_map/reshape | solution.py:100
  24.1 7.2 %copy.179 = bf16[4,16,3,16,8,16]{5,3,1,4,2,0:T(8,128)(2,1)} copy(bf16[4,16,3,16,8,16]{5,4,3,2,1,0:T(8,128)(2,1)} %reshape.640) | data formatting | bytes 1572864 | tf_op jit(solution)/shard_map/reshape | solution.py:100
  31.3 11.6 %reshape.641 = bf16[96,4096]{1,0:T(8,128)(2,1)S(1)} reshape(bf16[4,3,8,16,16,16]{5,4,3,2,1,0:T(8,128)(2,1)} %bitcast.139) | data formatting | bytes 1572864 | tf_op jit(solution)/shard_map/reshape | solution.py:101
  43.0 3.7 collective-permute-start.6
  49.8 3.4 collective-permute-start.2
  53.8 37.3 %collective-permute-done.2 = bf16[64,18,1]{2,1,0:T(8,128)(2,1)S(1)} collective-permute-done((bf16[64,18,1]{2,1,0:T(8,128)(2,1)S(1)}, bf16[64,18,1]{2,1,0:T(8,128)(2,1)S(1)}, u32[]{:S(2)}, u32[]{:S(2)}) %collective-permute-start.2) | collective-permute-done | bytes 2336 | tf_op jit(solution)/shard_map/ppermute | solution.py:30
  95.1 4.9 %copy.181 = f32[4,16,1,16,8,16]{5,3,1,4,0,2:T(8,128)} copy(f32[4,16,1,16,8,16]{5,4,3,1,0,2:T(8,128)} %reshape.660) | data formatting | bytes 1048576 | tf_op jit(solution)/shard_map/convert_element_type | solution.py:155
  100.0 5.4 %reshape.657 = f32[32,4096]{1,0:T(8,128)} reshape(f32[4,1,8,16,16,16]{5,4,3,2,0,1:T(8,128)} %bitcast.161) | data formatting | bytes 1048576 | tf_op jit(solution)/shard_map/convert_element_type | solution.py:155
  105.4 12.6 %collective-permute-done.3 = bf16[64,18,1]{2,1,0:T(8,128)(2,1)} collective-permute-done((bf16[64,18,1]{2,1,0:T(8,128)(2,1)S(1)}, bf16[64,18,1]{2,1,0:T(8,128)(2,1)}, u32[]{:S(2)}, u32[]{:S(2)}) %collective-permute-start.3) | collective-permute-done | bytes 2336 | tf_op jit(solution)/shard_map/ppermute | solution.py:33
  121.2 2.9 gather_fusion
  124.1 2.9 gather_fusion.1
  131.6 2.8 reshape.643
  134.4 6.5 %copy.180 = f32[4,1,8,16,16,16]{5,2,4,3,0,1:T(8,128)} copy(f32[4,1,8,16,16,16]{5,4,3,2,0,1:T(8,128)} %reshape.643) | data formatting | bytes 1048576 | tf_op jit(solution)/shard_map/reshape | solution.py:157
  140.9 3.2 mul.741
  145.1 2.5 collective-permute-start.10
  148.7 6.6 %collective-permute-start.11 = (f32[3,5,1]{1,2,0:T(1,128)S(1)}, f32[3,5,1]{1,2,0:T(1,128)S(1)}, u32[]{:S(2)}, u32[]{:S(2)}) collective-permute-start(f32[3,5,1]{1,2,0:T(1,128)S(1)} %squeeze.25), channel_id=1, source_target_pairs={{0,1},{1,2},{2,3},{3,4},{4,5},{5,6},{6,7},{8,9},{9,10},{10,11},{11... | collective-permute-start | bytes 188 | tf_op jit(solution)/shard_map/ppermute | solution.py:22
  162.0 5.6 %collective-permute-done.13 = f32[3,5,2,1]{3,2,1,0:T(2,128)S(1)} collective-permute-done((f32[3,5,2,1]{3,2,1,0:T(2,128)S(1)}, f32[3,5,2,1]{3,2,1,0:T(2,128)S(1)}, u32[]{:S(2)}, u32[]{:S(2)}) %collective-permute-start.13) | collective-permute-done | bytes 152 | tf_op jit(solution)/shard_map/ppermute | solution.py:22
  169.7 4.8 %collective-permute-start.14 = (f32[3,5,9]{2,0,1:T(4,128)S(1)}, f32[3,5,9]{2,0,1:T(4,128)S(1)}, u32[]{:S(2)}, u32[]{:S(2)}) collective-permute-start(f32[3,5,9]{2,0,1:T(4,128)S(1)} %bitcast.181), channel_id=1, source_target_pairs={{0,8},{8,16},{16,24},{1,9},{9,17},{17,25},{2,10},{10,18},{18,26},{... | collective-permute-start | bytes 1628 | tf_op jit(solution)/shard_map/ppermute | solution.py:22
  175.6 5.1 %collective-permute-start.15 = (f32[3,5,1]{1,2,0:T(1,128)S(1)}, f32[3,5,1]{1,2,0:T(1,128)S(1)}, u32[]{:S(2)}, u32[]{:S(2)}) collective-permute-start(f32[3,5,1]{1,2,0:T(1,128)S(1)} %squeeze.27), channel_id=1, source_target_pairs={{0,1},{1,2},{2,3},{3,4},{4,5},{5,6},{6,7},{8,9},{9,10},{10,11},{11... | collective-permute-start | bytes 188 | tf_op jit(solution)/shard_map/ppermute | solution.py:22
  182.9 43.8 %all-reduce.25 = (f32[]{:T(128)}, f32[]{:T(128)}) all-reduce(f32[]{:T(128)} %get-tuple-element.130, f32[]{:T(128)} %get-tuple-element.129), channel_id=1, replica_groups=mesh['gx'=4,'gy'=8] {'gx','gy'}, use_global_device_ids=true, to_apply=%region_7.9 | all-reduce | flops 2 | bytes 16 | tf_op jit(solution)/shard_map/psum | solution.py:128
  228.7 40.2 %psum.44 = f32[]{:T(128)} all-reduce(f32[]{:T(128)} %get-tuple-element.135), channel_id=1, replica_groups=mesh['gx'=4,'gy'=8] {'gx','gy'}, use_global_device_ids=true, to_apply=%region_18.20 | all-reduce | flops 1 | bytes 8 | tf_op jit(solution)/shard_map/psum | solution.py:128
  274.7 4.6 %collective-permute-done.17 = f32[3,5,2,1]{3,2,1,0:T(2,128)S(1)} collective-permute-done((f32[3,5,2,1]{3,2,1,0:T(2,128)S(1)}, f32[3,5,2,1]{3,2,1,0:T(2,128)S(1)}, u32[]{:S(2)}, u32[]{:S(2)}) %collective-permute-start.17) | collective-permute-done | bytes 152 | tf_op jit(solution)/shard_map/ppermute | solution.py:22
  281.3 3.2 collective-permute-start.18
  285.6 3.0 collective-permute-start.19
  290.9 43.4 %psum.45 = f32[]{:T(128)} all-reduce(f32[]{:T(128)} %multiply_reduce_fusion.18), channel_id=1, replica_groups=mesh['gx'=4,'gy'=8] {'gx','gy'}, use_global_device_ids=true, to_apply=%region_27.29 | all-reduce | flops 1 | bytes 8 | tf_op jit(solution)/shard_map/psum | solution.py:179
  336.3 40.2 %psum.46 = f32[]{:T(128)} all-reduce(f32[]{:T(128)} %get-tuple-element.133), channel_id=1, replica_groups=mesh['gx'=4,'gy'=8] {'gx','gy'}, use_global_device_ids=true, to_apply=%region_29.31 | all-reduce | flops 1 | bytes 8 | tf_op jit(solution)/shard_map/psum | solution.py:128
  382.2 4.6 %collective-permute-done.21 = f32[3,5,2,1]{3,2,1,0:T(2,128)S(1)} collective-permute-done((f32[3,5,2,1]{3,2,1,0:T(2,128)S(1)}, f32[3,5,2,1]{3,2,1,0:T(2,128)S(1)}, u32[]{:S(2)}, u32[]{:S(2)}) %collective-permute-start.21) | collective-permute-done | bytes 152 | tf_op jit(solution)/shard_map/ppermute | solution.py:22
  388.9 3.2 collective-permute-start.22
  393.2 3.0 collective-permute-start.23
  396.3 3.9 reshape.656
  401.1 41.6 %psum.47 = f32[]{:T(128)} all-reduce(f32[]{:T(128)} %multiply_reduce_fusion.16), channel_id=1, replica_groups=mesh['gx'=4,'gy'=8] {'gx','gy'}, use_global_device_ids=true, to_apply=%region_38.40 | all-reduce | flops 1 | bytes 8 | tf_op jit(solution)/shard_map/psum | solution.py:179
  (228 shorter events, 61.2 us)
Async XLA Ops:
  0.6 16.7 %collective-permute-start.4 = (bf16[64,16,128]{2,1,0:T(8,128)(2,1)}, bf16[64,16,128]{2,1,0:T(8,128)(2,1)S(1)}, u32[]{:S(2)}, u32[]{:S(2)}) collective-permute-start(bf16[64,16,128]{2,1,0:T(8,128)(2,1)} %param.25), channel_id=1, source_target_pairs={{0,8},{8,16},{16,24},{1,9},{9,17},{17,25},{2,10},{10,18},{18,26},{... | collective-permute-start | bytes 786440 | tf_op jit(solution)/shard_map/ppermute | solution.py:30
  3.0 14.4 %collective-permute-start.5 = (bf16[64,16,128]{2,1,0:T(8,128)(2,1)}, bf16[64,16,128]{2,1,0:T(8,128)(2,1)S(1)}, u32[]{:S(2)}, u32[]{:S(2)}) collective-permute-start(bf16[64,16,128]{2,1,0:T(8,128)(2,1)} %param.25), channel_id=1, source_target_pairs={{8,0},{16,8},{24,16},{9,1},{17,9},{25,17},{10,2},{18,10},{26,18},{... | collective-permute-start | bytes 786440 | tf_op jit(solution)/shard_map/ppermute | solution.py:33
  5.3 10.8 %collective-permute-start = (bf16[64,1,128]{2,1,0:T(2,128)(2,1)S(1)}, bf16[64,1,128]{2,1,0:T(2,128)(2,1)S(1)}, u32[]{:S(2)}, u32[]{:S(2)}) collective-permute-start(bf16[64,1,128]{2,1,0:T(2,128)(2,1)S(1)} %get-tuple-element.145), channel_id=1, source_target_pairs={{0,8},{8,16},{16,24},{1,9},{9,17},{17,25},{2,10},{10,18},{18,26},{... | collective-permute-start | bytes 49160 | tf_op jit(solution)/shard_map/ppermute | solution.py:30
  10.5 5.7 %collective-permute-start.1 = (bf16[64,1,128]{2,1,0:T(2,128)(2,1)S(1)}, bf16[64,1,128]{2,1,0:T(2,128)(2,1)S(1)}, u32[]{:S(2)}, u32[]{:S(2)}) collective-permute-start(bf16[64,1,128]{2,1,0:T(2,128)(2,1)S(1)} %get-tuple-element.146), channel_id=1, source_target_pairs={{8,0},{16,8},{24,16},{9,1},{17,9},{25,17},{10,2},{18,10},{26,18},{... | collective-permute-start | bytes 49160 | tf_op jit(solution)/shard_map/ppermute | solution.py:33
  16.2 1.2 copy-start.5
  16.2 1.2 copy-start.7
  43.0 49.6 %copy-start = (bf16[64,16,128]{2,1,0:T(8,128)(2,1)S(1)}, bf16[64,16,128]{2,1,0:T(8,128)(2,1)}, u32[]{:S(2)}) copy-start(bf16[64,16,128]{2,1,0:T(8,128)(2,1)} %param.24) | copy-start | bytes 786436
  43.0 78.2 %collective-permute-start.6 = (bf16[96,4096]{1,0:T(8,128)(2,1)S(1)}, bf16[96,4096]{1,0:T(8,128)(2,1)}, u32[]{:S(2)}, u32[]{:S(2)}) collective-permute-start(bf16[96,4096]{1,0:T(8,128)(2,1)S(1)} %reshape.641), channel_id=1, source_target_pairs={{2,0},{3,1},{4,2},{5,3},{6,4},{7,5},{0,6},{1,7},{10,8},{11,9},{12,... | collective-permute-start | bytes 2359304 | tf_op jit(solution)/shard_map/ppermute | solution.py:41
  46.7 77.4 %collective-permute-start.7 = (bf16[96,4096]{1,0:T(8,128)(2,1)S(1)}, bf16[96,4096]{1,0:T(8,128)(2,1)}, u32[]{:S(2)}, u32[]{:S(2)}) collective-permute-start(bf16[96,4096]{1,0:T(8,128)(2,1)S(1)} %reshape.641), channel_id=1, source_target_pairs={{1,0},{2,1},{3,2},{4,3},{5,4},{6,5},{7,6},{0,7},{9,8},{10,9},{11,1... | collective-permute-start | bytes 2359304 | tf_op jit(solution)/shard_map/ppermute | solution.py:41
  48.0 78.9 %collective-permute-start.8 = (bf16[96,4096]{1,0:T(8,128)(2,1)S(1)}, bf16[96,4096]{1,0:T(8,128)(2,1)S(1)}, u32[]{:S(2)}, u32[]{:S(2)}) collective-permute-start(bf16[96,4096]{1,0:T(8,128)(2,1)S(1)} %reshape.641), channel_id=1, source_target_pairs={{7,0},{0,1},{1,2},{2,3},{3,4},{4,5},{5,6},{6,7},{15,8},{8,9},{9,10... | collective-permute-start | bytes 2359304 | tf_op jit(solution)/shard_map/ppermute | solution.py:41
  48.7 79.7 %collective-permute-start.9 = (bf16[96,4096]{1,0:T(8,128)(2,1)S(1)}, bf16[96,4096]{1,0:T(8,128)(2,1)S(1)}, u32[]{:S(2)}, u32[]{:S(2)}) collective-permute-start(bf16[96,4096]{1,0:T(8,128)(2,1)S(1)} %reshape.641), channel_id=1, source_target_pairs={{6,0},{7,1},{0,2},{1,3},{2,4},{3,5},{4,6},{5,7},{14,8},{15,9},{8,1... | collective-permute-start | bytes 2359304 | tf_op jit(solution)/shard_map/ppermute | solution.py:41
  49.8 41.3 %collective-permute-start.2 = (bf16[64,18,1]{2,1,0:T(8,128)(2,1)S(1)}, bf16[64,18,1]{2,1,0:T(8,128)(2,1)S(1)}, u32[]{:S(2)}, u32[]{:S(2)}) collective-permute-start(bf16[64,18,1]{2,1,0:T(8,128)(2,1)S(1)} %get-tuple-element.143), channel_id=1, source_target_pairs={{0,1},{1,2},{2,3},{3,4},{4,5},{5,6},{6,7},{8,9},{9,10},{10,11},{11... | collective-permute-start | bytes 6920 | tf_op jit(solution)/shard_map/ppermute | solution.py:30
  91.1 26.9 %collective-permute-start.3 = (bf16[64,18,1]{2,1,0:T(8,128)(2,1)S(1)}, bf16[64,18,1]{2,1,0:T(8,128)(2,1)}, u32[]{:S(2)}, u32[]{:S(2)}) collective-permute-start(bf16[64,18,1]{2,1,0:T(8,128)(2,1)S(1)} %get-tuple-element.144), channel_id=1, source_target_pairs={{1,0},{2,1},{3,2},{4,3},{5,4},{6,5},{7,6},{9,8},{10,9},{11,10},{12... | collective-permute-start | bytes 6920 | tf_op jit(solution)/shard_map/ppermute | solution.py:33
  100.0 18.0 %copy-start.6 = (bf16[64,1,128]{2,1,0:T(2,128)(2,1)S(1)}, bf16[64,1,128]{2,1,0:T(2,128)(2,1)}, u32[]{:S(2)}) copy-start(bf16[64,1,128]{2,1,0:T(2,128)(2,1)} %copy-done.5) | copy-start | bytes 49156
  100.0 18.0 %copy-start.8 = (bf16[64,1,128]{2,1,0:T(2,128)(2,1)S(1)}, bf16[64,1,128]{2,1,0:T(2,128)(2,1)}, u32[]{:S(2)}) copy-start(bf16[64,1,128]{2,1,0:T(2,128)(2,1)} %copy-done.7) | copy-start | bytes 49156
  128.4 1.1 copy-start.4
  128.4 1.1 copy-start.15
  128.4 1.1 copy-start.16
  145.1 3.4 collective-permute-start.10
  148.7 7.9 %collective-permute-start.11 = (f32[3,5,1]{1,2,0:T(1,128)S(1)}, f32[3,5,1]{1,2,0:T(1,128)S(1)}, u32[]{:S(2)}, u32[]{:S(2)}) collective-permute-start(f32[3,5,1]{1,2,0:T(1,128)S(1)} %squeeze.25), channel_id=1, source_target_pairs={{0,1},{1,2},{2,3},{3,4},{4,5},{5,6},{6,7},{8,9},{9,10},{10,11},{11... | collective-permute-start | bytes 188 | tf_op jit(solution)/shard_map/ppermute | solution.py:22
  157.1 3.5 collective-permute-start.12
  160.6 7.0 %collective-permute-start.13 = (f32[3,5,2,1]{3,2,1,0:T(2,128)S(1)}, f32[3,5,2,1]{3,2,1,0:T(2,128)S(1)}, u32[]{:S(2)}, u32[]{:S(2)}) collective-permute-start(f32[3,5,2,1]{3,2,1,0:T(2,128)S(1)} %fusion.47), channel_id=1, source_target_pairs={{1,0},{2,1},{3,2},{4,3},{5,4},{6,5},{7,6},{9,8},{10,9},{11,10},{12... | collective-permute-start | bytes 368 | tf_op jit(solution)/shard_map/ppermute | solution.py:22
  169.7 5.7 %collective-permute-start.14 = (f32[3,5,9]{2,0,1:T(4,128)S(1)}, f32[3,5,9]{2,0,1:T(4,128)S(1)}, u32[]{:S(2)}, u32[]{:S(2)}) collective-permute-start(f32[3,5,9]{2,0,1:T(4,128)S(1)} %bitcast.181), channel_id=1, source_target_pairs={{0,8},{8,16},{16,24},{1,9},{9,17},{17,25},{2,10},{10,18},{18,26},{... | collective-permute-start | bytes 1628 | tf_op jit(solution)/shard_map/ppermute | solution.py:22
  175.6 6.4 %collective-permute-start.15 = (f32[3,5,1]{1,2,0:T(1,128)S(1)}, f32[3,5,1]{1,2,0:T(1,128)S(1)}, u32[]{:S(2)}, u32[]{:S(2)}) collective-permute-start(f32[3,5,1]{1,2,0:T(1,128)S(1)} %squeeze.27), channel_id=1, source_target_pairs={{0,1},{1,2},{2,3},{3,4},{4,5},{5,6},{6,7},{8,9},{9,10},{10,11},{11... | collective-permute-start | bytes 188 | tf_op jit(solution)/shard_map/ppermute | solution.py:22
  270.3 3.1 collective-permute-start.16
  273.4 5.9 %collective-permute-start.17 = (f32[3,5,2,1]{3,2,1,0:T(2,128)S(1)}, f32[3,5,2,1]{3,2,1,0:T(2,128)S(1)}, u32[]{:S(2)}, u32[]{:S(2)}) collective-permute-start(f32[3,5,2,1]{3,2,1,0:T(2,128)S(1)} %fusion.46), channel_id=1, source_target_pairs={{1,0},{2,1},{3,2},{4,3},{5,4},{6,5},{7,6},{9,8},{10,9},{11,10},{12... | collective-permute-start | bytes 368 | tf_op jit(solution)/shard_map/ppermute | solution.py:22
  281.3 4.1 collective-permute-start.18
  285.6 4.3 collective-permute-start.19
  377.8 3.1 collective-permute-start.20
  380.9 5.9 %collective-permute-start.21 = (f32[3,5,2,1]{3,2,1,0:T(2,128)S(1)}, f32[3,5,2,1]{3,2,1,0:T(2,128)S(1)}, u32[]{:S(2)}, u32[]{:S(2)}) collective-permute-start(f32[3,5,2,1]{3,2,1,0:T(2,128)S(1)} %fusion.45), channel_id=1, source_target_pairs={{1,0},{2,1},{3,2},{4,3},{5,4},{6,5},{7,6},{9,8},{10,9},{11,10},{12... | collective-permute-start | bytes 368 | tf_op jit(solution)/shard_map/ppermute | solution.py:22
  388.9 4.1 collective-permute-start.22
  393.2 7.0 %collective-permute-start.23 = (f32[3,5,1]{1,2,0:T(1,128)S(1)}, f32[3,5,1]{1,2,0:T(1,128)S(1)}, u32[]{:S(2)}, u32[]{:S(2)}) collective-permute-start(f32[3,5,1]{1,2,0:T(1,128)S(1)} %squeeze.31), channel_id=1, source_target_pairs={{0,1},{1,2},{2,3},{3,4},{4,5},{5,6},{6,7},{8,9},{9,10},{10,11},{11... | collective-permute-start | bytes 188 | tf_op jit(solution)/shard_map/ppermute | solution.py:22
  (14 other events, 12.8 us)
where the time goes:
time: 446 us; the launch traced here: 445 us
  blocking collectives  209 us (47%)
  waiting for transfers between devices  77.4 us (17%)
  local copies, waits for them, and re-layouts  69.5 us (16%)
  starting transfers between devices  60.9 us (14%)
  other arithmetic  19 us (4%)
  between operations  8.49 us (2%)
    psum x3, blocking collectives, squared(): return lax.psum(jnp.sum(vector * vector), ('gx', 'gy'))  124 us
    psum x2, blocking collectives, body(): step_size = norm_now / lax.psum(jnp.sum(direction * curved), ('gx', 'gy'))  85 us
    ppermute x14, starting transfers between devices, from_behind(): return lax.ppermute(array, axis, pairs)  39.3 us
    ppermute x3, waiting for transfers between devices, padded_2(): lax.ppermute(lax.slice_in_dim(block, block.shape[dim] - width, None, axis...  37.3 us
    ppermute x14, waiting for transfers between devices, from_behind(): return lax.ppermute(array, axis, pairs)  27.5 us
    reshape x2, local copies, waits for them, and re-layouts, local_bricks(): image.reshape(depth_count, EDGE, width_count, EDGE, height_count, EDGE)  12.9 us
    convert_element_type x3, local copies, waits for them, and re-layouts, body(): mismatch_rows = reference_rows.astype(jnp.float32) - warped  12.8 us
    ppermute x3, waiting for transfers between devices, padded_2(): lax.ppermute(lax.slice_in_dim(block, 0, width, axis=dim), axis, backward)  12.6 us
  transfers between devices with their start and end apart: 24, of which 15 were waited for; matrix products, arithmetic and copies ran while one was open for 8% of the time, Pallas kernels for 0%

commit v1 on v0

v1 whole, which is shorter than its diff:
```python
import functools

import jax
import jax.numpy as jnp
import numpy as np
from jax import lax
from jax.experimental import pallas as pl
from jax.experimental.pallas import tpu as pltpu
from jax.sharding import PartitionSpec as P

EDGE = 16
EZ = 4
EYD = 8
SPAN = 2
ITERS = 3
NEL = 32
VOL = 4096
NZ = EZ * EDGE
NY = EYD * EDGE
LAMBDA = 0.05

PAIRS = ((0, 0), (0, 1), (0, 2), (1, 1), (1, 2), (2, 2))
HROWS = 56

F32 = jnp.float32
BF16 = jnp.bfloat16

UPPER = (np.arange(EDGE) + 0.5) / EDGE
HAT = np.stack([1.0 - UPPER, UPPER])
PRODUCTS = np.stack([HAT[0] * HAT[0], HAT[0] * HAT[1], HAT[1] * HAT[1]])


def along_y_weights(weights):
    table = np.zeros((EZ, NY, 128), np.float32)
    for group, row in enumerate(weights):
        for ez in range(EZ):
            for ey in range(EYD):
                table[ez, ey * EDGE : (ey + 1) * EDGE, group * NEL + ez * EYD + ey] = row / VOL
    return table


def moment_tables():
    across = np.zeros((HROWS, 18 * EDGE), np.float32)
    for slab in range(18):
        for wx in range(3):
            across[slab * 3 + wx, slab * EDGE : (slab + 1) * EDGE] = PRODUCTS[wx]
    return across, along_y_weights(PRODUCTS)


def load_tables():
    across = np.zeros((16, 6 * EDGE), np.float32)
    for slab in range(6):
        for bx in range(2):
            across[bx * 8 + slab, slab * EDGE : (slab + 1) * EDGE] = HAT[bx]
    single = along_y_weights(HAT)
    along = np.concatenate([single, np.roll(single, 2 * NEL, axis=2)], axis=1)
    return across, along


def exact_dot(a, b):
    return jnp.dot(a, b, precision=lax.Precision.HIGHEST, preferred_element_type=F32)


def lanes(shape):
    return lax.broadcasted_iota(jnp.int32, shape, len(shape) - 1)


def rows_of(shape):
    return lax.broadcasted_iota(jnp.int32, shape, len(shape) - 2)


def even(value):
    return lax.rem(value, 2) == 0


def ask_kernel(gx_count, route, within, xshift, ref, m0, m1, m2, m3, f0, f1, own, place, count):
    gx, gy = lax.axis_index("gx"), lax.axis_index("gy")
    for j in range(5):
        count[j] = 0
    gx_even, gy_even, half_even = even(gx), even(gy), even(gy // 2)
    row, lane = rows_of((8, 128)), lanes((8, 128))

    def visit(e, asked):
        offset = route[e] - SPAN
        moved = jnp.clip(gx + xshift[e] - 1, 0, gx_count - 1) - gx
        ahead = jnp.where(gx_even, 1, 2)
        bank = jnp.where(moved == 0, 0, jnp.where(moved == 1, ahead, 3 - ahead))
        code = bank * NEL + (e // EYD) * EYD + within[e]
        near = jnp.where((offset == 1) == gy_even, 0, 1)
        far = jnp.where((offset == 2) == half_even, 2, 3)
        j = jnp.where(offset == 0, 4, jnp.where(jnp.abs(offset) == 1, near, far))
        slot = count[j]
        count[j] = slot + 1
        place[e] = j * 8 + slot
        return jnp.where((row == j) & (lane == slot), code.astype(F32), asked)

    asked = lax.fori_loop(0, NEL, visit, jnp.zeros((8, 128), F32), unroll=True)
    own[...] = asked
    m2[...] = asked
    m3[...] = asked
    m0[8:, :] = asked
    m1[8:, :] = asked
    image = ref[...]
    first = jnp.where(gy_even, NY - 1, 0)
    wanted = jnp.where(row == 0, first, jnp.where(row == 1, NY - 1 - first, -1))
    pick = (lane == wanted).astype(F32).astype(BF16)
    columns = lax.dot_general(pick, image.reshape(NZ * EDGE, NY), (((1,), (1,)), ((), ())), preferred_element_type=F32)
    for i in range(8):
        m0[i : i + 1, :] = columns[0:1, i * 128 : (i + 1) * 128]
        m1[i : i + 1, :] = columns[1:2, i * 128 : (i + 1) * 128]
    image = image.astype(F32)
    low, high = image[:, 0, :], image[:, EDGE - 1, :]
    f0[...] = jnp.where(gx_even, high, low).astype(BF16)
    f1[...] = jnp.where(gx_even, low, high).astype(BF16)


def ask(route, within, xshift, ref):
    smem = pl.BlockSpec(memory_space=pltpu.SMEM)
    vmem = pl.BlockSpec(memory_space=pltpu.VMEM)
    return pl.pallas_call(
        functools.partial(ask_kernel, lax.axis_size("gx")),
        out_shape=(
            jax.ShapeDtypeStruct((16, 128), F32),
            jax.ShapeDtypeStruct((16, 128), F32),
            jax.ShapeDtypeStruct((8, 128), F32),
            jax.ShapeDtypeStruct((8, 128), F32),
            jax.ShapeDtypeStruct((NZ, NY), BF16),
            jax.ShapeDtypeStruct((NZ, NY), BF16),
            jax.ShapeDtypeStruct((8, 128), F32),
            jax.ShapeDtypeStruct((NEL,), jnp.int32),
        ),
        in_specs=[smem] * 3 + [vmem],
        out_specs=(vmem,) * 7 + (smem,),
        scratch_shapes=[pltpu.SMEM((8,), jnp.int32)],
        name="ask",
    )(route, within, xshift, ref)


def serve_kernel(own, d0, d1, q0, q1, q2, q3, q4, o0, o1, o2, o3, o4, banks, sems):
    copies = [pltpu.make_async_copy(src, banks.at[i], sems.at[i]) for i, src in enumerate((own, d0, d1))]
    for copy in copies:
        copy.start()
    for copy in copies:
        copy.wait()
    lane = lanes((EDGE * EDGE, NY))
    for j, (asked, out) in enumerate(((q0, o0), (q1, o1), (q2, o2), (q3, o3), (q4, o4))):
        line = 8 + j if j < 2 else j

        def visit(slot, packed, asked=asked, line=line):
            code = asked[line, slot].astype(jnp.int32)
            bank, ez, column = code // NEL, lax.rem(code, NEL) // EYD, lax.rem(code, EYD)
            slab = banks[bank, pl.ds(ez * EDGE, EDGE)].reshape(EDGE * EDGE, NY).astype(F32)
            turned = pltpu.roll(slab, lax.rem((slot - column + EYD) * EDGE, NY), 1)
            return jnp.where(lane // EDGE == slot, turned, packed)

        packed = lax.fori_loop(0, 8, visit, jnp.zeros((EDGE * EDGE, NY), F32))
        out[...] = packed.reshape(EDGE, EDGE, NY).astype(BF16)


def serve(own, d0, d1, asked):
    smem = pl.BlockSpec(memory_space=pltpu.SMEM)
    vmem = pl.BlockSpec(memory_space=pltpu.VMEM)
    anywhere = pl.BlockSpec(memory_space=pl.ANY)
    return pl.pallas_call(
        serve_kernel,
        out_shape=(jax.ShapeDtypeStruct((EDGE, EDGE, NY), BF16),) * 5,
        in_specs=[anywhere] * 3 + [smem] * 5,
        out_specs=(vmem,) * 5,
        scratch_shapes=[pltpu.VMEM((3, NZ, EDGE, NY), BF16), pltpu.SemaphoreType.DMA((3,))],
        name="serve",
    )(own, d0, d1, *asked)


def moments_kernel(gy_count, ref, a0, a1, r0, r1, frac, across, along, grad, packed, portions, side, slabs):
    gx, gy = lax.axis_index("gx"), lax.axis_index("gy")
    gx_even, gy_even = even(gx), even(gy)
    side[...] = jnp.zeros((8, NZ * EDGE), F32)
    keep0 = jnp.where(gy_even, gy < gy_count - 1, gy > 0).astype(F32)
    keep1 = jnp.where(gy_even, gy > 0, gy < gy_count - 1).astype(F32)
    for i in range(8):
        side[0:1, i * 128 : (i + 1) * 128] = r0[i : i + 1, :] * keep0
        side[1:2, i * 128 : (i + 1) * 128] = r1[i : i + 1, :] * keep1
    row, lane = rows_of((8, 128)), lanes((8, 128))
    target0 = jnp.where(gy_even, NY - 1, 0)
    spot = jnp.where(row == 0, target0, jnp.where(row == 1, NY - 1 - target0, -1))
    spread = (lane == spot).astype(F32).astype(BF16)
    rim = lax.dot_general(
        side[...].astype(BF16), spread, (((0,), (0,)), ((), ())), preferred_element_type=F32
    ).reshape(NZ, EDGE, NY)
    from0, from1 = a0[...].astype(F32), a1[...].astype(F32)
    before = jnp.where(gx_even, from1, from0)
    after = jnp.where(gx_even, from0, from1)
    total = jnp.zeros((HROWS, 128), F32)
    lane2, row2 = lanes((EDGE, NY)), rows_of((EDGE, NY))
    for ez in range(EZ):
        collected = [[jnp.zeros((EDGE, NY), F32) for _ in range(3)] for _ in PAIRS]
        for k in range(EDGE):
            z = ez * EDGE + k
            plane = ref[z].astype(F32)
            below = ref[z - 1].astype(F32) if z > 0 else jnp.zeros((EDGE, NY), F32)
            above = ref[z + 1].astype(F32) if z + 1 < NZ else jnp.zeros((EDGE, NY), F32)
            rim_z = rim[z]
            nxt = jnp.where(row2 == EDGE - 1, after[z : z + 1, :], pltpu.roll(plane, EDGE - 1, 0))
            prv = jnp.where(row2 == 0, before[z : z + 1, :], pltpu.roll(plane, 1, 0))
            right = jnp.where(lane2 == NY - 1, rim_z, pltpu.roll(plane, NY - 1, 1))
            left = jnp.where(lane2 == 0, rim_z, pltpu.roll(plane, 1, 1))
            rounded = [((above - below) * 0.5).astype(BF16), ((nxt - prv) * 0.5).astype(BF16), ((right - left) * 0.5).astype(BF16)]
            for c in range(3):
                grad[c, z] = rounded[c]
            g = [value.astype(F32) for value in rounded]
            for p, (c, d) in enumerate(PAIRS):
                product = g[c] * g[d]
                for w in range(3):
                    collected[p][w] = collected[p][w] + float(PRODUCTS[w, k]) * product
        for p in range(len(PAIRS)):
            for w in range(3):
                slabs[(p * 3 + w) * EDGE : (p * 3 + w + 1) * EDGE, :] = collected[p][w]
        total = total + exact_dot(exact_dot(across[...], slabs[...]), along[ez])
    packed[...] = pltpu.roll(total, lax.rem(gx, 4) * NEL, 1)
    element, lane_e = rows_of((EYD, 128)), lanes((EYD, 128))
    unfold = (lane_e // EDGE == element).astype(F32).astype(BF16)
    for ez in range(EZ):
        tenths = frac[ez * EYD : (ez + 1) * EYD, :].astype(F32).astype(BF16)
        wide = lax.dot_general(tenths, unfold, (((0,), (0,)), ((), ())), preferred_element_type=F32)
        portions[ez, 0:3, :] = wide * (1.0 / EDGE)


def moments(ref, faces_x, faces_y, fractions):
    across, along = moment_tables()
    vmem = pl.BlockSpec(memory_space=pltpu.VMEM)
    return pl.pallas_call(
        functools.partial(moments_kernel, lax.axis_size("gy")),
        out_shape=(
            jax.ShapeDtypeStruct((3, NZ, EDGE, NY), BF16),
            jax.ShapeDtypeStruct((HROWS, 128), F32),
            jax.ShapeDtypeStruct((EZ, 8, 128), F32),
        ),
        in_specs=[vmem] * 8,
        out_specs=(vmem,) * 3,
        scratch_shapes=[pltpu.VMEM((8, NZ * EDGE), F32), pltpu.VMEM((18 * EDGE, NY), F32)],
        name="moments",
    )(ref, *faces_x, *faces_y, fractions, jnp.asarray(across), jnp.asarray(along))


def warp_kernel(place, b0, b1, b2, b3, b4, ref, grad, portions, across, along, mismatch, packed, bricks, slabs, sems):
    gx = lax.axis_index("gx")
    copies = [pltpu.make_async_copy(src, bricks.at[i], sems.at[i]) for i, src in enumerate((b0, b1, b2, b3, b4))]
    for copy in copies:
        copy.start()
    for copy in copies:
        copy.wait()
    flat = (EDGE * EDGE, NY)
    lane = lanes(flat)
    at_x_rim = lax.rem(lax.broadcasted_iota(jnp.int32, flat, 0), EDGE) == EDGE - 1
    at_y_rim = lax.rem(lane, EDGE) == EDGE - 1
    total = jnp.zeros((8, 128), F32)
    for ez in range(EZ):

        def visit(b, fetched, ez=ez):
            code = place[ez * EYD + b]
            slab = bricks[code // 8].reshape(flat).astype(F32)
            turned = pltpu.roll(slab, lax.rem((b - lax.rem(code, 8) + EYD) * EDGE, NY), 1)
            return jnp.where(lane // EDGE == b, turned, fetched)

        blended = lax.fori_loop(0, EYD, visit, jnp.zeros(flat, F32))
        portion = portions[ez]
        ty, tx, tz = portion[2:3, :], portion[1:2, :], portion[0:1, :]
        shifted = jnp.where(at_y_rim, blended, pltpu.roll(blended, NY - 1, 1))
        blended = (1.0 - ty) * blended + ty * shifted
        shifted = jnp.where(at_x_rim, blended, pltpu.roll(blended, EDGE * EDGE - 1, 0))
        blended = (1.0 - tx) * blended + tx * shifted
        shifted = jnp.concatenate([blended[EDGE:], blended[-EDGE:]], axis=0)
        blended = (1.0 - tz) * blended + tz * shifted
        blended = blended.reshape(EDGE, EDGE, NY)
        collected = [[jnp.zeros((EDGE, NY), F32) for _ in range(2)] for _ in range(3)]
        for k in range(EDGE):
            z = ez * EDGE + k
            apart = ref[z].astype(F32) - blended[k]
            mismatch[z] = apart
            for c in range(3):
                term = grad[c, z].astype(F32) * apart
                for a in range(2):
                    collected[c][a] = collected[c][a] + float(HAT[a, k]) * term
        for c in range(3):
            for a in range(2):
                slabs[(c * 2 + a) * EDGE : (c * 2 + a + 1) * EDGE, :] = collected[c][a]
        summed = exact_dot(across[...], slabs[...])
        total = total + exact_dot(jnp.concatenate([summed[:8], summed[8:]], axis=1), along[ez])
    packed[...] = pltpu.roll(total, lax.rem(gx, 4) * NEL, 1)


def warp(place, bricks, ref, grad, portions):
    across, along = load_tables()
    smem = pl.BlockSpec(memory_space=pltpu.SMEM)
    vmem = pl.BlockSpec(memory_space=pltpu.VMEM)
    anywhere = pl.BlockSpec(memory_space=pl.ANY)
    return pl.pallas_call(
        warp_kernel,
        out_shape=(jax.ShapeDtypeStruct((NZ, EDGE, NY), F32), jax.ShapeDtypeStruct((8, 128), F32)),
        in_specs=[smem] + [anywhere] * 5 + [vmem] * 5,
        out_specs=(vmem, vmem),
        scratch_shapes=[
            pltpu.VMEM((5, EDGE, EDGE, NY), BF16),
            pltpu.VMEM((6 * EDGE, NY), F32),
            pltpu.SemaphoreType.DMA((5,)),
        ],
        name="warp",
    )(place, *bricks, ref, grad, portions, jnp.asarray(across), jnp.asarray(along))


def spread_groups(block_of, groups, gx_count, store):
    tiles = -(-gx_count // 4)
    for tile in range(tiles):
        members = range(4 * tile, min(4 * tile + 4, gx_count))
        blocks = {gx: block_of(gx) for gx in members}
        for group in range(groups):
            merged = jnp.zeros_like(blocks[members[0]])
            lane = lanes(merged.shape)
            for gx in members:
                merged = jnp.where(lane // NEL == (group + gx) % 4, blocks[gx], merged)
            store(group, tile, pltpu.roll(merged, (128 - NEL * group) % 128, 1) if group else merged)


def solve_kernel(gx_count, gy_count, hess, load, out, coef, rhs):
    gx, gy = lax.axis_index("gx"), lax.axis_index("gy")
    tiles = -(-gx_count // 4)
    width = 128 * tiles

    def unpack(row, _):
        def hess_block(column):
            return hess[jnp.bitwise_xor(row, gy) * gx_count + jnp.bitwise_xor(gx, column)]

        def store_hess(group, tile, value):
            coef[tile, pl.ds(row * 3 * HROWS + group * HROWS, HROWS), :] = value

        def load_block(column):
            return load[column * gy_count + row]

        def store_load(group, tile, value):
            rhs[tile, pl.ds(row * 32 + group * 8, 8), :] = value

        spread_groups(hess_block, 3, gx_count, store_hess)
        spread_groups(load_block, 4, gx_count, store_load)
        return 0

    lax.fori_loop(0, gy_count, unpack, 0)
    shape = (gy_count, width)
    lane, row = lanes(shape), rows_of(shape)
    in_z, in_y, in_x = lax.rem(lane, NEL) // EYD, lax.rem(lane, EYD), lane // NEL
    last_z, first_z = in_z == EZ - 1, in_z == 0
    last_x, first_x = in_x >= gx_count - 1, in_x == 0
    last_y, first_y = in_y == EYD - 1, in_y == 0
    end_y, begin_y = last_y & (row == gy_count - 1), first_y & (row == 0)

    def turn(value, by, axis):
        size = shape[axis]
        by = by % size
        return pltpu.roll(value, by, axis) if by else value

    def corners(main, top):
        found = []
        for a in range(2):
            z_part = main if a == 0 else jnp.where(last_z, top, turn(main, -EYD, 1))
            for b in range(2):
                x_part = z_part if b == 0 else jnp.where(last_x, 0.0, turn(z_part, -NEL, 1))
                for d in range(2):
                    if d == 0:
                        found.append(x_part)
                    else:
                        wrapped = turn(turn(x_part, -1, 0), EYD - 1, 1)
                        moved = jnp.where(last_y, wrapped, turn(x_part, -1, 1))
                        found.append(jnp.where(end_y, 0.0, moved))
        return found

    def settle(parts):
        z_parts = []
        for a in range(2):
            x_parts = []
            for b in range(2):
                base, extra = parts[a * 4 + b * 2], parts[a * 4 + b * 2 + 1]
                wrapped = turn(turn(extra, 1, 0), 1 - EYD, 1)
                moved = jnp.where(first_y, wrapped, turn(extra, 1, 1))
                x_parts.append(base + jnp.where(begin_y, 0.0, moved))
            z_parts.append(x_parts[0] + jnp.where(first_x, 0.0, turn(x_parts[1], NEL, 1)))
        main = z_parts[0] + jnp.where(first_z, 0.0, turn(z_parts[1], EYD, 1))
        return main, jnp.where(last_z, z_parts[1], 0.0)

    def strided(ref, start, stride):
        found = [ref[tile, pl.ds(start, gy_count, stride=stride), :] for tile in range(tiles)]
        return found[0] if tiles == 1 else jnp.concatenate(found, axis=1)

    def channel(p, wz, wx, wy):
        return strided(coef, wy * HROWS + (p * 3 + wz) * 3 + wx, 3 * HROWS)

    pair_of = {}
    for p, (c, d) in enumerate(PAIRS):
        pair_of[c, d] = pair_of[d, c] = p
    bits = [(a, b, d) for a in range(2) for b in range(2) for d in range(2)]

    def curved_by(vector):
        known = [corners(main, top) for main, top in vector]
        sums = [[None] * 8 for _ in range(3)]

        def add(c, n, term):
            sums[c][n] = term if sums[c][n] is None else sums[c][n] + term

        for p, (c, d) in enumerate(PAIRS):
            for wz in range(3):
                for wx in range(3):
                    for wy in range(3):
                        factor = channel(p, wz, wx, wy)
                        for n, low in enumerate(bits):
                            for m, high in enumerate(bits):
                                if (low[0] + high[0], low[1] + high[1], low[2] + high[2]) == (wz, wx, wy):
                                    add(c, n, factor * known[d][m])
                                    if c != d:
                                        add(d, n, factor * known[c][m])
        result = []
        for c in range(3):
            main, top = settle(sums[c])
            result.append((main + LAMBDA * vector[c][0], top + LAMBDA * vector[c][1]))
        return result

    def inner(one, two):
        summed = sum(a[0] * b[0] + a[1] * b[1] for a, b in zip(one, two))
        return jnp.sum(jnp.sum(summed, axis=1, keepdims=True), axis=0, keepdims=True)

    def combine(one, factor, two):
        return [(a[0] + factor * b[0], a[1] + factor * b[1]) for a, b in zip(one, two)]

    residual = []
    for c in range(3):
        parts = [strided(rhs, (b * 2 + d) * 8 + c * 2 + a, 32) for a, b, d in bits]
        residual.append(settle(parts))
    direction = residual
    increment = None
    norm_now = inner(residual, residual)
    for iteration in range(ITERS):
        curved = curved_by(direction)
        step = norm_now / inner(direction, curved)
        if increment is None:
            increment = [(step * a, step * b) for a, b in direction]
        else:
            increment = combine(increment, step, direction)
        if iteration + 1 < ITERS:
            residual = combine(residual, -step, curved)
            norm_next = inner(residual, residual)
            direction = combine(residual, norm_next / norm_now, direction)
            norm_now = norm_next
    mine = (row == gy) & (in_x == gx)
    for c in range(3):
        for part, levels in ((increment[c][0], range(EZ)), (increment[c][1], [EZ])):
            line = jnp.sum(jnp.where(mine, part, 0.0), axis=0, keepdims=True)
            short = line[:, 0:128]
            for tile in range(1, tiles):
                short = short + line[:, tile * 128 : (tile + 1) * 128]
            short = pltpu.roll(jnp.broadcast_to(short, (8, 128)), lax.rem(128 - lax.rem(gx, 4) * NEL, 128), 1)
            for level in levels:
                start = min(level, EZ - 1) * EYD
                out[c, level] = short[0:1, start : start + EYD]


def solve(hess, load):
    gx_count, gy_count = lax.axis_size("gx"), lax.axis_size("gy")
    tiles = -(-gx_count // 4)
    vmem = pl.BlockSpec(memory_space=pltpu.VMEM)
    return pl.pallas_call(
        functools.partial(solve_kernel, gx_count, gy_count),
        out_shape=jax.ShapeDtypeStruct((3, EZ + 1, 1, EYD), F32),
        in_specs=[vmem, vmem],
        out_specs=vmem,
        scratch_shapes=[
            pltpu.VMEM((tiles, gy_count * 3 * HROWS, 128), F32),
            pltpu.VMEM((tiles, gy_count * 32, 128), F32),
        ],
        compiler_params=pltpu.CompilerParams(vmem_limit_bytes=48 * 1024 * 1024),
        name="solve",
    )(hess, load)


def swap(array, axis, partner):
    size = lax.axis_size(axis)
    pairs = [(i, partner(i)) for i in range(size)]
    return lax.ppermute(array, axis, [(i, j) for i, j in pairs if 0 <= j < size])


def swap_x(array, kind):
    if kind == 0:
        return swap(array, "gx", lambda i: i ^ 1)
    return swap(array, "gx", lambda i: i + 1 if i % 2 else i - 1)


def swap_y(array, kind):
    size = lax.axis_size("gy")
    partner = (
        lambda i: i ^ 1,
        lambda i: (i + 1 if i % 2 else i - 1) % size,
        lambda i: i ^ 2,
        lambda i: (i + 2 if i // 2 % 2 else i - 2) % size,
    )[kind]
    return swap(array, "gy", partner)


def everyones(block):
    known = block[None]
    for axis in ("gx", "gy"):
        step = 1
        while step < lax.axis_size(axis):
            known = jnp.concatenate([known, swap(known, axis, lambda i, step=step: i ^ step)], axis=0)
            step *= 2
    return known


def body(reference_image, deformed_image, route, within, xshift, fractions):
    d0, d1 = swap_x(deformed_image, 0), swap_x(deformed_image, 1)
    m0, m1, m2, m3, f0, f1, own, place = ask(
        route.reshape(NEL), within.reshape(NEL), xshift.reshape(NEL), reference_image
    )
    a0, a1 = swap_x(f0, 0), swap_x(f1, 1)
    q = [swap_y(m, kind) for kind, m in enumerate((m0, m1, m2, m3))]
    *served, at_home = serve(deformed_image, d0, d1, (*q, own))
    bricks = [swap_y(s, kind) for kind, s in enumerate(served)] + [at_home]
    grad, packed, portions = moments(reference_image, (a0, a1), (q[0], q[1]), fractions.reshape(NEL, 3))
    hess = everyones(packed)
    mismatch, part = warp(place, bricks, reference_image, grad, portions)
    devices = lax.axis_size("gx") * lax.axis_size("gy")
    load = lax.all_to_all(jnp.broadcast_to(part[None], (devices, 8, 128)), ("gx", "gy"), 0, 0)
    return solve(hess, load), mismatch


def solution(mesh):
    placed = (
        P(None, "gx", "gy"),
        P(None, "gx", "gy"),
        P("gx", "gy", None, None),
        P("gx", "gy", None),
        P("gx", "gy", None),
        P("gx", "gy", None, None),
    )
    return jax.shard_map(
        body,
        mesh=mesh,
        in_specs=placed,
        out_specs=(P(None, None, "gx", "gy"), P(None, "gx", "gy")),
        check_vma=False,
    )
```

time: 446 us -> 102 us (0.23)
  blocking collectives: 209 us -> 0 us
  local copies, waits for them, and re-layouts: 69.5 us -> 4.14 us
  waiting for transfers between devices: 77.4 us -> 37.1 us
  starting transfers between devices: 60.9 us -> 33.5 us
  Pallas kernels: 0 us -> 25 us
  other arithmetic: 19 us -> 0.78 us
  between operations: 8.49 us -> 0.86 us
    psum x5 -> x0, blocking collectives: 209 us -> none  [the longest x3 124 us: squared(): return lax.psum(jnp.sum(vector * vector), ('gx', 'gy'))]
    ppermute x24 -> x17, waiting for transfers between devices: 77.4 us -> 29.4 us  [swap(): lax.ppermute(array, axis, [(i, j) for i, j in pairs if 0 <= j < size])]
    reshape x10 -> x1, local copies, waits for them, and re-layouts: 38.3 us -> 0.68 us  [body(): fractions.reshape(NEL, 3)]
    ppermute x24 -> x17, starting transfers between devices: 60.9 us -> 30.9 us  [swap(): lax.ppermute(array, axis, [(i, j) for i, j in pairs if 0 <= j < size])]
    pallas_call x0 -> x5, Pallas kernels: none -> 25 us  [the longest x1 8.24 us: warp(): pl.pallas_call(warp_kernel, out_shape=(jax.ShapeDtypeStruct((NZ, EDGE, NY...]
    convert_element_type x3 -> x0, local copies, waits for them, and re-layouts: 12.8 us -> none  [body(): mismatch_rows = reference_rows.astype(jnp.float32) - warped]
    gather x5 -> x0, local copies, waits for them, and re-layouts: 8.59 us -> none  [the longest x4 7.88 us: body(): picked = jnp.take(window, source_index, axis=0)]
    all_to_all x0 -> x1, waiting for transfers between devices: none -> 7.69 us  [body(): lax.all_to_all(jnp.broadcast_to(part[None], (devices, 8, 128)), ('gx', 'g...]
  transfers between devices with their start and end apart: 24 -> 18, of which waited for: 15 -> 9; matrix products, arithmetic and copies ran while one was open for 8% -> 2% of each run, Pallas kernels for 0% -> 15%
where the time goes in v1:
time: 102 us; the launch traced here: 101 us
  waiting for transfers between devices  37.1 us (36%)
  starting transfers between devices  33.5 us (33%)
  Pallas kernels  25 us (25%)
  local copies, waits for them, and re-layouts  4.14 us (4%)
    ppermute x17, starting transfers between devices, swap(): lax.ppermute(array, axis, [(i, j) for i, j in pairs if 0 <= j < size])  30.9 us
    ppermute x17, waiting for transfers between devices, swap(): lax.ppermute(array, axis, [(i, j) for i, j in pairs if 0 <= j < size])  29.4 us
    pallas_call x1, Pallas kernels, warp(): pl.pallas_call(warp_kernel, out_shape=(jax.ShapeDtypeStruct((NZ, EDGE, NY...  8.24 us
    all_to_all x1, waiting for transfers between devices, body(): lax.all_to_all(jnp.broadcast_to(part[None], (devices, 8, 128)), ('gx', 'g...  7.69 us
    pallas_call x1, Pallas kernels, serve(): pl.pallas_call(serve_kernel, out_shape=(jax.ShapeDtypeStruct((EDGE, EDGE,...  7.16 us
    pallas_call x1, Pallas kernels, moments(): pl.pallas_call(functools.partial(moments_kernel, lax.axis_size('gy')), ou...  4.02 us
    pallas_call x1, Pallas kernels, solve(): pl.pallas_call(functools.partial(solve_kernel, gx_count, gy_count), out_s...  3.52 us
    all_to_all x1, starting transfers between devices, body(): lax.all_to_all(jnp.broadcast_to(part[None], (devices, 8, 128)), ('gx', 'g...  2.57 us
  transfers between devices with their start and end apart: 18, of which 9 were waited for; matrix products, arithmetic and copies ran while one was open for 2% of the time, Pallas kernels for 15%

profile of v1, /device:TPU:0, one launch (start us, length us, event | category | flops | bytes accessed | tf_op | source)
XLA Modules:
  0.0 101.4 jit_solution(10811687459420494698)
XLA Ops:
  0.6 2.1 %ask.1 = (f32[16,128]{1,0:T(8,128)}, f32[16,128]{1,0:T(8,128)}, f32[8,128]{1,0:T(8,128)}, f32[8,128]{1,0:T(8,128)}, bf16[64,128]{1,0:T(8,128)(2,1)}, /*index=5*/...) custom-call(s32[32]{0:T(128)} %bitcast.12, s32[32]{0:T(128)} %bitcast.13, s32[32]{0:T(128)} %bitcast.14, ...), custom_call_target="tpu_custom_call" | custom-call | tf_op jit(solution)/shard_map/ask/pallas_call | solution.py:120
  3.3 0.8 collective-permute-start.1
  4.0 2.5 %collective-permute-start.2 = (f32[16,128]{1,0:T(8,128)}, f32[16,128]{1,0:T(8,128)S(1)}, u32[]{:S(2)}, u32[]{:S(2)}) collective-permute-start(f32[16,128]{1,0:T(8,128)} %get-tuple-element.22), channel_id=1, source_target_pairs={{0,1},{1,0},{2,3},{3,2},{4,5},{5,4},{6,7},{7,6},{8,9},{9,8},{10,11... | collective-permute-start | bytes 24584 | tf_op jit(solution)/shard_map/ppermute | solution.py:484
  6.5 3.6 %collective-permute-start.3 = (f32[16,128]{1,0:T(8,128)}, f32[16,128]{1,0:T(8,128)S(1)}, u32[]{:S(2)}, u32[]{:S(2)}) collective-permute-start(f32[16,128]{1,0:T(8,128)} %get-tuple-element.23), channel_id=1, source_target_pairs={{0,7},{1,2},{2,1},{3,4},{4,3},{5,6},{6,5},{7,0},{8,15},{9,10},{10,... | collective-permute-start | bytes 24584 | tf_op jit(solution)/shard_map/ppermute | solution.py:484
  10.1 0.7 copy.13
  10.8 2.3 %collective-permute-done.3.r1.q1 = f32[16,128]{1,0:T(8,128)S(1)} collective-permute-done((f32[16,128]{1,0:T(8,128)}, f32[16,128]{1,0:T(8,128)S(1)}, u32[]{:S(2)}, u32[]{:S(2)}) %collective-permute-start.3) | collective-permute-done | bytes 8224 | tf_op jit(solution)/shard_map/ppermute | solution.py:484
  13.7 4.0 %moments.1 = (bf16[3,64,16,128]{3,2,1,0:T(8,128)(2,1)}, f32[56,128]{1,0:T(8,128)}, f32[4,8,128]{2,1,0:T(8,128)}) custom-call(bf16[64,16,128]{2,1,0:T(8,128)(2,1)} %ref.5, bf16[64,128]{1,0:T(8,128)(2,1)} %copy-done.10, bf16[64,128]{1,0:T(8,128)(2,1)} %copy-done.11, f32[16,128]{1,0:T(8,128)} %copy-done.8, f32[16,128]{1,0:T(8,128)} %copy-done.9, ...), custom_call_target="tpu_custom_call" | custom-call | tf_op jit(solution)/shard_map/moments/pallas_call | solution.py:231
  17.7 1.5 %collective-permute-start.4 = (f32[1,56,128]{2,1,0:T(8,128)}, f32[1,56,128]{2,1,0:T(8,128)S(1)}, u32[]{:S(2)}, u32[]{:S(2)}) collective-permute-start(f32[1,56,128]{2,1,0:T(8,128)} %bitcast.7), channel_id=1, source_target_pairs={{0,8},{8,0},{16,24},{24,16},{1,9},{9,1},{17,25},{25,17},{2,10},{10... | collective-permute-start | bytes 86024 | tf_op jit(solution)/shard_map/ppermute | solution.py:484
  19.2 1.1 %collective-permute-done.4 = f32[1,56,128]{2,1,0:T(8,128)S(1)} collective-permute-done((f32[1,56,128]{2,1,0:T(8,128)}, f32[1,56,128]{2,1,0:T(8,128)S(1)}, u32[]{:S(2)}, u32[]{:S(2)}) %collective-permute-start.4) | collective-permute-done | bytes 28704 | tf_op jit(solution)/shard_map/ppermute | solution.py:484
  20.2 0.8 pad_maximum_fusion.2
  21.0 2.4 %collective-permute-start.5 = (f32[2,56,128]{2,1,0:T(8,128)S(1)}, f32[2,56,128]{2,1,0:T(8,128)S(1)}, u32[]{:S(2)}, u32[]{:S(2)}) collective-permute-start(f32[2,56,128]{2,1,0:T(8,128)S(1)} %pad_maximum_fusion.2), channel_id=1, source_target_pairs={{0,16},{8,24},{16,0},{24,8},{1,17},{9,25},{17,1},{25,9},{2,18},{10... | collective-permute-start | bytes 172040 | tf_op jit(solution)/shard_map/ppermute | solution.py:484
  23.4 0.7 collective-permute-start.10
  24.0 1.6 %collective-permute-done.5 = f32[2,56,128]{2,1,0:T(8,128)S(1)} collective-permute-done((f32[2,56,128]{2,1,0:T(8,128)S(1)}, f32[2,56,128]{2,1,0:T(8,128)S(1)}, u32[]{:S(2)}, u32[]{:S(2)}) %collective-permute-start.5) | collective-permute-done | bytes 57376 | tf_op jit(solution)/shard_map/ppermute | solution.py:484
  25.7 5.2 %collective-permute-done.6 = f32[4,56,128]{2,1,0:T(8,128)S(1)} collective-permute-done((f32[4,56,128]{2,1,0:T(8,128)S(1)}, f32[4,56,128]{2,1,0:T(8,128)S(1)}, u32[]{:S(2)}, u32[]{:S(2)}) %collective-permute-start.6) | collective-permute-done | bytes 114720 | tf_op jit(solution)/shard_map/ppermute | solution.py:484
  31.1 6.8 %collective-permute-done.7 = f32[8,56,128]{2,1,0:T(8,128)S(1)} collective-permute-done((f32[8,56,128]{2,1,0:T(8,128)S(1)}, f32[8,56,128]{2,1,0:T(8,128)S(1)}, u32[]{:S(2)}, u32[]{:S(2)}) %collective-permute-start.7) | collective-permute-done | bytes 229408 | tf_op jit(solution)/shard_map/ppermute | solution.py:484
  38.0 1.6 %collective-permute-start.8 = (f32[16,56,128]{2,1,0:T(8,128)S(1)}, f32[16,56,128]{2,1,0:T(8,128)S(1)}, u32[]{:S(2)}, u32[]{:S(2)}) collective-permute-start(f32[16,56,128]{2,1,0:T(8,128)S(1)} %get-tuple-element.38), channel_id=1, source_target_pairs={{0,4},{1,5},{2,6},{3,7},{4,0},{5,1},{6,2},{7,3},{8,12},{9,13},{10,... | collective-permute-start | bytes 1376264 | tf_op jit(solution)/shard_map/ppermute | solution.py:484
  39.6 1.7 %collective-permute-start.11 = (f32[8,128]{1,0:T(8,128)S(1)}, f32[8,128]{1,0:T(8,128)S(1)}, u32[]{:S(2)}, u32[]{:S(2)}) collective-permute-start(f32[8,128]{1,0:T(8,128)S(1)} %copy-done.16), channel_id=1, source_target_pairs={{0,2},{1,3},{2,0},{3,1},{4,6},{5,7},{6,4},{7,5},{8,10},{9,11},{10,... | collective-permute-start | bytes 12296 | tf_op jit(solution)/shard_map/ppermute | solution.py:484
  41.3 1.1 %collective-permute-start.12 = (f32[8,128]{1,0:T(8,128)S(1)}, f32[8,128]{1,0:T(8,128)S(1)}, u32[]{:S(2)}, u32[]{:S(2)}) collective-permute-start(f32[8,128]{1,0:T(8,128)S(1)} %copy-done.15), channel_id=1, source_target_pairs={{0,6},{1,7},{2,4},{3,5},{4,2},{5,3},{6,0},{7,1},{8,14},{9,15},{10,... | collective-permute-start | bytes 12296 | tf_op jit(solution)/shard_map/ppermute | solution.py:484
  42.4 6.4 %collective-permute-done.11.q2 = f32[8,128]{1,0:T(8,128)S(1)} collective-permute-done((f32[8,128]{1,0:T(8,128)S(1)}, f32[8,128]{1,0:T(8,128)S(1)}, u32[]{:S(2)}, u32[]{:S(2)}) %collective-permute-start.11) | collective-permute-done | bytes 4128 | tf_op jit(solution)/shard_map/ppermute | solution.py:484
  48.8 1.6 %collective-permute-done.12.q3 = f32[8,128]{1,0:T(8,128)S(1)} collective-permute-done((f32[8,128]{1,0:T(8,128)S(1)}, f32[8,128]{1,0:T(8,128)S(1)}, u32[]{:S(2)}, u32[]{:S(2)}) %collective-permute-start.12) | collective-permute-done | bytes 4128 | tf_op jit(solution)/shard_map/ppermute | solution.py:484
  51.3 7.2 %serve.1 = (bf16[16,16,128]{2,1,0:T(8,128)(2,1)}, bf16[16,16,128]{2,1,0:T(8,128)(2,1)}, bf16[16,16,128]{2,1,0:T(8,128)(2,1)}, bf16[16,16,128]{2,1,0:T(8,128)(2,1)}, bf16[16,16,128]{2,1,0:T(8,128)(2,1)}) custom-call(bf16[64,16,128]{2,1,0:T(8,128)(2,1)} %own.1, bf16[64,16,128]{2,1,0:T(8,128)(2,1)} %copy-done.2, bf16[64,16,128]{2,1,0:T(8,128)(2,1)} %copy-done.3, ...), custom_call_target="tpu_custom_call" | custom-call | tf_op jit(solution)/shard_map/serve/pallas_call | solution.py:164
  58.4 1.1 %collective-permute-start.13 = (bf16[16,16,128]{2,1,0:T(8,128)(2,1)}, bf16[16,16,128]{2,1,0:T(8,128)(2,1)S(1)}, u32[]{:S(2)}, u32[]{:S(2)}) collective-permute-start(bf16[16,16,128]{2,1,0:T(8,128)(2,1)} %get-tuple-element.29), channel_id=1, source_target_pairs={{0,1},{1,0},{2,3},{3,2},{4,5},{5,4},{6,7},{7,6},{8,9},{9,8},{10,11... | collective-permute-start | bytes 196616 | tf_op jit(solution)/shard_map/ppermute | solution.py:484
  59.6 3.1 %collective-permute-start.14 = (bf16[16,16,128]{2,1,0:T(8,128)(2,1)}, bf16[16,16,128]{2,1,0:T(8,128)(2,1)S(1)}, u32[]{:S(2)}, u32[]{:S(2)}) collective-permute-start(bf16[16,16,128]{2,1,0:T(8,128)(2,1)} %get-tuple-element.30), channel_id=1, source_target_pairs={{0,7},{1,2},{2,1},{3,4},{4,3},{5,6},{6,5},{7,0},{8,15},{9,10},{10,... | collective-permute-start | bytes 196616 | tf_op jit(solution)/shard_map/ppermute | solution.py:484
  62.6 6.7 %collective-permute-start.15 = (bf16[16,16,128]{2,1,0:T(8,128)(2,1)}, bf16[16,16,128]{2,1,0:T(8,128)(2,1)S(1)}, u32[]{:S(2)}, u32[]{:S(2)}) collective-permute-start(bf16[16,16,128]{2,1,0:T(8,128)(2,1)} %get-tuple-element.31), channel_id=1, source_target_pairs={{0,2},{1,3},{2,0},{3,1},{4,6},{5,7},{6,4},{7,5},{8,10},{9,11},{10,... | collective-permute-start | bytes 196616 | tf_op jit(solution)/shard_map/ppermute | solution.py:484
  69.4 3.6 %collective-permute-start.16 = (bf16[16,16,128]{2,1,0:T(8,128)(2,1)}, bf16[16,16,128]{2,1,0:T(8,128)(2,1)S(1)}, u32[]{:S(2)}, u32[]{:S(2)}) collective-permute-start(bf16[16,16,128]{2,1,0:T(8,128)(2,1)} %get-tuple-element.32), channel_id=1, source_target_pairs={{0,6},{1,7},{2,4},{3,5},{4,2},{5,3},{6,0},{7,1},{8,14},{9,15},{10,... | collective-permute-start | bytes 196616 | tf_op jit(solution)/shard_map/ppermute | solution.py:484
  73.0 4.3 %collective-permute-done.16.b3 = bf16[16,16,128]{2,1,0:T(8,128)(2,1)S(1)} collective-permute-done((bf16[16,16,128]{2,1,0:T(8,128)(2,1)}, bf16[16,16,128]{2,1,0:T(8,128)(2,1)S(1)}, u32[]{:S(2)}, u32[]{:S(2)}) %collective-permute-start.16) | collective-permute-done | bytes 65568 | tf_op jit(solution)/shard_map/ppermute | solution.py:484
  77.4 0.6 copy-done.7
  78.0 8.2 %warp.1 = (f32[64,16,128]{2,1,0:T(8,128)}, f32[8,128]{1,0:T(8,128)}) custom-call(s32[32]{0:T(128)} %get-tuple-element.25.place, bf16[16,16,128]{2,1,0:T(8,128)(2,1)} %copy-done.4, bf16[16,16,128]{2,1,0:T(8,128)(2,1)} %copy-done.5, bf16[16,16,128]{2,1,0:T(8,128)(2,1)} %copy-done.6, bf16[16,16,128]{2,1,0:T(8,128)(2,1)} %copy-done.7, ...), custom_call_target="tpu_custom_call" | custom-call | tf_op jit(solution)/shard_map/warp/pallas_call | solution.py:297
  86.2 1.3 %broadcast_in_dim.10 = f32[32,8,128]{2,1,0:T(8,128)} broadcast(f32[8,128]{1,0:T(8,128)} %get-tuple-element.36), dimensions={1,2} | broadcast | bytes 135168 | tf_op jit(solution)/shard_map/broadcast_in_dim | solution.py:527
  87.6 2.6 %all-to-all-start = ((f32[32,8,128]{2,1,0:T(8,128)}), f32[32,8,128]{2,1,0:T(8,128)S(1)}, u32[]{:S(2)}, u32[]{:S(2)}) async-start(f32[32,8,128]{2,1,0:T(8,128)} %broadcast_in_dim.10), calls=%async_computation | async-start | bytes 262144 | tf_op jit(solution)/shard_map/all_to_all | solution.py:527
  90.2 7.7 %all-to-all-done.load = f32[32,8,128]{2,1,0:T(8,128)S(1)} async-done(((f32[32,8,128]{2,1,0:T(8,128)}), f32[32,8,128]{2,1,0:T(8,128)S(1)}, u32[]{:S(2)}, u32[]{:S(2)}) %all-to-all-start) | async-done | bytes 131104 | tf_op jit(solution)/shard_map/all_to_all | solution.py:527
  97.9 3.5 %solve.1 = f32[3,5,1,8]{3,2,1,0:T(1,128)} custom-call(f32[32,56,128]{2,1,0:T(8,128)S(1)} %constant_dynamic-update-slice_fusion.5.hess, f32[32,8,128]{2,1,0:T(8,128)S(1)} %all-to-all-done.load), custom_call_target="tpu_custom_call" | custom-call | tf_op jit(solution)/shard_map/solve/pallas_call | solution.py:467
  (54 shorter events, 2.2 us)
Async XLA Ops:
  2.7 10.3 %collective-permute-start = (bf16[64,128]{1,0:T(8,128)(2,1)}, bf16[64,128]{1,0:T(8,128)(2,1)S(1)}, u32[]{:S(2)}, u32[]{:S(2)}) collective-permute-start(bf16[64,128]{1,0:T(8,128)(2,1)} %get-tuple-element.20), channel_id=1, source_target_pairs={{0,8},{8,0},{16,24},{24,16},{1,9},{9,1},{17,25},{25,17},{2,10},{10... | collective-permute-start | bytes 49160 | tf_op jit(solution)/shard_map/ppermute | solution.py:484
  3.3 6.8 %copy-start.14 = (s32[1,1,32,3]{2,1,3,0:T(1,128)S(1)}, s32[1,1,32,3]{2,1,3,0:T(1,128)}, u32[]{:S(2)}) copy-start(s32[1,1,32,3]{2,1,3,0:T(1,128)} %param.15) | copy-start | bytes 1156
  3.3 9.8 %collective-permute-start.1 = (bf16[64,128]{1,0:T(8,128)(2,1)}, bf16[64,128]{1,0:T(8,128)(2,1)S(1)}, u32[]{:S(2)}, u32[]{:S(2)}) collective-permute-start(bf16[64,128]{1,0:T(8,128)(2,1)} %get-tuple-element.21), channel_id=1, source_target_pairs={{8,16},{16,8},{9,17},{17,9},{10,18},{18,10},{11,19},{19,11},{12,20... | collective-permute-start | bytes 49160 | tf_op jit(solution)/shard_map/ppermute | solution.py:484
  4.0 6.7 %collective-permute-start.2 = (f32[16,128]{1,0:T(8,128)}, f32[16,128]{1,0:T(8,128)S(1)}, u32[]{:S(2)}, u32[]{:S(2)}) collective-permute-start(f32[16,128]{1,0:T(8,128)} %get-tuple-element.22), channel_id=1, source_target_pairs={{0,1},{1,0},{2,3},{3,2},{4,5},{5,4},{6,7},{7,6},{8,9},{9,8},{10,11... | collective-permute-start | bytes 24584 | tf_op jit(solution)/shard_map/ppermute | solution.py:484
  6.5 6.6 %collective-permute-start.3 = (f32[16,128]{1,0:T(8,128)}, f32[16,128]{1,0:T(8,128)S(1)}, u32[]{:S(2)}, u32[]{:S(2)}) collective-permute-start(f32[16,128]{1,0:T(8,128)} %get-tuple-element.23), channel_id=1, source_target_pairs={{0,7},{1,2},{2,1},{3,4},{4,3},{5,6},{6,5},{7,0},{8,15},{9,10},{10,... | collective-permute-start | bytes 24584 | tf_op jit(solution)/shard_map/ppermute | solution.py:484
  10.8 2.3 %copy-start.8 = (f32[16,128]{1,0:T(8,128)}, f32[16,128]{1,0:T(8,128)S(1)}, u32[]{:S(2)}) copy-start(f32[16,128]{1,0:T(8,128)S(1)} %collective-permute-done.2.r0.q0) | copy-start | bytes 24580
  13.1 0.6 copy-start.10
  13.7 9.7 %copy-start.1 = (bf16[64,16,128]{2,1,0:T(8,128)(2,1)S(1)}, bf16[64,16,128]{2,1,0:T(8,128)(2,1)}, u32[]{:S(2)}) copy-start(bf16[64,16,128]{2,1,0:T(8,128)(2,1)} %own.1) | copy-start | bytes 786436
  17.7 7.9 %copy-start = (f32[56,128]{1,0:T(8,128)S(1)}, f32[56,128]{1,0:T(8,128)}, u32[]{:S(2)}) copy-start(f32[56,128]{1,0:T(8,128)} %get-tuple-element.24) | copy-start | bytes 86020
  17.7 2.5 %collective-permute-start.4 = (f32[1,56,128]{2,1,0:T(8,128)}, f32[1,56,128]{2,1,0:T(8,128)S(1)}, u32[]{:S(2)}, u32[]{:S(2)}) collective-permute-start(f32[1,56,128]{2,1,0:T(8,128)} %bitcast.7), channel_id=1, source_target_pairs={{0,8},{8,0},{16,24},{24,16},{1,9},{9,1},{17,25},{25,17},{2,10},{10... | collective-permute-start | bytes 86024 | tf_op jit(solution)/shard_map/ppermute | solution.py:484
  21.0 4.6 %collective-permute-start.5 = (f32[2,56,128]{2,1,0:T(8,128)S(1)}, f32[2,56,128]{2,1,0:T(8,128)S(1)}, u32[]{:S(2)}, u32[]{:S(2)}) collective-permute-start(f32[2,56,128]{2,1,0:T(8,128)S(1)} %pad_maximum_fusion.2), channel_id=1, source_target_pairs={{0,16},{8,24},{16,0},{24,8},{1,17},{9,25},{17,1},{25,9},{2,18},{10... | collective-permute-start | bytes 172040 | tf_op jit(solution)/shard_map/ppermute | solution.py:484
  23.4 27.1 %collective-permute-start.9 = (bf16[64,16,128]{2,1,0:T(8,128)(2,1)S(1)}, bf16[64,16,128]{2,1,0:T(8,128)(2,1)S(1)}, u32[]{:S(2)}, u32[]{:S(2)}) collective-permute-start(bf16[64,16,128]{2,1,0:T(8,128)(2,1)S(1)} %copy-done.1), channel_id=1, source_target_pairs={{0,8},{8,0},{16,24},{24,16},{1,9},{9,1},{17,25},{25,17},{2,10},{10... | collective-permute-start | bytes 786440 | tf_op jit(solution)/shard_map/ppermute | solution.py:484
  23.4 27.1 %collective-permute-start.10 = (bf16[64,16,128]{2,1,0:T(8,128)(2,1)S(1)}, bf16[64,16,128]{2,1,0:T(8,128)(2,1)S(1)}, u32[]{:S(2)}, u32[]{:S(2)}) collective-permute-start(bf16[64,16,128]{2,1,0:T(8,128)(2,1)S(1)} %copy-done.1), channel_id=1, source_target_pairs={{8,16},{16,8},{9,17},{17,9},{10,18},{18,10},{11,19},{19,11},{12,20... | collective-permute-start | bytes 786440 | tf_op jit(solution)/shard_map/ppermute | solution.py:484
  25.6 5.3 %collective-permute-start.6 = (f32[4,56,128]{2,1,0:T(8,128)S(1)}, f32[4,56,128]{2,1,0:T(8,128)S(1)}, u32[]{:S(2)}, u32[]{:S(2)}) collective-permute-start(f32[4,56,128]{2,1,0:T(8,128)S(1)} %pad_maximum_fusion.1), channel_id=1, source_target_pairs={{0,1},{1,0},{2,3},{3,2},{4,5},{5,4},{6,7},{7,6},{8,9},{9,8},{10,11... | collective-permute-start | bytes 344072 | tf_op jit(solution)/shard_map/ppermute | solution.py:484
  31.0 7.0 %collective-permute-start.7 = (f32[8,56,128]{2,1,0:T(8,128)S(1)}, f32[8,56,128]{2,1,0:T(8,128)S(1)}, u32[]{:S(2)}, u32[]{:S(2)}) collective-permute-start(f32[8,56,128]{2,1,0:T(8,128)S(1)} %pad_maximum_fusion), channel_id=1, source_target_pairs={{0,2},{1,3},{2,0},{3,1},{4,6},{5,7},{6,4},{7,5},{8,10},{9,11},{10,... | collective-permute-start | bytes 688136 | tf_op jit(solution)/shard_map/ppermute | solution.py:484
  37.9 1.7 %copy-start.16 = (f32[8,128]{1,0:T(8,128)S(1)}, f32[8,128]{1,0:T(8,128)}, u32[]{:S(2)}) copy-start(f32[8,128]{1,0:T(8,128)} %get-tuple-element.26) | copy-start | bytes 12292
  38.0 3.4 %copy-start.15 = (f32[8,128]{1,0:T(8,128)S(1)}, f32[8,128]{1,0:T(8,128)}, u32[]{:S(2)}) copy-start(f32[8,128]{1,0:T(8,128)} %get-tuple-element.27) | copy-start | bytes 12292
  38.0 52.2 %collective-permute-start.8 = (f32[16,56,128]{2,1,0:T(8,128)S(1)}, f32[16,56,128]{2,1,0:T(8,128)S(1)}, u32[]{:S(2)}, u32[]{:S(2)}) collective-permute-start(f32[16,56,128]{2,1,0:T(8,128)S(1)} %get-tuple-element.38), channel_id=1, source_target_pairs={{0,4},{1,5},{2,6},{3,7},{4,0},{5,1},{6,2},{7,3},{8,12},{9,13},{10,... | collective-permute-start | bytes 1376264 | tf_op jit(solution)/shard_map/ppermute | solution.py:484
  39.6 9.3 %collective-permute-start.11 = (f32[8,128]{1,0:T(8,128)S(1)}, f32[8,128]{1,0:T(8,128)S(1)}, u32[]{:S(2)}, u32[]{:S(2)}) collective-permute-start(f32[8,128]{1,0:T(8,128)S(1)} %copy-done.16), channel_id=1, source_target_pairs={{0,2},{1,3},{2,0},{3,1},{4,6},{5,7},{6,4},{7,5},{8,10},{9,11},{10,... | collective-permute-start | bytes 12296 | tf_op jit(solution)/shard_map/ppermute | solution.py:484
  41.3 9.2 %collective-permute-start.12 = (f32[8,128]{1,0:T(8,128)S(1)}, f32[8,128]{1,0:T(8,128)S(1)}, u32[]{:S(2)}, u32[]{:S(2)}) collective-permute-start(f32[8,128]{1,0:T(8,128)S(1)} %copy-done.15), channel_id=1, source_target_pairs={{0,6},{1,7},{2,4},{3,5},{4,2},{5,3},{6,0},{7,1},{8,14},{9,15},{10,... | collective-permute-start | bytes 12296 | tf_op jit(solution)/shard_map/ppermute | solution.py:484
  48.8 1.7 %copy-start.12 = (f32[8,128]{1,0:T(8,128)}, f32[8,128]{1,0:T(8,128)S(1)}, u32[]{:S(2)}) copy-start(f32[8,128]{1,0:T(8,128)S(1)} %collective-permute-done.11.q2) | copy-start | bytes 12292
  50.5 0.7 copy-start.2
  50.5 0.8 copy-start.3
  58.4 14.5 %collective-permute-start.13 = (bf16[16,16,128]{2,1,0:T(8,128)(2,1)}, bf16[16,16,128]{2,1,0:T(8,128)(2,1)S(1)}, u32[]{:S(2)}, u32[]{:S(2)}) collective-permute-start(bf16[16,16,128]{2,1,0:T(8,128)(2,1)} %get-tuple-element.29), channel_id=1, source_target_pairs={{0,1},{1,0},{2,3},{3,2},{4,5},{5,4},{6,7},{7,6},{8,9},{9,8},{10,11... | collective-permute-start | bytes 196616 | tf_op jit(solution)/shard_map/ppermute | solution.py:484
  59.6 13.4 %collective-permute-start.14 = (bf16[16,16,128]{2,1,0:T(8,128)(2,1)}, bf16[16,16,128]{2,1,0:T(8,128)(2,1)S(1)}, u32[]{:S(2)}, u32[]{:S(2)}) collective-permute-start(bf16[16,16,128]{2,1,0:T(8,128)(2,1)} %get-tuple-element.30), channel_id=1, source_target_pairs={{0,7},{1,2},{2,1},{3,4},{4,3},{5,6},{6,5},{7,0},{8,15},{9,10},{10,... | collective-permute-start | bytes 196616 | tf_op jit(solution)/shard_map/ppermute | solution.py:484
  62.6 10.3 %collective-permute-start.15 = (bf16[16,16,128]{2,1,0:T(8,128)(2,1)}, bf16[16,16,128]{2,1,0:T(8,128)(2,1)S(1)}, u32[]{:S(2)}, u32[]{:S(2)}) collective-permute-start(bf16[16,16,128]{2,1,0:T(8,128)(2,1)} %get-tuple-element.31), channel_id=1, source_target_pairs={{0,2},{1,3},{2,0},{3,1},{4,6},{5,7},{6,4},{7,5},{8,10},{9,11},{10,... | collective-permute-start | bytes 196616 | tf_op jit(solution)/shard_map/ppermute | solution.py:484
  69.4 8.0 %collective-permute-start.16 = (bf16[16,16,128]{2,1,0:T(8,128)(2,1)}, bf16[16,16,128]{2,1,0:T(8,128)(2,1)S(1)}, u32[]{:S(2)}, u32[]{:S(2)}) collective-permute-start(bf16[16,16,128]{2,1,0:T(8,128)(2,1)} %get-tuple-element.32), channel_id=1, source_target_pairs={{0,6},{1,7},{2,4},{3,5},{4,2},{5,3},{6,0},{7,1},{8,14},{9,15},{10,... | collective-permute-start | bytes 196616 | tf_op jit(solution)/shard_map/ppermute | solution.py:484
  73.0 4.4 %copy-start.4 = (bf16[16,16,128]{2,1,0:T(8,128)(2,1)}, bf16[16,16,128]{2,1,0:T(8,128)(2,1)S(1)}, u32[]{:S(2)}) copy-start(bf16[16,16,128]{2,1,0:T(8,128)(2,1)S(1)} %collective-permute-done.13.b0) | copy-start | bytes 196612
  73.0 4.4 %copy-start.5 = (bf16[16,16,128]{2,1,0:T(8,128)(2,1)}, bf16[16,16,128]{2,1,0:T(8,128)(2,1)S(1)}, u32[]{:S(2)}) copy-start(bf16[16,16,128]{2,1,0:T(8,128)(2,1)S(1)} %collective-permute-done.14.b1) | copy-start | bytes 196612
  73.0 4.4 %copy-start.6 = (bf16[16,16,128]{2,1,0:T(8,128)(2,1)}, bf16[16,16,128]{2,1,0:T(8,128)(2,1)S(1)}, u32[]{:S(2)}) copy-start(bf16[16,16,128]{2,1,0:T(8,128)(2,1)S(1)} %collective-permute-done.15.b2) | copy-start | bytes 196612
  77.3 0.6 copy-start.7
  87.6 10.3 %all-to-all-start = ((f32[32,8,128]{2,1,0:T(8,128)}), f32[32,8,128]{2,1,0:T(8,128)S(1)}, u32[]{:S(2)}, u32[]{:S(2)}) async-start(f32[32,8,128]{2,1,0:T(8,128)} %broadcast_in_dim.10), calls=%async_computation | async-start | bytes 262144 | tf_op jit(solution)/shard_map/all_to_all | solution.py:527
  (3 other events, 1.8 us)

commit v2 on v1

--- a/solution.py
+++ b/solution.py
@@ -21,6 +21,7 @@
 
 PAIRS = ((0, 0), (0, 1), (0, 2), (1, 1), (1, 2), (2, 2))
 HROWS = 56
+LIMIT = 32 * 1024 * 1024
 
 F32 = jnp.float32
 BF16 = jnp.bfloat16
@@ -30,31 +31,22 @@
 PRODUCTS = np.stack([HAT[0] * HAT[0], HAT[0] * HAT[1], HAT[1] * HAT[1]])
 
 
-def along_y_weights(weights):
-    table = np.zeros((EZ, NY, 128), np.float32)
-    for group, row in enumerate(weights):
-        for ez in range(EZ):
-            for ey in range(EYD):
-                table[ez, ey * EDGE : (ey + 1) * EDGE, group * NEL + ez * EYD + ey] = row / VOL
-    return table
-
-
-def moment_tables():
-    across = np.zeros((HROWS, 18 * EDGE), np.float32)
-    for slab in range(18):
-        for wx in range(3):
-            across[slab * 3 + wx, slab * EDGE : (slab + 1) * EDGE] = PRODUCTS[wx]
-    return across, along_y_weights(PRODUCTS)
-
-
-def load_tables():
-    across = np.zeros((16, 6 * EDGE), np.float32)
-    for slab in range(6):
-        for bx in range(2):
-            across[bx * 8 + slab, slab * EDGE : (slab + 1) * EDGE] = HAT[bx]
-    single = along_y_weights(HAT)
-    along = np.concatenate([single, np.roll(single, 2 * NEL, axis=2)], axis=1)
-    return across, along
+def hat_product(which, position):
+    upper = (position.astype(F32) + 0.5) * (1.0 / EDGE)
+    lower = 1.0 - upper
+    return jnp.where(which == 0, lower * lower, jnp.where(which == 1, lower * upper, upper * upper))
+
+
+def hat_weight(which, position):
+    upper = (position.astype(F32) + 0.5) * (1.0 / EDGE)
+    return jnp.where(which == 0, 1.0 - upper, upper)
+
+
+def along_y(weight, groups):
+    shape = (NY, 128)
+    row, lane = rows_of(shape), lanes(shape)
+    inside = (row // EDGE == lax.rem(lane, NEL)) & (lane // NEL < groups)
+    return jnp.where(inside, weight(lane // NEL, lax.rem(row, EDGE)) * (1.0 / VOL), 0.0)
 
 
 def exact_dot(a, b):
@@ -73,7 +65,11 @@
     return lax.rem(value, 2) == 0
 
 
-def ask_kernel(gx_count, route, within, xshift, ref, m0, m1, m2, m3, f0, f1, own, place, count):
+def takes(microseconds):
+    return pl.CostEstimate(flops=0, bytes_accessed=int(microseconds * 3.69e6), transcendentals=0)
+
+
+def ask_kernel(gx_count, route, within, xshift, ref, deformed, m0, m1, m2, m3, thick, own, place, count):
     gx, gy = lax.axis_index("gx"), lax.axis_index("gy")
     for j in range(5):
         count[j] = 0
@@ -108,13 +104,13 @@
     for i in range(8):
         m0[i : i + 1, :] = columns[0:1, i * 128 : (i + 1) * 128]
         m1[i : i + 1, :] = columns[1:2, i * 128 : (i + 1) * 128]
+    thick[0:NZ] = deformed[...]
     image = image.astype(F32)
-    low, high = image[:, 0, :], image[:, EDGE - 1, :]
-    f0[...] = jnp.where(gx_even, high, low).astype(BF16)
-    f1[...] = jnp.where(gx_even, low, high).astype(BF16)
-
-
-def ask(route, within, xshift, ref):
+    for k, face in enumerate((image[:, 0, :], image[:, EDGE - 1, :])):
+        thick[NZ + k * EZ : NZ + (k + 1) * EZ] = face.astype(BF16).reshape(EZ, EDGE, NY)
+
+
+def ask(route, within, xshift, ref, deformed):
     smem = pl.BlockSpec(memory_space=pltpu.SMEM)
     vmem = pl.BlockSpec(memory_space=pltpu.VMEM)
     return pl.pallas_call(
@@ -124,54 +120,65 @@
             jax.ShapeDtypeStruct((16, 128), F32),
             jax.ShapeDtypeStruct((8, 128), F32),
             jax.ShapeDtypeStruct((8, 128), F32),
-            jax.ShapeDtypeStruct((NZ, NY), BF16),
-            jax.ShapeDtypeStruct((NZ, NY), BF16),
+            jax.ShapeDtypeStruct((NZ + 2 * EZ, EDGE, NY), BF16),
             jax.ShapeDtypeStruct((8, 128), F32),
             jax.ShapeDtypeStruct((NEL,), jnp.int32),
         ),
-        in_specs=[smem] * 3 + [vmem],
-        out_specs=(vmem,) * 7 + (smem,),
+        in_specs=[smem] * 3 + [vmem] * 2,
+        out_specs=(vmem,) * 6 + (smem,),
         scratch_shapes=[pltpu.SMEM((8,), jnp.int32)],
+        cost_estimate=takes(2.0),
         name="ask",
-    )(route, within, xshift, ref)
-
-
-def serve_kernel(own, d0, d1, q0, q1, q2, q3, q4, o0, o1, o2, o3, o4, banks, sems):
-    copies = [pltpu.make_async_copy(src, banks.at[i], sems.at[i]) for i, src in enumerate((own, d0, d1))]
-    for copy in copies:
-        copy.start()
-    for copy in copies:
-        copy.wait()
-    lane = lanes((EDGE * EDGE, NY))
-    for j, (asked, out) in enumerate(((q0, o0), (q1, o1), (q2, o2), (q3, o3), (q4, o4))):
-        line = 8 + j if j < 2 else j
-
-        def visit(slot, packed, asked=asked, line=line):
-            code = asked[line, slot].astype(jnp.int32)
-            bank, ez, column = code // NEL, lax.rem(code, NEL) // EYD, lax.rem(code, EYD)
-            slab = banks[bank, pl.ds(ez * EDGE, EDGE)].reshape(EDGE * EDGE, NY).astype(F32)
-            turned = pltpu.roll(slab, lax.rem((slot - column + EYD) * EDGE, NY), 1)
-            return jnp.where(lane // EDGE == slot, turned, packed)
-
-        packed = lax.fori_loop(0, 8, visit, jnp.zeros((EDGE * EDGE, NY), F32))
-        out[...] = packed.reshape(EDGE, EDGE, NY).astype(BF16)
-
-
-def serve(own, d0, d1, asked):
+    )(route, within, xshift, ref, deformed)
+
+
+def gather_columns(table, slabs, sources, places):
+    table[...] = jnp.zeros_like(table)
+    shape = (EDGE, NY)
+    row, lane = rows_of(shape), lanes(shape)
+    for i, (source, place) in enumerate(zip(sources, places)):
+        start = pl.multiple_of(i * NY + source * EDGE, EDGE)
+        table[pl.ds(start, EDGE), :] = (lane == row + place * EDGE).astype(F32).astype(BF16)
+    return jnp.dot(jnp.concatenate(slabs, axis=1), table[...], preferred_element_type=F32)
+
+
+def serve_kernel(lines, *refs):
+    count = len(lines)
+    asked, outs = refs[3 : 3 + count], refs[3 + count : 3 + 2 * count]
+    banks, tables = refs[3 + 2 * count :]
+    for i in range(3):
+        banks[i] = refs[i][0:NZ]
+    for j in range(count):
+        slabs, columns = [], []
+        for slot in range(8):
+            code = asked[j][lines[j], slot].astype(jnp.int32)
+            slab = banks[code // NEL, pl.ds(lax.rem(code, NEL) // EYD * EDGE, EDGE)]
+            slabs.append(slab.reshape(EDGE * EDGE, NY))
+            columns.append(lax.rem(code, EYD))
+        packed = gather_columns(tables.at[j], slabs, columns, range(8))
+        outs[j][...] = packed.reshape(EDGE, EDGE, NY).astype(BF16)
+
+
+def serve(own, d0, d1, asked, lines):
     smem = pl.BlockSpec(memory_space=pltpu.SMEM)
     vmem = pl.BlockSpec(memory_space=pltpu.VMEM)
-    anywhere = pl.BlockSpec(memory_space=pl.ANY)
+    count = len(lines)
     return pl.pallas_call(
-        serve_kernel,
-        out_shape=(jax.ShapeDtypeStruct((EDGE, EDGE, NY), BF16),) * 5,
-        in_specs=[anywhere] * 3 + [smem] * 5,
-        out_specs=(vmem,) * 5,
-        scratch_shapes=[pltpu.VMEM((3, NZ, EDGE, NY), BF16), pltpu.SemaphoreType.DMA((3,))],
+        functools.partial(serve_kernel, lines),
+        out_shape=(jax.ShapeDtypeStruct((EDGE, EDGE, NY), BF16),) * count,
+        in_specs=[vmem] * 3 + [smem] * count,
+        out_specs=(vmem,) * count,
+        scratch_shapes=[
+            pltpu.VMEM((3, NZ, EDGE, NY), BF16),
+            pltpu.VMEM((count, 8 * NY, NY), BF16),
+        ],
+        compiler_params=pltpu.CompilerParams(vmem_limit_bytes=LIMIT),
+        cost_estimate=takes(1.0 + 0.2 * count),
         name="serve",
     )(own, d0, d1, *asked)
 
 
-def moments_kernel(gy_count, ref, a0, a1, r0, r1, frac, across, along, grad, packed, portions, side, slabs):
+def moments_kernel(gy_count, ref, a0, a1, r0, r1, frac, grad, packed, portions, side, slabs):
     gx, gy = lax.axis_index("gx"), lax.axis_index("gy")
     gx_even, gy_even = even(gx), even(gy)
     side[...] = jnp.zeros((8, NZ * EDGE), F32)
@@ -187,9 +194,15 @@
     rim = lax.dot_general(
         side[...].astype(BF16), spread, (((0,), (0,)), ((), ())), preferred_element_type=F32
     ).reshape(NZ, EDGE, NY)
-    from0, from1 = a0[...].astype(F32), a1[...].astype(F32)
-    before = jnp.where(gx_even, from1, from0)
-    after = jnp.where(gx_even, from0, from1)
+    low0, high0, low1, high1 = (
+        thick[NZ + k * EZ : NZ + (k + 1) * EZ].astype(F32).reshape(NZ, NY) for thick in (a0, a1) for k in range(2)
+    )
+    before = jnp.where(gx_even, high1, high0)
+    after = jnp.where(gx_even, low0, low1)
+    shape = (HROWS, 18 * EDGE)
+    row_a, lane_a = rows_of(shape), lanes(shape)
+    across = jnp.where(row_a // 3 == lane_a // EDGE, hat_product(lax.rem(row_a, 3), lax.rem(lane_a, EDGE)), 0.0)
+    along = along_y(hat_product, 3)
     total = jnp.zeros((HROWS, 128), F32)
     lane2, row2 = lanes((EDGE, NY)), rows_of((EDGE, NY))
     for ez in range(EZ):
@@ -215,7 +228,8 @@
         for p in range(len(PAIRS)):
             for w in range(3):
                 slabs[(p * 3 + w) * EDGE : (p * 3 + w + 1) * EDGE, :] = collected[p][w]
-        total = total + exact_dot(exact_dot(across[...], slabs[...]), along[ez])
+        found = exact_dot(exact_dot(across, slabs[...]), along)
+        total = total + (pltpu.roll(found, ez * EYD, 1) if ez else found)
     packed[...] = pltpu.roll(total, lax.rem(gx, 4) * NEL, 1)
     element, lane_e = rows_of((EYD, 128)), lanes((EYD, 128))
     unfold = (lane_e // EDGE == element).astype(F32).astype(BF16)
@@ -226,7 +240,6 @@
 
 
 def moments(ref, faces_x, faces_y, fractions):
-    across, along = moment_tables()
     vmem = pl.BlockSpec(memory_space=pltpu.VMEM)
     return pl.pallas_call(
         functools.partial(moments_kernel, lax.axis_size("gy")),
@@ -235,34 +248,34 @@
             jax.ShapeDtypeStruct((HROWS, 128), F32),
             jax.ShapeDtypeStruct((EZ, 8, 128), F32),
         ),
-        in_specs=[vmem] * 8,
+        in_specs=[vmem] * 6,
         out_specs=(vmem,) * 3,
         scratch_shapes=[pltpu.VMEM((8, NZ * EDGE), F32), pltpu.VMEM((18 * EDGE, NY), F32)],
+        compiler_params=pltpu.CompilerParams(vmem_limit_bytes=LIMIT),
+        cost_estimate=takes(2.2),
         name="moments",
-    )(ref, *faces_x, *faces_y, fractions, jnp.asarray(across), jnp.asarray(along))
-
-
-def warp_kernel(place, b0, b1, b2, b3, b4, ref, grad, portions, across, along, mismatch, packed, bricks, slabs, sems):
+    )(ref, *faces_x, *faces_y, fractions)
+
+
+def warp_kernel(place, b0, b1, b2, b3, b4, ref, grad, portions, mismatch, packed, bricks, tables, slabs):
     gx = lax.axis_index("gx")
-    copies = [pltpu.make_async_copy(src, bricks.at[i], sems.at[i]) for i, src in enumerate((b0, b1, b2, b3, b4))]
-    for copy in copies:
-        copy.start()
-    for copy in copies:
-        copy.wait()
+    for i, source in enumerate((b0, b1, b2, b3, b4)):
+        bricks[i] = source[...]
     flat = (EDGE * EDGE, NY)
     lane = lanes(flat)
     at_x_rim = lax.rem(lax.broadcasted_iota(jnp.int32, flat, 0), EDGE) == EDGE - 1
     at_y_rim = lax.rem(lane, EDGE) == EDGE - 1
+    shape = (16, 6 * EDGE)
+    row_a, lane_a = rows_of(shape), lanes(shape)
+    across = jnp.where(lax.rem(row_a, 8) == lane_a // EDGE, hat_weight(row_a // 8, lax.rem(lane_a, EDGE)), 0.0)
+    along = along_y(hat_weight, 2)
+    along = jnp.concatenate([along, pltpu.roll(along, 2 * NEL, 1)], axis=0)
     total = jnp.zeros((8, 128), F32)
     for ez in range(EZ):
 
-        def visit(b, fetched, ez=ez):
-            code = place[ez * EYD + b]
-            slab = bricks[code // 8].reshape(flat).astype(F32)
-            turned = pltpu.roll(slab, lax.rem((b - lax.rem(code, 8) + EYD) * EDGE, NY), 1)
-            return jnp.where(lane // EDGE == b, turned, fetched)
-
-        blended = lax.fori_loop(0, EYD, visit, jnp.zeros(flat, F32))
+        codes = [place[ez * EYD + b] for b in range(EYD)]
+        found = [bricks[code // 8].reshape(flat) for code in codes]
+        blended = gather_columns(tables.at[ez], found, [lax.rem(code, 8) for code in codes], range(EYD))
         portion = portions[ez]
         ty, tx, tz = portion[2:3, :], portion[1:2, :], portion[0:1, :]
         shifted = jnp.where(at_y_rim, blended, pltpu.roll(blended, NY - 1, 1))
@@ -284,28 +297,30 @@
         for c in range(3):
             for a in range(2):
                 slabs[(c * 2 + a) * EDGE : (c * 2 + a + 1) * EDGE, :] = collected[c][a]
-        summed = exact_dot(across[...], slabs[...])
-        total = total + exact_dot(jnp.concatenate([summed[:8], summed[8:]], axis=1), along[ez])
-    packed[...] = pltpu.roll(total, lax.rem(gx, 4) * NEL, 1)
+        summed = exact_dot(across, slabs[...])
+        found = exact_dot(jnp.concatenate([summed[:8], summed[8:]], axis=1), along)
+        total = total + (pltpu.roll(found, ez * EYD, 1) if ez else found)
+    packed[...] = jnp.broadcast_to(pltpu.roll(total, lax.rem(gx, 4) * NEL, 1), packed.shape)
 
 
 def warp(place, bricks, ref, grad, portions):
-    across, along = load_tables()
     smem = pl.BlockSpec(memory_space=pltpu.SMEM)
     vmem = pl.BlockSpec(memory_space=pltpu.VMEM)
-    anywhere = pl.BlockSpec(memory_space=pl.ANY)
+    devices = lax.axis_size("gx") * lax.axis_size("gy")
     return pl.pallas_call(
         warp_kernel,
-        out_shape=(jax.ShapeDtypeStruct((NZ, EDGE, NY), F32), jax.ShapeDtypeStruct((8, 128), F32)),
-        in_specs=[smem] + [anywhere] * 5 + [vmem] * 5,
+        out_shape=(jax.ShapeDtypeStruct((NZ, EDGE, NY), F32), jax.ShapeDtypeStruct((devices, 8, 128), F32)),
+        in_specs=[smem] + [vmem] * 8,
         out_specs=(vmem, vmem),
         scratch_shapes=[
             pltpu.VMEM((5, EDGE, EDGE, NY), BF16),
+            pltpu.VMEM((EZ, EYD * NY, NY), BF16),
             pltpu.VMEM((6 * EDGE, NY), F32),
-            pltpu.SemaphoreType.DMA((5,)),
         ],
+        compiler_params=pltpu.CompilerParams(vmem_limit_bytes=LIMIT),
+        cost_estimate=takes(4.0),
         name="warp",
-    )(place, *bricks, ref, grad, portions, jnp.asarray(across), jnp.asarray(along))
+    )(place, *bricks, ref, grad, portions)
 
 
 def spread_groups(block_of, groups, gx_count, store):
@@ -323,12 +338,13 @@
 
 def solve_kernel(gx_count, gy_count, hess, load, out, coef, rhs):
     gx, gy = lax.axis_index("gx"), lax.axis_index("gy")
+    steps = gather_steps(gx_count, gy_count)
     tiles = -(-gx_count // 4)
     width = 128 * tiles
 
     def unpack(row, _):
         def hess_block(column):
-            return hess[jnp.bitwise_xor(row, gy) * gx_count + jnp.bitwise_xor(gx, column)]
+            return hess[block_index(steps, dict(gx=jnp.bitwise_xor(gx, column), gy=jnp.bitwise_xor(gy, row)))]
 
         def store_hess(group, tile, value):
             coef[tile, pl.ds(row * 3 * HROWS + group * HROWS, HROWS), :] = value
@@ -473,7 +489,8 @@
             pltpu.VMEM((tiles, gy_count * 3 * HROWS, 128), F32),
             pltpu.VMEM((tiles, gy_count * 32, 128), F32),
         ],
-        compiler_params=pltpu.CompilerParams(vmem_limit_bytes=48 * 1024 * 1024),
+        compiler_params=pltpu.CompilerParams(vmem_limit_bytes=LIMIT),
+        cost_estimate=takes(3.5),
         name="solve",
     )(hess, load)
 
@@ -501,31 +518,53 @@
     return swap(array, "gy", partner)
 
 
-def everyones(block):
-    known = block[None]
-    for axis in ("gx", "gy"):
-        step = 1
-        while step < lax.axis_size(axis):
-            known = jnp.concatenate([known, swap(known, axis, lambda i, step=step: i ^ step)], axis=0)
-            step *= 2
-    return known
+def gather_steps(gx_count, gy_count):
+    steps = []
+    for axis, size in (("gy", gy_count), ("gx", gx_count)):
+        bit = size // 2
+        while bit:
+            steps.append((axis, bit))
+            bit //= 2
+    return steps
+
+
+def block_index(steps, relative):
+    found = 0
+    for k, (axis, bit) in enumerate(steps):
+        found = found + jnp.where(jnp.bitwise_and(relative[axis], bit) != 0, 1 << k, 0)
+    return found
 
 
 def body(reference_image, deformed_image, route, within, xshift, fractions):
-    d0, d1 = swap_x(deformed_image, 0), swap_x(deformed_image, 1)
-    m0, m1, m2, m3, f0, f1, own, place = ask(
-        route.reshape(NEL), within.reshape(NEL), xshift.reshape(NEL), reference_image
+    m0, m1, m2, m3, thick, own, place = ask(
+        route.reshape(NEL), within.reshape(NEL), xshift.reshape(NEL), reference_image, deformed_image
     )
-    a0, a1 = swap_x(f0, 0), swap_x(f1, 1)
     q = [swap_y(m, kind) for kind, m in enumerate((m0, m1, m2, m3))]
-    *served, at_home = serve(deformed_image, d0, d1, (*q, own))
-    bricks = [swap_y(s, kind) for kind, s in enumerate(served)] + [at_home]
-    grad, packed, portions = moments(reference_image, (a0, a1), (q[0], q[1]), fractions.reshape(NEL, 3))
-    hess = everyones(packed)
-    mismatch, part = warp(place, bricks, reference_image, grad, portions)
-    devices = lax.axis_size("gx") * lax.axis_size("gy")
-    load = lax.all_to_all(jnp.broadcast_to(part[None], (devices, 8, 128)), ("gx", "gy"), 0, 0)
-    return solve(hess, load), mismatch
+    d0, d1 = swap_x(thick, 0), swap_x(thick, 1)
+    *q, d0, d1 = lax.optimization_barrier((*q, d0, d1))
+    image, _ = lax.optimization_barrier((reference_image, q))
+    grad, packed, portions = moments(image, (d0, d1), (q[0], q[1]), fractions.reshape(NEL, 3))
+    q[2], packed = lax.optimization_barrier((q[2], packed))
+    served = serve(deformed_image, d0, d1, q, (8, 9, 2, 3))
+    own, _ = lax.optimization_barrier((own, served))
+    (at_home,) = serve(deformed_image, d0, d1, [own], (4,))
+    known = packed[None]
+    bricks = [swap_y(block, kind) for kind, block in enumerate(served)] + [at_home]
+    steps = gather_steps(lax.axis_size("gx"), lax.axis_size("gy"))
+    for k, (axis, bit) in enumerate(steps):
+        if k == 1:
+            known, _ = lax.optimization_barrier((known, at_home))
+        if k == len(steps) - 3:
+            bricks, known = lax.optimization_barrier((bricks, known))
+            mismatch, part = warp(place, bricks, reference_image, grad, portions)
+        if k == len(steps) - 2:
+            known, part = lax.optimization_barrier((known, part))
+            load = lax.all_to_all(part, ("gx", "gy"), 0, 0)
+        pieces = 4 if k + 1 == len(steps) else 1
+        size = known.shape[0] // pieces
+        sent = [swap(known[i * size : (i + 1) * size], axis, lambda i, bit=bit: i ^ bit) for i in range(pieces)]
+        known = jnp.concatenate([known, *sent], axis=0)
+    return solve(known, load), mismatch
 
 
 def solution(mesh):

time: 102 us -> 58.1 us (0.57)
  waiting for transfers between devices: 37.1 us -> 16.2 us
  Pallas kernels: 25 us -> 15 us
  starting transfers between devices: 33.5 us -> 24.4 us
  local copies, waits for them, and re-layouts: 4.14 us -> 1.47 us
    ppermute x17 -> x18, waiting for transfers between devices: 29.4 us -> 10.9 us  [swap(): lax.ppermute(array, axis, [(i, j) for i, j in pairs if 0 <= j < size])]
    ppermute x17 -> x18, starting transfers between devices: 30.9 us -> 21.8 us  [swap(): lax.ppermute(array, axis, [(i, j) for i, j in pairs if 0 <= j < size])]
    pallas_call x1 -> x2, Pallas kernels: 7.16 us -> 2.77 us  [serve(): pl.pallas_call(functools.partial(serve_kernel, lines), out_shape=(jax.Sha...]
    pallas_call x1, Pallas kernels: 8.24 us -> 4.04 us  [warp(): pl.pallas_call(warp_kernel, out_shape=(jax.ShapeDtypeStruct((NZ, EDGE, NY...]
    all_to_all x1, waiting for transfers between devices: 7.69 us -> 5.32 us  [body(): load = lax.all_to_all(part, ('gx', 'gy'), 0, 0)]
    pallas_call x1, Pallas kernels: 4.02 us -> 2.23 us  [moments(): pl.pallas_call(functools.partial(moments_kernel, lax.axis_size('gy')), ou...]
    broadcast_in_dim x1 -> x0, local copies, waits for them, and re-layouts: 1.35 us -> none  [body(): jnp.broadcast_to(part[None], (devices, 8, 128))]
    unnamed x38 -> x17, local copies, waits for them, and re-layouts: 2.04 us -> 1.34 us
  transfers between devices with their start and end apart: 18 -> 19, of which waited for: 9 -> 8; matrix products, arithmetic and copies ran while one was open for 2% -> 0% of each run, Pallas kernels for 15% -> 12%
where the time goes in v2:
time: 58.1 us; the launch traced here: 57.9 us
  starting transfers between devices  24.4 us (42%)
  waiting for transfers between devices  16.2 us (28%)
  Pallas kernels  15 us (26%)
  local copies, waits for them, and re-layouts  1.47 us (3%)
  between operations  0.84 us (1%)
    ppermute x18, starting transfers between devices, swap(): lax.ppermute(array, axis, [(i, j) for i, j in pairs if 0 <= j < size])  21.8 us
    ppermute x18, waiting for transfers between devices, swap(): lax.ppermute(array, axis, [(i, j) for i, j in pairs if 0 <= j < size])  10.9 us
    all_to_all x1, waiting for transfers between devices, body(): load = lax.all_to_all(part, ('gx', 'gy'), 0, 0)  5.32 us
    pallas_call x1, Pallas kernels, warp(): pl.pallas_call(warp_kernel, out_shape=(jax.ShapeDtypeStruct((NZ, EDGE, NY...  4.04 us
    pallas_call x1, Pallas kernels, solve(): pl.pallas_call(functools.partial(solve_kernel, gx_count, gy_count), out_s...  3.58 us
    pallas_call x2, Pallas kernels, serve(): pl.pallas_call(functools.partial(serve_kernel, lines), out_shape=(jax.Sha...  2.77 us
    all_to_all x1, starting transfers between devices, body(): load = lax.all_to_all(part, ('gx', 'gy'), 0, 0)  2.57 us
    pallas_call x1, Pallas kernels, ask(): pl.pallas_call(functools.partial(ask_kernel, lax.axis_size('gx')), out_sh...  2.34 us
  transfers between devices with their start and end apart: 19, of which 8 were waited for; matrix products, arithmetic and copies ran while one was open for 0% of the time, Pallas kernels for 12%

profile of v2, /device:TPU:0, one launch (start us, length us, event | category | flops | bytes accessed | tf_op | source)
XLA Modules:
  0.0 57.9 jit_solution(5767999178603259363)
XLA Ops:
  0.6 2.3 %ask.1 = (f32[16,128]{1,0:T(8,128)}, f32[16,128]{1,0:T(8,128)}, f32[8,128]{1,0:T(8,128)}, f32[8,128]{1,0:T(8,128)}, bf16[72,16,128]{2,1,0:T(8,128)(2,1)}, /*index=5*/f32[8,128]{1,0:T(8,128)}, s32[32]{0:T(128)}) custom-call(s32[32]{0:T(128)} %bitcast.8, s32[32]{0:T(128)} %bitcast.9, s32[32]{0:T(128)} %bitcast.10, bf16[64,16,128]{2,1,0:T(8,128)(2,1)} %ref.4, ...), custom_call_target="tpu_custom_call" | custom-call | bytes 7380000 | tf_op jit(solution)/shard_map/ask/pallas_call | solution.py:116
  3.0 0.5 collective-permute-start.4
  3.5 0.7 %collective-permute-start.5 = (bf16[72,16,128]{2,1,0:T(8,128)(2,1)}, bf16[72,16,128]{2,1,0:T(8,128)(2,1)S(1)}, u32[]{:S(2)}, u32[]{:S(2)}) collective-permute-start(bf16[72,16,128]{2,1,0:T(8,128)(2,1)} %get-tuple-element.41), channel_id=1, source_target_pairs={{8,16},{16,8},{9,17},{17,9},{10,18},{18,10},{11,19},{19,11},{12,20... | collective-permute-start | bytes 884744 | tf_op jit(solution)/shard_map/ppermute | solution.py:501
  4.2 2.7 %collective-permute-start.2 = (f32[8,128]{1,0:T(8,128)}, f32[8,128]{1,0:T(8,128)S(1)}, u32[]{:S(2)}, u32[]{:S(2)}) collective-permute-start(f32[8,128]{1,0:T(8,128)} %get-tuple-element.39), channel_id=1, source_target_pairs={{0,2},{1,3},{2,0},{3,1},{4,6},{5,7},{6,4},{7,5},{8,10},{9,11},{10,... | collective-permute-start | bytes 12296 | tf_op jit(solution)/shard_map/ppermute | solution.py:501
  6.9 1.5 %collective-permute-start = (f32[16,128]{1,0:T(8,128)}, f32[16,128]{1,0:T(8,128)S(1)}, u32[]{:S(2)}, u32[]{:S(2)}) collective-permute-start(f32[16,128]{1,0:T(8,128)} %get-tuple-element.37), channel_id=1, source_target_pairs={{0,1},{1,0},{2,3},{3,2},{4,5},{5,4},{6,7},{7,6},{8,9},{9,8},{10,11... | collective-permute-start | bytes 24584 | tf_op jit(solution)/shard_map/ppermute | solution.py:501
  8.3 2.4 %collective-permute-start.1 = (f32[16,128]{1,0:T(8,128)}, f32[16,128]{1,0:T(8,128)S(1)}, u32[]{:S(2)}, u32[]{:S(2)}) collective-permute-start(f32[16,128]{1,0:T(8,128)} %get-tuple-element.38), channel_id=1, source_target_pairs={{0,7},{1,2},{2,1},{3,4},{4,3},{5,6},{6,5},{7,0},{8,15},{9,10},{10,... | collective-permute-start | bytes 24584 | tf_op jit(solution)/shard_map/ppermute | solution.py:501
  10.8 1.9 %collective-permute-start.3 = (f32[8,128]{1,0:T(8,128)S(1)}, f32[8,128]{1,0:T(8,128)S(1)}, u32[]{:S(2)}, u32[]{:S(2)}) collective-permute-start(f32[8,128]{1,0:T(8,128)S(1)} %copy-done.5), channel_id=1, source_target_pairs={{0,6},{1,7},{2,4},{3,5},{4,2},{5,3},{6,0},{7,1},{8,14},{9,15},{10,... | collective-permute-start | bytes 12296 | tf_op jit(solution)/shard_map/ppermute | solution.py:501
  12.8 3.4 %collective-permute-done.3.refs_6_ = f32[8,128]{1,0:T(8,128)S(1)} collective-permute-done((f32[8,128]{1,0:T(8,128)S(1)}, f32[8,128]{1,0:T(8,128)S(1)}, u32[]{:S(2)}, u32[]{:S(2)}) %collective-permute-start.3) | collective-permute-done | bytes 4128 | tf_op jit(solution)/shard_map/ppermute | solution.py:501
  16.2 2.2 %moments.1 = (bf16[3,64,16,128]{3,2,1,0:T(8,128)(2,1)S(1)}, f32[56,128]{1,0:T(8,128)S(1)}, f32[4,8,128]{2,1,0:T(8,128)S(1)}) custom-call(bf16[64,16,128]{2,1,0:T(8,128)(2,1)S(1)} %copy-done, bf16[72,16,128]{2,1,0:T(8,128)(2,1)S(1)} %collective-permute-done.4.a0.refs_1_, bf16[72,16,128]{2,1,0:T(8,128)(2,1)S(1)} %collective-permute-done.5.a1.refs_2_, ...), custom_call_target="tpu_custom_call" | custom-call | bytes 8118000 | tf_op jit(solution)/shard_map/moments/pallas_call | solution.py:244
  18.5 1.8 %serve.2 = (bf16[16,16,128]{2,1,0:T(8,128)(2,1)S(1)}, bf16[16,16,128]{2,1,0:T(8,128)(2,1)S(1)}, bf16[16,16,128]{2,1,0:T(8,128)(2,1)S(1)}, bf16[16,16,128]{2,1,0:T(8,128)(2,1)S(1)}) custom-call(bf16[64,16,128]{2,1,0:T(8,128)(2,1)S(1)} %copy-done.1, bf16[72,16,128]{2,1,0:T(8,128)(2,1)S(1)} %collective-permute-done.4.a0.refs_1_, ...), custom_call_target="tpu_custom_call" | custom-call | bytes 6642000 | tf_op jit(solution)/shard_map/serve/pallas_call | solution.py:166
  20.3 0.7 %copy-done.2 = f32[8,128]{1,0:T(8,128)S(1)} copy-done((f32[8,128]{1,0:T(8,128)S(1)}, f32[8,128]{1,0:T(8,128)}, u32[]{:S(2)}) %copy-start.2) | copy-done | bytes 4120
  21.0 1.0 %serve.3.b4 = bf16[16,16,128]{2,1,0:T(8,128)(2,1)S(1)} custom-call(bf16[64,16,128]{2,1,0:T(8,128)(2,1)S(1)} %copy-done.1, bf16[72,16,128]{2,1,0:T(8,128)(2,1)S(1)} %collective-permute-done.4.a0.refs_1_, bf16[72,16,128]{2,1,0:T(8,128)(2,1)S(1)} %collective-permute-done.5.a1.refs_2_, f32[8,128]{1,0:T(8,128)S(1)} %copy-done.2), custom_call_target="tpu_custom_call" | custom-call | bytes 4428000 | tf_op jit(solution)/shard_map/serve/pallas_call | solution.py:166
  22.0 1.5 %collective-permute-done.10 = f32[1,56,128]{2,1,0:T(8,128)S(1)} collective-permute-done((f32[1,56,128]{2,1,0:T(8,128)S(1)}, f32[1,56,128]{2,1,0:T(8,128)S(1)}, u32[]{:S(2)}, u32[]{:S(2)}) %collective-permute-start.10) | collective-permute-done | bytes 28704 | tf_op jit(solution)/shard_map/ppermute | solution.py:501
  23.5 1.0 %collective-permute-start.11 = (f32[2,56,128]{2,1,0:T(8,128)S(1)}, f32[2,56,128]{2,1,0:T(8,128)S(1)}, u32[]{:S(2)}, u32[]{:S(2)}) collective-permute-start(f32[2,56,128]{2,1,0:T(8,128)S(1)} %pad_maximum_fusion.2), channel_id=1, source_target_pairs={{0,2},{1,3},{2,0},{3,1},{4,6},{5,7},{6,4},{7,5},{8,10},{9,11},{10,... | collective-permute-start | bytes 172040 | tf_op jit(solution)/shard_map/ppermute | solution.py:501
  24.5 1.5 %collective-permute-start.6 = (bf16[16,16,128]{2,1,0:T(8,128)(2,1)S(1)}, bf16[16,16,128]{2,1,0:T(8,128)(2,1)S(1)}, u32[]{:S(2)}, u32[]{:S(2)}) collective-permute-start(bf16[16,16,128]{2,1,0:T(8,128)(2,1)S(1)} %get-tuple-element.51), channel_id=1, source_target_pairs={{0,1},{1,0},{2,3},{3,2},{4,5},{5,4},{6,7},{7,6},{8,9},{9,8},{10,11... | collective-permute-start | bytes 196616 | tf_op jit(solution)/shard_map/ppermute | solution.py:501
  26.0 1.9 %collective-permute-start.7 = (bf16[16,16,128]{2,1,0:T(8,128)(2,1)S(1)}, bf16[16,16,128]{2,1,0:T(8,128)(2,1)S(1)}, u32[]{:S(2)}, u32[]{:S(2)}) collective-permute-start(bf16[16,16,128]{2,1,0:T(8,128)(2,1)S(1)} %get-tuple-element.52), channel_id=1, source_target_pairs={{0,7},{1,2},{2,1},{3,4},{4,3},{5,6},{6,5},{7,0},{8,15},{9,10},{10,... | collective-permute-start | bytes 196616 | tf_op jit(solution)/shard_map/ppermute | solution.py:501
  27.9 0.1 collective-permute-start.8
  28.0 1.9 %collective-permute-start.9 = (bf16[16,16,128]{2,1,0:T(8,128)(2,1)S(1)}, bf16[16,16,128]{2,1,0:T(8,128)(2,1)S(1)}, u32[]{:S(2)}, u32[]{:S(2)}) collective-permute-start(bf16[16,16,128]{2,1,0:T(8,128)(2,1)S(1)} %get-tuple-element.54), channel_id=1, source_target_pairs={{0,6},{1,7},{2,4},{3,5},{4,2},{5,3},{6,0},{7,1},{8,14},{9,15},{10,... | collective-permute-start | bytes 196616 | tf_op jit(solution)/shard_map/ppermute | solution.py:501
  29.9 3.9 %collective-permute-done.7.b1 = bf16[16,16,128]{2,1,0:T(8,128)(2,1)S(1)} collective-permute-done((bf16[16,16,128]{2,1,0:T(8,128)(2,1)S(1)}, bf16[16,16,128]{2,1,0:T(8,128)(2,1)S(1)}, u32[]{:S(2)}, u32[]{:S(2)}) %collective-permute-start.7) | collective-permute-done | bytes 65568 | tf_op jit(solution)/shard_map/ppermute | solution.py:501
  33.8 0.4 collective-permute-done.9.b3
  34.2 1.6 %collective-permute-start.12 = (f32[4,56,128]{2,1,0:T(8,128)S(1)}, f32[4,56,128]{2,1,0:T(8,128)S(1)}, u32[]{:S(2)}, u32[]{:S(2)}) collective-permute-start(f32[4,56,128]{2,1,0:T(8,128)S(1)} %pad_maximum_fusion.1), channel_id=1, source_target_pairs={{0,1},{1,0},{2,3},{3,2},{4,5},{5,4},{6,7},{7,6},{8,9},{9,8},{10,11... | collective-permute-start | bytes 344072 | tf_op jit(solution)/shard_map/ppermute | solution.py:501
  35.8 0.6 %copy-done.3 = s32[32]{0:T(128)S(1)} copy-done((s32[32]{0:T(128)S(1)}, s32[32]{0:T(128)}, u32[]{:S(2)}) %copy-start.3) | copy-done | bytes 152
  36.4 4.0 %warp.1 = (f32[64,16,128]{2,1,0:T(8,128)}, f32[32,8,128]{2,1,0:T(8,128)}) custom-call(s32[32]{0:T(128)S(1)} %copy-done.3, bf16[16,16,128]{2,1,0:T(8,128)(2,1)S(1)} %collective-permute-done.6.b0, bf16[16,16,128]{2,1,0:T(8,128)(2,1)S(1)} %collective-permute-done.7.b1, bf16[16,16,128]{2,1,0:T(8,128)(2,1)S(1)} %collective-permute-done.8.b2, ...), custom_call_target="tpu_custom_call" | custom-call | bytes 14760000 | tf_op jit(solution)/shard_map/warp/pallas_call | solution.py:310
  40.5 2.9 %collective-permute-start.13 = (f32[8,56,128]{2,1,0:T(8,128)S(1)}, f32[8,56,128]{2,1,0:T(8,128)S(1)}, u32[]{:S(2)}, u32[]{:S(2)}) collective-permute-start(f32[8,56,128]{2,1,0:T(8,128)S(1)} %pad_maximum_fusion), channel_id=1, source_target_pairs={{0,16},{8,24},{16,0},{24,8},{1,17},{9,25},{17,1},{25,9},{2,18},{10... | collective-permute-start | bytes 688136 | tf_op jit(solution)/shard_map/ppermute | solution.py:501
  43.5 0.5 collective-permute-start.15
  44.0 2.6 %all-to-all-start = ((f32[32,8,128]{2,1,0:T(8,128)}), f32[32,8,128]{2,1,0:T(8,128)S(1)}, u32[]{:S(2)}, u32[]{:S(2)}) async-start(f32[32,8,128]{2,1,0:T(8,128)} %get-tuple-element.70), calls=%async_computation | async-start | bytes 262144 | tf_op jit(solution)/shard_map/all_to_all | solution.py:562
  46.6 0.8 %collective-permute-done.13 = f32[8,56,128]{2,1,0:T(8,128)S(1)} collective-permute-done((f32[8,56,128]{2,1,0:T(8,128)S(1)}, f32[8,56,128]{2,1,0:T(8,128)S(1)}, u32[]{:S(2)}, u32[]{:S(2)}) %collective-permute-start.13) | collective-permute-done | bytes 229408 | tf_op jit(solution)/shard_map/ppermute | solution.py:501
  47.5 0.5 collective-permute-start.17
  48.1 0.7 %collective-permute-done.16 = f32[4,56,128]{2,1,0:T(8,128)S(1)} collective-permute-done((f32[4,56,128]{2,1,0:T(8,128)S(1)}, f32[4,56,128]{2,1,0:T(8,128)S(1)}, u32[]{:S(2)}, u32[]{:S(2)}) %collective-permute-start.16) | collective-permute-done | bytes 114720 | tf_op jit(solution)/shard_map/ppermute | solution.py:501
  48.8 0.2 collective-permute-done.17
  49.0 5.3 %all-to-all-done.load = f32[32,8,128]{2,1,0:T(8,128)S(1)} async-done(((f32[32,8,128]{2,1,0:T(8,128)}), f32[32,8,128]{2,1,0:T(8,128)S(1)}, u32[]{:S(2)}, u32[]{:S(2)}) %all-to-all-start) | async-done | bytes 131104 | tf_op jit(solution)/shard_map/all_to_all | solution.py:562
  54.3 3.6 %solve.1 = f32[3,5,1,8]{3,2,1,0:T(1,128)} custom-call(f32[32,56,128]{2,1,0:T(8,128)S(1)} %constant_dynamic-update-slice_fusion.hess, f32[32,8,128]{2,1,0:T(8,128)S(1)} %all-to-all-done.load), custom_call_target="tpu_custom_call" | custom-call | bytes 12915000 | tf_op jit(solution)/shard_map/solve/pallas_call | solution.py:483
  (36 shorter events, 0.4 us)
Async XLA Ops:
  0.6 15.6 %copy-start = (bf16[64,16,128]{2,1,0:T(8,128)(2,1)S(1)}, bf16[64,16,128]{2,1,0:T(8,128)(2,1)}, u32[]{:S(2)}) copy-start(bf16[64,16,128]{2,1,0:T(8,128)(2,1)} %ref.4) | copy-start | bytes 786436
  3.0 7.8 %copy-start.5 = (f32[8,128]{1,0:T(8,128)S(1)}, f32[8,128]{1,0:T(8,128)}, u32[]{:S(2)}) copy-start(f32[8,128]{1,0:T(8,128)} %get-tuple-element.40) | copy-start | bytes 12292
  3.0 13.2 %collective-permute-start.4 = (bf16[72,16,128]{2,1,0:T(8,128)(2,1)}, bf16[72,16,128]{2,1,0:T(8,128)(2,1)S(1)}, u32[]{:S(2)}, u32[]{:S(2)}) collective-permute-start(bf16[72,16,128]{2,1,0:T(8,128)(2,1)} %get-tuple-element.41), channel_id=1, source_target_pairs={{0,8},{8,0},{16,24},{24,16},{1,9},{9,1},{17,25},{25,17},{2,10},{10... | collective-permute-start | bytes 884744 | tf_op jit(solution)/shard_map/ppermute | solution.py:501
  3.5 12.7 %collective-permute-start.5 = (bf16[72,16,128]{2,1,0:T(8,128)(2,1)}, bf16[72,16,128]{2,1,0:T(8,128)(2,1)S(1)}, u32[]{:S(2)}, u32[]{:S(2)}) collective-permute-start(bf16[72,16,128]{2,1,0:T(8,128)(2,1)} %get-tuple-element.41), channel_id=1, source_target_pairs={{8,16},{16,8},{9,17},{17,9},{10,18},{18,10},{11,19},{19,11},{12,20... | collective-permute-start | bytes 884744 | tf_op jit(solution)/shard_map/ppermute | solution.py:501
  4.2 6.6 %collective-permute-start.2 = (f32[8,128]{1,0:T(8,128)}, f32[8,128]{1,0:T(8,128)S(1)}, u32[]{:S(2)}, u32[]{:S(2)}) collective-permute-start(f32[8,128]{1,0:T(8,128)} %get-tuple-element.39), channel_id=1, source_target_pairs={{0,2},{1,3},{2,0},{3,1},{4,6},{5,7},{6,4},{7,5},{8,10},{9,11},{10,... | collective-permute-start | bytes 12296 | tf_op jit(solution)/shard_map/ppermute | solution.py:501
  6.8 5.8 %copy-start.4 = (s32[1,1,32,3]{2,1,3,0:T(1,128)S(1)}, s32[1,1,32,3]{2,1,3,0:T(1,128)}, u32[]{:S(2)}) copy-start(s32[1,1,32,3]{2,1,3,0:T(1,128)} %param.11) | copy-start | bytes 1156
  6.9 9.4 %collective-permute-start = (f32[16,128]{1,0:T(8,128)}, f32[16,128]{1,0:T(8,128)S(1)}, u32[]{:S(2)}, u32[]{:S(2)}) collective-permute-start(f32[16,128]{1,0:T(8,128)} %get-tuple-element.37), channel_id=1, source_target_pairs={{0,1},{1,0},{2,3},{3,2},{4,5},{5,4},{6,7},{7,6},{8,9},{9,8},{10,11... | collective-permute-start | bytes 24584 | tf_op jit(solution)/shard_map/ppermute | solution.py:501
  8.3 7.9 %collective-permute-start.1 = (f32[16,128]{1,0:T(8,128)}, f32[16,128]{1,0:T(8,128)S(1)}, u32[]{:S(2)}, u32[]{:S(2)}) collective-permute-start(f32[16,128]{1,0:T(8,128)} %get-tuple-element.38), channel_id=1, source_target_pairs={{0,7},{1,2},{2,1},{3,4},{4,3},{5,6},{6,5},{7,0},{8,15},{9,10},{10,... | collective-permute-start | bytes 24584 | tf_op jit(solution)/shard_map/ppermute | solution.py:501
  10.8 5.4 %collective-permute-start.3 = (f32[8,128]{1,0:T(8,128)S(1)}, f32[8,128]{1,0:T(8,128)S(1)}, u32[]{:S(2)}, u32[]{:S(2)}) collective-permute-start(f32[8,128]{1,0:T(8,128)S(1)} %copy-done.5), channel_id=1, source_target_pairs={{0,6},{1,7},{2,4},{3,5},{4,2},{5,3},{6,0},{7,1},{8,14},{9,15},{10,... | collective-permute-start | bytes 12296 | tf_op jit(solution)/shard_map/ppermute | solution.py:501
  16.2 2.3 %copy-start.1 = (bf16[64,16,128]{2,1,0:T(8,128)(2,1)S(1)}, bf16[64,16,128]{2,1,0:T(8,128)(2,1)}, u32[]{:S(2)}) copy-start(bf16[64,16,128]{2,1,0:T(8,128)(2,1)} %refs_0_.3) | copy-start | bytes 786436
  18.5 5.0 %collective-permute-start.10 = (f32[1,56,128]{2,1,0:T(8,128)S(1)}, f32[1,56,128]{2,1,0:T(8,128)S(1)}, u32[]{:S(2)}, u32[]{:S(2)}) collective-permute-start(f32[1,56,128]{2,1,0:T(8,128)S(1)} %bitcast.6), channel_id=1, source_target_pairs={{0,4},{1,5},{2,6},{3,7},{4,0},{5,1},{6,2},{7,3},{8,12},{9,13},{10,... | collective-permute-start | bytes 86024 | tf_op jit(solution)/shard_map/ppermute | solution.py:501
  20.3 0.7 %copy-start.2 = (f32[8,128]{1,0:T(8,128)S(1)}, f32[8,128]{1,0:T(8,128)}, u32[]{:S(2)}) copy-start(f32[8,128]{1,0:T(8,128)} %get-tuple-element.56.refs_3_) | copy-start | bytes 12292
  23.5 6.4 %collective-permute-start.11 = (f32[2,56,128]{2,1,0:T(8,128)S(1)}, f32[2,56,128]{2,1,0:T(8,128)S(1)}, u32[]{:S(2)}, u32[]{:S(2)}) collective-permute-start(f32[2,56,128]{2,1,0:T(8,128)S(1)} %pad_maximum_fusion.2), channel_id=1, source_target_pairs={{0,2},{1,3},{2,0},{3,1},{4,6},{5,7},{6,4},{7,5},{8,10},{9,11},{10,... | collective-permute-start | bytes 172040 | tf_op jit(solution)/shard_map/ppermute | solution.py:501
  24.5 5.4 %collective-permute-start.6 = (bf16[16,16,128]{2,1,0:T(8,128)(2,1)S(1)}, bf16[16,16,128]{2,1,0:T(8,128)(2,1)S(1)}, u32[]{:S(2)}, u32[]{:S(2)}) collective-permute-start(bf16[16,16,128]{2,1,0:T(8,128)(2,1)S(1)} %get-tuple-element.51), channel_id=1, source_target_pairs={{0,1},{1,0},{2,3},{3,2},{4,5},{5,4},{6,7},{7,6},{8,9},{9,8},{10,11... | collective-permute-start | bytes 196616 | tf_op jit(solution)/shard_map/ppermute | solution.py:501
  26.0 7.8 %collective-permute-start.7 = (bf16[16,16,128]{2,1,0:T(8,128)(2,1)S(1)}, bf16[16,16,128]{2,1,0:T(8,128)(2,1)S(1)}, u32[]{:S(2)}, u32[]{:S(2)}) collective-permute-start(bf16[16,16,128]{2,1,0:T(8,128)(2,1)S(1)} %get-tuple-element.52), channel_id=1, source_target_pairs={{0,7},{1,2},{2,1},{3,4},{4,3},{5,6},{6,5},{7,0},{8,15},{9,10},{10,... | collective-permute-start | bytes 196616 | tf_op jit(solution)/shard_map/ppermute | solution.py:501
  27.9 5.9 %collective-permute-start.8 = (bf16[16,16,128]{2,1,0:T(8,128)(2,1)S(1)}, bf16[16,16,128]{2,1,0:T(8,128)(2,1)S(1)}, u32[]{:S(2)}, u32[]{:S(2)}) collective-permute-start(bf16[16,16,128]{2,1,0:T(8,128)(2,1)S(1)} %get-tuple-element.53), channel_id=1, source_target_pairs={{0,2},{1,3},{2,0},{3,1},{4,6},{5,7},{6,4},{7,5},{8,10},{9,11},{10,... | collective-permute-start | bytes 196616 | tf_op jit(solution)/shard_map/ppermute | solution.py:501
  28.0 6.2 %collective-permute-start.9 = (bf16[16,16,128]{2,1,0:T(8,128)(2,1)S(1)}, bf16[16,16,128]{2,1,0:T(8,128)(2,1)S(1)}, u32[]{:S(2)}, u32[]{:S(2)}) collective-permute-start(bf16[16,16,128]{2,1,0:T(8,128)(2,1)S(1)} %get-tuple-element.54), channel_id=1, source_target_pairs={{0,6},{1,7},{2,4},{3,5},{4,2},{5,3},{6,0},{7,1},{8,14},{9,15},{10,... | collective-permute-start | bytes 196616 | tf_op jit(solution)/shard_map/ppermute | solution.py:501
  34.2 6.3 %collective-permute-start.12 = (f32[4,56,128]{2,1,0:T(8,128)S(1)}, f32[4,56,128]{2,1,0:T(8,128)S(1)}, u32[]{:S(2)}, u32[]{:S(2)}) collective-permute-start(f32[4,56,128]{2,1,0:T(8,128)S(1)} %pad_maximum_fusion.1), channel_id=1, source_target_pairs={{0,1},{1,0},{2,3},{3,2},{4,5},{5,4},{6,7},{7,6},{8,9},{9,8},{10,11... | collective-permute-start | bytes 344072 | tf_op jit(solution)/shard_map/ppermute | solution.py:501
  35.8 0.6 %copy-start.3 = (s32[32]{0:T(128)S(1)}, s32[32]{0:T(128)}, u32[]{:S(2)}) copy-start(s32[32]{0:T(128)} %get-tuple-element.60.place) | copy-start | bytes 388
  40.5 6.9 %collective-permute-start.13 = (f32[8,56,128]{2,1,0:T(8,128)S(1)}, f32[8,56,128]{2,1,0:T(8,128)S(1)}, u32[]{:S(2)}, u32[]{:S(2)}) collective-permute-start(f32[8,56,128]{2,1,0:T(8,128)S(1)} %pad_maximum_fusion), channel_id=1, source_target_pairs={{0,16},{8,24},{16,0},{24,8},{1,17},{9,25},{17,1},{25,9},{2,18},{10... | collective-permute-start | bytes 688136 | tf_op jit(solution)/shard_map/ppermute | solution.py:501
  43.4 4.6 %collective-permute-start.14 = (f32[4,56,128]{2,1,0:T(8,128)S(1)}, f32[4,56,128]{2,1,0:T(8,128)S(1)}, u32[]{:S(2)}, u32[]{:S(2)}) collective-permute-start(f32[4,56,128]{2,1,0:T(8,128)S(1)} %get-tuple-element.75), channel_id=1, source_target_pairs={{0,8},{8,0},{16,24},{24,16},{1,9},{9,1},{17,25},{25,17},{2,10},{10... | collective-permute-start | bytes 344072 | tf_op jit(solution)/shard_map/ppermute | solution.py:501
  43.5 4.5 %collective-permute-start.15 = (f32[4,56,128]{2,1,0:T(8,128)S(1)}, f32[4,56,128]{2,1,0:T(8,128)S(1)}, u32[]{:S(2)}, u32[]{:S(2)}) collective-permute-start(f32[4,56,128]{2,1,0:T(8,128)S(1)} %get-tuple-element.74), channel_id=1, source_target_pairs={{0,8},{8,0},{16,24},{24,16},{1,9},{9,1},{17,25},{25,17},{2,10},{10... | collective-permute-start | bytes 344072 | tf_op jit(solution)/shard_map/ppermute | solution.py:501
  44.0 10.3 %all-to-all-start = ((f32[32,8,128]{2,1,0:T(8,128)}), f32[32,8,128]{2,1,0:T(8,128)S(1)}, u32[]{:S(2)}, u32[]{:S(2)}) async-start(f32[32,8,128]{2,1,0:T(8,128)} %get-tuple-element.70), calls=%async_computation | async-start | bytes 262144 | tf_op jit(solution)/shard_map/all_to_all | solution.py:562
  47.4 1.4 %collective-permute-start.16 = (f32[4,56,128]{2,1,0:T(8,128)S(1)}, f32[4,56,128]{2,1,0:T(8,128)S(1)}, u32[]{:S(2)}, u32[]{:S(2)}) collective-permute-start(f32[4,56,128]{2,1,0:T(8,128)S(1)} %get-tuple-element.73), channel_id=1, source_target_pairs={{0,8},{8,0},{16,24},{24,16},{1,9},{9,1},{17,25},{25,17},{2,10},{10... | collective-permute-start | bytes 344072 | tf_op jit(solution)/shard_map/ppermute | solution.py:501
  47.5 1.5 %collective-permute-start.17 = (f32[4,56,128]{2,1,0:T(8,128)S(1)}, f32[4,56,128]{2,1,0:T(8,128)S(1)}, u32[]{:S(2)}, u32[]{:S(2)}) collective-permute-start(f32[4,56,128]{2,1,0:T(8,128)S(1)} %get-tuple-element.72), channel_id=1, source_target_pairs={{0,8},{8,0},{16,24},{24,16},{1,9},{9,1},{17,25},{25,17},{2,10},{10... | collective-permute-start | bytes 344072 | tf_op jit(solution)/shard_map/ppermute | solution.py:501

commit v3 on v2

--- a/solution.py
+++ b/solution.py
@@ -20,7 +20,9 @@
 LAMBDA = 0.05
 
 PAIRS = ((0, 0), (0, 1), (0, 2), (1, 1), (1, 2), (2, 2))
-HROWS = 56
+HROWS = 40
+SPLIT = 24
+KINDS = (3, 0, 1, 2)
 LIMIT = 32 * 1024 * 1024
 
 F32 = jnp.float32
@@ -45,12 +47,47 @@
 def along_y(weight, groups):
     shape = (NY, 128)
     row, lane = rows_of(shape), lanes(shape)
-    inside = (row // EDGE == lax.rem(lane, NEL)) & (lane // NEL < groups)
-    return jnp.where(inside, weight(lane // NEL, lax.rem(row, EDGE)) * (1.0 / VOL), 0.0)
-
-
-def exact_dot(a, b):
-    return jnp.dot(a, b, precision=lax.Precision.HIGHEST, preferred_element_type=F32)
+    group = lane // NEL
+    inside = (row // EDGE == lax.rem(lane, NEL)) & (group >= groups[0]) & (group <= groups[-1])
+    return jnp.where(inside, weight(group, lax.rem(row, EDGE)) * (1.0 / VOL), 0.0)
+
+
+def three_parts(value):
+    high = value.astype(BF16)
+    rest = value - high.astype(F32)
+    middle = rest.astype(BF16)
+    return [high, middle, (rest - middle.astype(F32)).astype(BF16)]
+
+
+def weighed(value, weights):
+    high = weights.astype(BF16)
+    both = jnp.concatenate([high, (weights - high.astype(F32)).astype(BF16)], axis=1)
+    found = jnp.dot(
+        jnp.concatenate(three_parts(value), axis=1),
+        jnp.concatenate([both] * 3, axis=0),
+        preferred_element_type=F32,
+    )
+    return found[:, :128] + found[:, 128:]
+
+
+def weighed_once(value, weights):
+    weights = weights.astype(BF16)
+    return jnp.dot(
+        jnp.concatenate(three_parts(value), axis=1),
+        jnp.concatenate([weights] * 3, axis=0),
+        preferred_element_type=F32,
+    )
+
+
+def layered(found, slab, slabs, weights):
+    total = None
+    for ez in range(EZ):
+        start = (ez * slabs + slab) * EDGE
+        part = found[start : start + EDGE] * weights
+        part = part[:8] + part[8:]
+        part = pltpu.roll(part, ez * EYD, 1) if ez else part
+        total = part if total is None else total + part
+    return jnp.sum(total, axis=0, keepdims=True)
 
 
 def lanes(shape):
@@ -76,7 +113,7 @@
     gx_even, gy_even, half_even = even(gx), even(gy), even(gy // 2)
     row, lane = rows_of((8, 128)), lanes((8, 128))
 
-    def visit(e, asked):
+    def visit(e, found):
         offset = route[e] - SPAN
         moved = jnp.clip(gx + xshift[e] - 1, 0, gx_count - 1) - gx
         ahead = jnp.where(gx_even, 1, 2)
@@ -87,10 +124,13 @@
         j = jnp.where(offset == 0, 4, jnp.where(jnp.abs(offset) == 1, near, far))
         slot = count[j]
         count[j] = slot + 1
-        place[e] = j * 8 + slot
-        return jnp.where((row == j) & (lane == slot), code.astype(F32), asked)
-
-    asked = lax.fori_loop(0, NEL, visit, jnp.zeros((8, 128), F32), unroll=True)
+        asked, places = found
+        asked = jnp.where((row == j) & (lane == slot), code.astype(F32), asked)
+        return asked, jnp.where(lane == e, j * 8 + slot, places)
+
+    zero = jnp.zeros((8, 128), jnp.int32)
+    asked, places = lax.fori_loop(0, NEL, visit, (zero.astype(F32), zero), unroll=True)
+    place[...] = places
     own[...] = asked
     m2[...] = asked
     m3[...] = asked
@@ -122,10 +162,10 @@
             jax.ShapeDtypeStruct((8, 128), F32),
             jax.ShapeDtypeStruct((NZ + 2 * EZ, EDGE, NY), BF16),
             jax.ShapeDtypeStruct((8, 128), F32),
-            jax.ShapeDtypeStruct((NEL,), jnp.int32),
+            jax.ShapeDtypeStruct((8, 128), jnp.int32),
         ),
         in_specs=[smem] * 3 + [vmem] * 2,
-        out_specs=(vmem,) * 6 + (smem,),
+        out_specs=(vmem,) * 7,
         scratch_shapes=[pltpu.SMEM((8,), jnp.int32)],
         cost_estimate=takes(2.0),
         name="ask",
@@ -145,11 +185,16 @@
 def serve_kernel(lines, *refs):
     count = len(lines)
     asked, outs = refs[3 : 3 + count], refs[3 + count : 3 + 2 * count]
-    banks, tables = refs[3 + 2 * count :]
+    banks, tables, last, sem = refs[3 + 2 * count :]
+    copy = pltpu.make_async_copy(asked[-1], last, sem)
+    copy.start()
+    asked = (*asked[:-1], last)
     for i in range(3):
         banks[i] = refs[i][0:NZ]
     for j in range(count):
         slabs, columns = [], []
+        if j == count - 1:
+            copy.wait()
         for slot in range(8):
             code = asked[j][lines[j], slot].astype(jnp.int32)
             slab = banks[code // NEL, pl.ds(lax.rem(code, NEL) // EYD * EDGE, EDGE)]
@@ -166,11 +211,13 @@
     return pl.pallas_call(
         functools.partial(serve_kernel, lines),
         out_shape=(jax.ShapeDtypeStruct((EDGE, EDGE, NY), BF16),) * count,
-        in_specs=[vmem] * 3 + [smem] * count,
+        in_specs=[vmem] * 3 + [smem] * (count - 1) + [vmem],
         out_specs=(vmem,) * count,
         scratch_shapes=[
             pltpu.VMEM((3, NZ, EDGE, NY), BF16),
             pltpu.VMEM((count, 8 * NY, NY), BF16),
+            pltpu.SMEM((8, 128), F32),
+            pltpu.SemaphoreType.DMA,
         ],
         compiler_params=pltpu.CompilerParams(vmem_limit_bytes=LIMIT),
         cost_estimate=takes(1.0 + 0.2 * count),
@@ -178,7 +225,7 @@
     )(own, d0, d1, *asked)
 
 
-def moments_kernel(gy_count, ref, a0, a1, r0, r1, frac, grad, packed, portions, side, slabs):
+def moments_kernel(gy_count, r1, r0, a1, a0, ref, frac, grad, packed, extra, portions, side, slabs):
     gx, gy = lax.axis_index("gx"), lax.axis_index("gy")
     gx_even, gy_even = even(gx), even(gy)
     side[...] = jnp.zeros((8, NZ * EDGE), F32)
@@ -199,11 +246,6 @@
     )
     before = jnp.where(gx_even, high1, high0)
     after = jnp.where(gx_even, low0, low1)
-    shape = (HROWS, 18 * EDGE)
-    row_a, lane_a = rows_of(shape), lanes(shape)
-    across = jnp.where(row_a // 3 == lane_a // EDGE, hat_product(lax.rem(row_a, 3), lax.rem(lane_a, EDGE)), 0.0)
-    along = along_y(hat_product, 3)
-    total = jnp.zeros((HROWS, 128), F32)
     lane2, row2 = lanes((EDGE, NY)), rows_of((EDGE, NY))
     for ez in range(EZ):
         collected = [[jnp.zeros((EDGE, NY), F32) for _ in range(3)] for _ in PAIRS]
@@ -227,10 +269,28 @@
                     collected[p][w] = collected[p][w] + float(PRODUCTS[w, k]) * product
         for p in range(len(PAIRS)):
             for w in range(3):
-                slabs[(p * 3 + w) * EDGE : (p * 3 + w + 1) * EDGE, :] = collected[p][w]
-        found = exact_dot(exact_dot(across, slabs[...]), along)
-        total = total + (pltpu.roll(found, ez * EYD, 1) if ez else found)
-    packed[...] = pltpu.roll(total, lax.rem(gx, 4) * NEL, 1)
+                start = (ez * 18 + p * 3 + w) * EDGE
+                slabs[start : start + EDGE, :] = collected[p][w]
+    found = weighed(slabs[...], along_y(hat_product, (0, 1, 2)))
+    across = [hat_product(w, row2) for w in range(3)]
+    row8, group8 = rows_of((8, 128)), lanes((8, 128)) // NEL
+    tiles = [jnp.zeros((8, 128), F32) for _ in range(HROWS // 8 + 1)]
+    for slab in range(18):
+        for w in range(3):
+            line = layered(found, slab, 18, across[w])
+            source = slab * 3 + w
+            if source < HROWS:
+                tiles[source // 8] = jnp.where((row8 == source % 8) & (group8 < 3), line, tiles[source // 8])
+            else:
+                for wy in range(3):
+                    spare = wy * 14 + source - HROWS
+                    turned = pltpu.roll(line, (3 - wy) * NEL, 1)
+                    tiles[spare // 8] = jnp.where((row8 == spare % 8) & (group8 == 3), turned, tiles[spare // 8])
+    total = jnp.concatenate(tiles, axis=0)
+    total = pltpu.roll(total, lax.rem(gx, 4) * NEL, 1)
+    packed[...] = total[:HROWS]
+    line = pltpu.roll(total[HROWS:], NEL, 1)[0:1] + pltpu.roll(total[HROWS:], 2 * NEL, 1)[1:2]
+    extra[...] = jnp.where(row == 6, line, 0.0)
     element, lane_e = rows_of((EYD, 128)), lanes((EYD, 128))
     unfold = (lane_e // EDGE == element).astype(F32).astype(BF16)
     for ez in range(EZ):
@@ -246,34 +306,31 @@
         out_shape=(
             jax.ShapeDtypeStruct((3, NZ, EDGE, NY), BF16),
             jax.ShapeDtypeStruct((HROWS, 128), F32),
+            jax.ShapeDtypeStruct((8, 128), F32),
             jax.ShapeDtypeStruct((EZ, 8, 128), F32),
         ),
         in_specs=[vmem] * 6,
-        out_specs=(vmem,) * 3,
-        scratch_shapes=[pltpu.VMEM((8, NZ * EDGE), F32), pltpu.VMEM((18 * EDGE, NY), F32)],
+        out_specs=(vmem,) * 4,
+        scratch_shapes=[pltpu.VMEM((8, NZ * EDGE), F32), pltpu.VMEM((EZ * 18 * EDGE, NY), F32)],
         compiler_params=pltpu.CompilerParams(vmem_limit_bytes=LIMIT),
         cost_estimate=takes(2.2),
         name="moments",
-    )(ref, *faces_x, *faces_y, fractions)
-
-
-def warp_kernel(place, b0, b1, b2, b3, b4, ref, grad, portions, mismatch, packed, bricks, tables, slabs):
+    )(faces_y[1], faces_y[0], faces_x[1], faces_x[0], ref, fractions)
+
+
+def warp_kernel(b0, b1, b2, b3, b4, place, ref, grad, portions, extra, mismatch, packed, bricks, tables, slabs, spots, sem):
     gx = lax.axis_index("gx")
-    for i, source in enumerate((b0, b1, b2, b3, b4)):
+    copy = pltpu.make_async_copy(place, spots, sem)
+    copy.start()
+    for i, source in zip((*KINDS, 4), (b0, b1, b2, b3, b4)):
         bricks[i] = source[...]
+    copy.wait()
     flat = (EDGE * EDGE, NY)
     lane = lanes(flat)
     at_x_rim = lax.rem(lax.broadcasted_iota(jnp.int32, flat, 0), EDGE) == EDGE - 1
     at_y_rim = lax.rem(lane, EDGE) == EDGE - 1
-    shape = (16, 6 * EDGE)
-    row_a, lane_a = rows_of(shape), lanes(shape)
-    across = jnp.where(lax.rem(row_a, 8) == lane_a // EDGE, hat_weight(row_a // 8, lax.rem(lane_a, EDGE)), 0.0)
-    along = along_y(hat_weight, 2)
-    along = jnp.concatenate([along, pltpu.roll(along, 2 * NEL, 1)], axis=0)
-    total = jnp.zeros((8, 128), F32)
     for ez in range(EZ):
-
-        codes = [place[ez * EYD + b] for b in range(EYD)]
+        codes = [spots[0, ez * EYD + b] for b in range(EYD)]
         found = [bricks[code // 8].reshape(flat) for code in codes]
         blended = gather_columns(tables.at[ez], found, [lax.rem(code, 8) for code in codes], range(EYD))
         portion = portions[ez]
@@ -296,31 +353,36 @@
                     collected[c][a] = collected[c][a] + float(HAT[a, k]) * term
         for c in range(3):
             for a in range(2):
-                slabs[(c * 2 + a) * EDGE : (c * 2 + a + 1) * EDGE, :] = collected[c][a]
-        summed = exact_dot(across, slabs[...])
-        found = exact_dot(jnp.concatenate([summed[:8], summed[8:]], axis=1), along)
-        total = total + (pltpu.roll(found, ez * EYD, 1) if ez else found)
-    packed[...] = jnp.broadcast_to(pltpu.roll(total, lax.rem(gx, 4) * NEL, 1), packed.shape)
-
-
-def warp(place, bricks, ref, grad, portions):
-    smem = pl.BlockSpec(memory_space=pltpu.SMEM)
+                start = (ez * 6 + c * 2 + a) * EDGE
+                slabs[start : start + EDGE, :] = collected[c][a]
+    found = weighed_once(slabs[...], along_y(lambda group, at: hat_weight(lax.rem(group, 2), at), (0, 1, 2, 3)))
+    across = hat_weight(lanes((EDGE, 128)) // (2 * NEL), rows_of((EDGE, 128)))
+    row8 = rows_of((8, 128))
+    total = jnp.zeros((8, 128), F32)
+    for slab in range(6):
+        total = jnp.where(row8 == slab, layered(found, slab, 6, across), total)
+    packed[...] = jnp.broadcast_to(pltpu.roll(total, lax.rem(gx, 4) * NEL, 1) + extra[...], packed.shape)
+
+
+def warp(place, bricks, ref, grad, portions, extra):
     vmem = pl.BlockSpec(memory_space=pltpu.VMEM)
     devices = lax.axis_size("gx") * lax.axis_size("gy")
     return pl.pallas_call(
         warp_kernel,
         out_shape=(jax.ShapeDtypeStruct((NZ, EDGE, NY), F32), jax.ShapeDtypeStruct((devices, 8, 128), F32)),
-        in_specs=[smem] + [vmem] * 8,
+        in_specs=[vmem] * 10,
         out_specs=(vmem, vmem),
         scratch_shapes=[
             pltpu.VMEM((5, EDGE, EDGE, NY), BF16),
             pltpu.VMEM((EZ, EYD * NY, NY), BF16),
-            pltpu.VMEM((6 * EDGE, NY), F32),
+            pltpu.VMEM((EZ * 6 * EDGE, NY), F32),
+            pltpu.SMEM((8, 128), jnp.int32),
+            pltpu.SemaphoreType.DMA,
         ],
         compiler_params=pltpu.CompilerParams(vmem_limit_bytes=LIMIT),
         cost_estimate=takes(4.0),
         name="warp",
-    )(place, *bricks, ref, grad, portions)
+    )(*bricks, place, ref, grad, portions, extra)
 
 
 def spread_groups(block_of, groups, gx_count, store):
@@ -336,18 +398,20 @@
             store(group, tile, pltpu.roll(merged, (128 - NEL * group) % 128, 1) if group else merged)
 
 
-def solve_kernel(gx_count, gy_count, hess, load, out, coef, rhs):
+def solve_kernel(gx_count, gy_count, first, second, load, out, coef, rhs):
     gx, gy = lax.axis_index("gx"), lax.axis_index("gy")
-    steps = gather_steps(gx_count, gy_count)
+    orders = gather_orders(gx_count, gy_count)
     tiles = -(-gx_count // 4)
     width = 128 * tiles
 
     def unpack(row, _):
         def hess_block(column):
-            return hess[block_index(steps, dict(gx=jnp.bitwise_xor(gx, column), gy=jnp.bitwise_xor(gy, row)))]
+            relative = dict(gx=jnp.bitwise_xor(gx, column), gy=jnp.bitwise_xor(gy, row))
+            parts = [half[block_index(order, relative)] for half, order in zip((first, second), orders)]
+            return jnp.concatenate(parts, axis=0)
 
         def store_hess(group, tile, value):
-            coef[tile, pl.ds(row * 3 * HROWS + group * HROWS, HROWS), :] = value
+            coef[tile, pl.ds(row * 4 * HROWS + group * HROWS, HROWS), :] = value
 
         def load_block(column):
             return load[column * gy_count + row]
@@ -355,7 +419,7 @@
         def store_load(group, tile, value):
             rhs[tile, pl.ds(row * 32 + group * 8, 8), :] = value
 
-        spread_groups(hess_block, 3, gx_count, store_hess)
+        spread_groups(hess_block, 4, gx_count, store_hess)
         spread_groups(load_block, 4, gx_count, store_load)
         return 0
 
@@ -406,7 +470,13 @@
         return found[0] if tiles == 1 else jnp.concatenate(found, axis=1)
 
     def channel(p, wz, wx, wy):
-        return strided(coef, wy * HROWS + (p * 3 + wz) * 3 + wx, 3 * HROWS)
+        source = (p * 3 + wz) * 3 + wx
+        if source < HROWS:
+            return strided(coef, wy * HROWS + source, 4 * HROWS)
+        spare = wy * 14 + source - HROWS
+        if spare < HROWS:
+            return strided(coef, 3 * HROWS + spare, 4 * HROWS)
+        return strided(rhs, (spare - HROWS) * 8 + 6, 32)
 
     pair_of = {}
     for p, (c, d) in enumerate(PAIRS):
@@ -435,11 +505,14 @@
         for c in range(3):
             main, top = settle(sums[c])
             result.append((main + LAMBDA * vector[c][0], top + LAMBDA * vector[c][1]))
-        return result
+        bent = sum(known[c][n] * sums[c][n] for c in range(3) for n in range(8))
+        return result, total(bent) + LAMBDA * inner(vector, vector)
+
+    def total(value):
+        return jnp.sum(jnp.sum(value, axis=0, keepdims=True), axis=1, keepdims=True)
 
     def inner(one, two):
-        summed = sum(a[0] * b[0] + a[1] * b[1] for a, b in zip(one, two))
-        return jnp.sum(jnp.sum(summed, axis=1, keepdims=True), axis=0, keepdims=True)
+        return total(sum(a[0] * b[0] + a[1] * b[1] for a, b in zip(one, two)))
 
     def combine(one, factor, two):
         return [(a[0] + factor * b[0], a[1] + factor * b[1]) for a, b in zip(one, two)]
@@ -452,8 +525,8 @@
     increment = None
     norm_now = inner(residual, residual)
     for iteration in range(ITERS):
-        curved = curved_by(direction)
-        step = norm_now / inner(direction, curved)
+        curved, bent = curved_by(direction)
+        step = norm_now / bent
         if increment is None:
             increment = [(step * a, step * b) for a, b in direction]
         else:
@@ -476,23 +549,23 @@
                 out[c, level] = short[0:1, start : start + EYD]
 
 
-def solve(hess, load):
+def solve(first, second, load):
     gx_count, gy_count = lax.axis_size("gx"), lax.axis_size("gy")
     tiles = -(-gx_count // 4)
     vmem = pl.BlockSpec(memory_space=pltpu.VMEM)
     return pl.pallas_call(
         functools.partial(solve_kernel, gx_count, gy_count),
         out_shape=jax.ShapeDtypeStruct((3, EZ + 1, 1, EYD), F32),
-        in_specs=[vmem, vmem],
+        in_specs=[vmem] * 3,
         out_specs=vmem,
         scratch_shapes=[
-            pltpu.VMEM((tiles, gy_count * 3 * HROWS, 128), F32),
+            pltpu.VMEM((tiles, gy_count * 4 * HROWS, 128), F32),
             pltpu.VMEM((tiles, gy_count * 32, 128), F32),
         ],
         compiler_params=pltpu.CompilerParams(vmem_limit_bytes=LIMIT),
         cost_estimate=takes(3.5),
         name="solve",
-    )(hess, load)
+    )(first, second, load)
 
 
 def swap(array, axis, partner):
@@ -519,13 +592,13 @@
 
 
 def gather_steps(gx_count, gy_count):
-    steps = []
-    for axis, size in (("gy", gy_count), ("gx", gx_count)):
-        bit = size // 2
-        while bit:
-            steps.append((axis, bit))
-            bit //= 2
-    return steps
+    far = [("gy", 1 << k) for k in range(1, gy_count.bit_length() - 1)]
+    return [*far, ("gy", 1), *[("gx", 1 << k) for k in reversed(range(gx_count.bit_length() - 1))]]
+
+
+def gather_orders(gx_count, gy_count):
+    steps = gather_steps(gx_count, gy_count)
+    return steps, [*steps[:-3], steps[-2], steps[-3], steps[-1]]
 
 
 def block_index(steps, relative):
@@ -535,36 +608,37 @@
     return found
 
 
+def doubled(known, step, pieces=1):
+    axis, bit = step
+    size = known.shape[0] // pieces
+    sent = [swap(known[i * size : (i + 1) * size], axis, lambda j: j ^ bit) for i in range(pieces)]
+    return jnp.concatenate([known, *sent], axis=0)
+
+
 def body(reference_image, deformed_image, route, within, xshift, fractions):
     m0, m1, m2, m3, thick, own, place = ask(
         route.reshape(NEL), within.reshape(NEL), xshift.reshape(NEL), reference_image, deformed_image
     )
-    q = [swap_y(m, kind) for kind, m in enumerate((m0, m1, m2, m3))]
-    d0, d1 = swap_x(thick, 0), swap_x(thick, 1)
-    *q, d0, d1 = lax.optimization_barrier((*q, d0, d1))
-    image, _ = lax.optimization_barrier((reference_image, q))
-    grad, packed, portions = moments(image, (d0, d1), (q[0], q[1]), fractions.reshape(NEL, 3))
-    q[2], packed = lax.optimization_barrier((q[2], packed))
-    served = serve(deformed_image, d0, d1, q, (8, 9, 2, 3))
-    own, _ = lax.optimization_barrier((own, served))
-    (at_home,) = serve(deformed_image, d0, d1, [own], (4,))
-    known = packed[None]
-    bricks = [swap_y(block, kind) for kind, block in enumerate(served)] + [at_home]
-    steps = gather_steps(lax.axis_size("gx"), lax.axis_size("gy"))
-    for k, (axis, bit) in enumerate(steps):
-        if k == 1:
-            known, _ = lax.optimization_barrier((known, at_home))
-        if k == len(steps) - 3:
-            bricks, known = lax.optimization_barrier((bricks, known))
-            mismatch, part = warp(place, bricks, reference_image, grad, portions)
-        if k == len(steps) - 2:
-            known, part = lax.optimization_barrier((known, part))
-            load = lax.all_to_all(part, ("gx", "gy"), 0, 0)
-        pieces = 4 if k + 1 == len(steps) else 1
-        size = known.shape[0] // pieces
-        sent = [swap(known[i * size : (i + 1) * size], axis, lambda i, bit=bit: i ^ bit) for i in range(pieces)]
-        known = jnp.concatenate([known, *sent], axis=0)
-    return solve(known, load), mismatch
+    asks = (m0, m1, m2, m3)
+    q = {kind: swap_y(asks[kind], kind) for kind in KINDS}
+    d1, d0 = swap_x(thick, 1), swap_x(thick, 0)
+    grad, packed, extra, portions = moments(reference_image, (d0, d1), (q[0], q[1]), fractions.reshape(NEL, 3))
+    *served, at_home = serve(deformed_image, d0, d1, [q[kind] for kind in KINDS] + [own], [8 * (k < 2) + k for k in KINDS] + [4])
+    known, at_home = lax.optimization_barrier((packed[None], at_home))
+    bricks = [swap_y(block, kind) for kind, block in zip(KINDS, served)] + [at_home]
+    orders = gather_orders(lax.axis_size("gx"), lax.axis_size("gy"))
+    steps = orders[0]
+    for step in steps[:-4]:
+        known = doubled(known, step)
+    bricks, known = lax.optimization_barrier((bricks, known))
+    mismatch, part = warp(place, bricks, reference_image, grad, portions, extra)
+    known = doubled(known, steps[-4])
+    known, part = lax.optimization_barrier((known, part))
+    load = lax.all_to_all(part, ("gx", "gy"), 0, 0)
+    halves = [known[:, :SPLIT], known[:, SPLIT:]]
+    for k in (-3, -2, -1):
+        halves = [doubled(half, order[k], 2 if k == -1 else 1) for half, order in zip(halves, orders)]
+    return solve(*halves, load), mismatch
 
 
 def solution(mesh):

time: 58.1 us -> 53.9 us (0.928)
  Pallas kernels: 15 us -> 13.1 us
  local copies, waits for them, and re-layouts: 1.47 us -> 0.18 us
  starting transfers between devices: 24.4 us -> 23.5 us
    all_to_all x1, waiting for transfers between devices: 5.32 us -> 0.01 us  [body(): load = lax.all_to_all(part, ('gx', 'gy'), 0, 0)]
    ppermute x18 -> x20, waiting for transfers between devices: 10.9 us -> 16 us  [swap(): lax.ppermute(array, axis, [(i, j) for i, j in pairs if 0 <= j < size])]
    pallas_call x1, Pallas kernels: 4.04 us -> 2.73 us  [warp(): pl.pallas_call(warp_kernel, out_shape=(jax.ShapeDtypeStruct((NZ, EDGE, NY...]
    unnamed x17 -> x18, local copies, waits for them, and re-layouts: 1.34 us -> 0.06 us
    ppermute x18 -> x20, starting transfers between devices: 21.8 us -> 20.9 us  [swap(): lax.ppermute(array, axis, [(i, j) for i, j in pairs if 0 <= j < size])]
    pallas_call x2 -> x1, Pallas kernels: 2.77 us -> 2.61 us  [serve(): pl.pallas_call(functools.partial(serve_kernel, lines), out_shape=(jax.Sha...]
  transfers between devices with their start and end apart: 19 -> 21, of which waited for: 8 -> 9; matrix products, arithmetic and copies ran while one was open for 0% -> 0% of each run, Pallas kernels for 12% -> 9%
where the time goes in v3:
time: 53.9 us; the launch traced here: 53.7 us
  starting transfers between devices  23.5 us (44%)
  waiting for transfers between devices  16 us (30%)
  Pallas kernels  13.1 us (24%)
  between operations  0.84 us (2%)
    ppermute x20, starting transfers between devices, swap(): lax.ppermute(array, axis, [(i, j) for i, j in pairs if 0 <= j < size])  20.9 us
    ppermute x20, waiting for transfers between devices, swap(): lax.ppermute(array, axis, [(i, j) for i, j in pairs if 0 <= j < size])  16 us
    pallas_call x1, Pallas kernels, solve(): pl.pallas_call(functools.partial(solve_kernel, gx_count, gy_count), out_s...  3.49 us
    pallas_call x1, Pallas kernels, warp(): pl.pallas_call(warp_kernel, out_shape=(jax.ShapeDtypeStruct((NZ, EDGE, NY...  2.73 us
    pallas_call x1, Pallas kernels, serve(): pl.pallas_call(functools.partial(serve_kernel, lines), out_shape=(jax.Sha...  2.61 us
    all_to_all x1, starting transfers between devices, body(): load = lax.all_to_all(part, ('gx', 'gy'), 0, 0)  2.58 us
    pallas_call x1, Pallas kernels, ask(): pl.pallas_call(functools.partial(ask_kernel, lax.axis_size('gx')), out_sh...  2.35 us
    pallas_call x1, Pallas kernels, moments(): pl.pallas_call(functools.partial(moments_kernel, lax.axis_size('gy')), ou...  1.94 us
  transfers between devices with their start and end apart: 21, of which 9 were waited for; matrix products, arithmetic and copies ran while one was open for 0% of the time, Pallas kernels for 9%

profile of v3, /device:TPU:0, one launch (start us, length us, event | category | flops | bytes accessed | tf_op | source)
XLA Modules:
  0.0 53.7 jit_solution(15372510810397839685)
XLA Ops:
  0.6 2.3 %ask.1 = (f32[16,128]{1,0:T(8,128)}, f32[16,128]{1,0:T(8,128)}, f32[8,128]{1,0:T(8,128)}, f32[8,128]{1,0:T(8,128)}, bf16[72,16,128]{2,1,0:T(8,128)(2,1)}, /*index=5*/f32[8,128]{1,0:T(8,128)}, s32[8,128]{1,0:T(8,128)}) custom-call(s32[32]{0:T(128)} %bitcast.8, s32[32]{0:T(128)} %bitcast.9, s32[32]{0:T(128)} %bitcast.10, bf16[64,16,128]{2,1,0:T(8,128)(2,1)} %ref.5, ...), custom_call_target="tpu_custom_call" | custom-call | bytes 7380000 | tf_op jit(solution)/shard_map/ask/pallas_call | solution.py:156
  3.0 0.5 collective-permute-start
  3.4 0.7 %collective-permute-start.1 = (bf16[72,16,128]{2,1,0:T(8,128)(2,1)}, bf16[72,16,128]{2,1,0:T(8,128)(2,1)S(1)}, u32[]{:S(2)}, u32[]{:S(2)}) collective-permute-start(bf16[72,16,128]{2,1,0:T(8,128)(2,1)} %get-tuple-element.30), channel_id=1, source_target_pairs={{8,16},{16,8},{9,17},{17,9},{10,18},{18,10},{11,19},{19,11},{12,20... | collective-permute-start | bytes 884744 | tf_op jit(solution)/shard_map/ppermute | solution.py:574
  4.1 2.6 %collective-permute-start.3 = (f32[16,128]{1,0:T(8,128)}, f32[16,128]{1,0:T(8,128)S(1)}, u32[]{:S(2)}, u32[]{:S(2)}) collective-permute-start(f32[16,128]{1,0:T(8,128)} %get-tuple-element.32), channel_id=1, source_target_pairs={{0,1},{1,0},{2,3},{3,2},{4,5},{5,4},{6,7},{7,6},{8,9},{9,8},{10,11... | collective-permute-start | bytes 24584 | tf_op jit(solution)/shard_map/ppermute | solution.py:574
  6.7 3.6 %collective-permute-start.4 = (f32[16,128]{1,0:T(8,128)}, f32[16,128]{1,0:T(8,128)S(1)}, u32[]{:S(2)}, u32[]{:S(2)}) collective-permute-start(f32[16,128]{1,0:T(8,128)} %get-tuple-element.33), channel_id=1, source_target_pairs={{0,7},{1,2},{2,1},{3,4},{4,3},{5,6},{6,5},{7,0},{8,15},{9,10},{10,... | collective-permute-start | bytes 24584 | tf_op jit(solution)/shard_map/ppermute | solution.py:574
  10.3 0.4 collective-permute-start.2
  10.7 0.1 copy.9
  10.8 2.4 %collective-permute-done.4.refs_5_.r1 = f32[16,128]{1,0:T(8,128)S(1)} collective-permute-done((f32[16,128]{1,0:T(8,128)}, f32[16,128]{1,0:T(8,128)S(1)}, u32[]{:S(2)}, u32[]{:S(2)}) %collective-permute-start.4) | collective-permute-done | bytes 8224 | tf_op jit(solution)/shard_map/ppermute | solution.py:574
  13.3 0.0 copy-start.1
  13.3 1.9 %moments.1 = (bf16[3,64,16,128]{3,2,1,0:T(8,128)(2,1)S(1)}, f32[40,128]{1,0:T(8,128)S(1)}, f32[8,128]{1,0:T(8,128)S(1)}, f32[4,8,128]{2,1,0:T(8,128)S(1)}) custom-call(f32[16,128]{1,0:T(8,128)S(1)} %collective-permute-done.4.refs_5_.r1, f32[16,128]{1,0:T(8,128)S(1)} %collective-permute-done.3.refs_4_.r0, ...), custom_call_target="tpu_custom_call" | custom-call | bytes 8118000 | tf_op jit(solution)/shard_map/moments/pallas_call | solution.py:304
  15.2 0.7 %collective-permute-done.2.refs_3_ = f32[8,128]{1,0:T(8,128)S(1)} collective-permute-done((f32[8,128]{1,0:T(8,128)}, f32[8,128]{1,0:T(8,128)S(1)}, u32[]{:S(2)}, u32[]{:S(2)}) %collective-permute-start.2) | collective-permute-done | bytes 4128 | tf_op jit(solution)/shard_map/ppermute | solution.py:574
  15.9 2.6 %serve.1 = (bf16[16,16,128]{2,1,0:T(8,128)(2,1)S(1)}, bf16[16,16,128]{2,1,0:T(8,128)(2,1)S(1)}, bf16[16,16,128]{2,1,0:T(8,128)(2,1)S(1)}, bf16[16,16,128]{2,1,0:T(8,128)(2,1)S(1)}, bf16[16,16,128]{2,1,0:T(8,128)(2,1)S(1)}) custom-call(bf16[64,16,128]{2,1,0:T(8,128)(2,1)S(1)} %copy-done.1, bf16[72,16,128]{2,1,0:T(8,128)(2,1)S(1)} %collective-permute-done.refs_1_.a0, ...), custom_call_target="tpu_custom_call" | custom-call | bytes 7380000 | tf_op jit(solution)/shard_map/serve/pallas_call | solution.py:211
  18.5 0.1 collective-permute-start.10
  18.6 2.3 %collective-permute-start.6 = (bf16[16,16,128]{2,1,0:T(8,128)(2,1)S(1)}, bf16[16,16,128]{2,1,0:T(8,128)(2,1)S(1)}, u32[]{:S(2)}, u32[]{:S(2)}) collective-permute-start(bf16[16,16,128]{2,1,0:T(8,128)(2,1)S(1)} %get-tuple-element.36), channel_id=1, source_target_pairs={{0,6},{1,7},{2,4},{3,5},{4,2},{5,3},{6,0},{7,1},{8,14},{9,15},{10,... | collective-permute-start | bytes 196616 | tf_op jit(solution)/shard_map/ppermute | solution.py:574
  20.9 1.2 %collective-permute-start.7 = (bf16[16,16,128]{2,1,0:T(8,128)(2,1)S(1)}, bf16[16,16,128]{2,1,0:T(8,128)(2,1)S(1)}, u32[]{:S(2)}, u32[]{:S(2)}) collective-permute-start(bf16[16,16,128]{2,1,0:T(8,128)(2,1)S(1)} %get-tuple-element.37), channel_id=1, source_target_pairs={{0,1},{1,0},{2,3},{3,2},{4,5},{5,4},{6,7},{7,6},{8,9},{9,8},{10,11... | collective-permute-start | bytes 196616 | tf_op jit(solution)/shard_map/ppermute | solution.py:574
  22.2 1.8 %collective-permute-start.8 = (bf16[16,16,128]{2,1,0:T(8,128)(2,1)S(1)}, bf16[16,16,128]{2,1,0:T(8,128)(2,1)S(1)}, u32[]{:S(2)}, u32[]{:S(2)}) collective-permute-start(bf16[16,16,128]{2,1,0:T(8,128)(2,1)S(1)} %get-tuple-element.38), channel_id=1, source_target_pairs={{0,7},{1,2},{2,1},{3,4},{4,3},{5,6},{6,5},{7,0},{8,15},{9,10},{10,... | collective-permute-start | bytes 196616 | tf_op jit(solution)/shard_map/ppermute | solution.py:574
  23.9 0.5 collective-permute-start.9
  24.4 0.9 %collective-permute-done.6.b0 = bf16[16,16,128]{2,1,0:T(8,128)(2,1)S(1)} collective-permute-done((bf16[16,16,128]{2,1,0:T(8,128)(2,1)S(1)}, bf16[16,16,128]{2,1,0:T(8,128)(2,1)S(1)}, u32[]{:S(2)}, u32[]{:S(2)}) %collective-permute-start.6) | collective-permute-done | bytes 65568 | tf_op jit(solution)/shard_map/ppermute | solution.py:574
  25.3 0.3 collective-permute-done.7.b1
  25.7 4.2 %collective-permute-done.8.b2 = bf16[16,16,128]{2,1,0:T(8,128)(2,1)S(1)} collective-permute-done((bf16[16,16,128]{2,1,0:T(8,128)(2,1)S(1)}, bf16[16,16,128]{2,1,0:T(8,128)(2,1)S(1)}, u32[]{:S(2)}, u32[]{:S(2)}) %collective-permute-start.8) | collective-permute-done | bytes 65568 | tf_op jit(solution)/shard_map/ppermute | solution.py:574
  29.8 2.7 %warp.1 = (f32[64,16,128]{2,1,0:T(8,128)}, f32[32,8,128]{2,1,0:T(8,128)}) custom-call(bf16[16,16,128]{2,1,0:T(8,128)(2,1)S(1)} %collective-permute-done.6.b0, bf16[16,16,128]{2,1,0:T(8,128)(2,1)S(1)} %collective-permute-done.7.b1, bf16[16,16,128]{2,1,0:T(8,128)(2,1)S(1)} %collective-permute-done.8.b2, bf16[16,16,128]{2,1,0:T(8,128)(2,1)S(1)} %collective-permute-done.9.b3, ...), custom_call_target="tpu_custom_call" | custom-call | bytes 14760000 | tf_op jit(solution)/shard_map/warp/pallas_call | solution.py:370
  32.6 2.2 %collective-permute-done.11 = f32[2,40,128]{2,1,0:T(8,128)S(1)} collective-permute-done((f32[2,40,128]{2,1,0:T(8,128)S(1)}, f32[2,40,128]{2,1,0:T(8,128)S(1)}, u32[]{:S(2)}, u32[]{:S(2)}) %collective-permute-start.11) | collective-permute-done | bytes 40992 | tf_op jit(solution)/shard_map/ppermute | solution.py:574
  34.8 2.8 %collective-permute-start.16 = (f32[4,16,128]{2,1,0:T(8,128)S(1)}, f32[4,16,128]{2,1,0:T(8,128)S(1)}, u32[]{:S(2)}, u32[]{:S(2)}) collective-permute-start(f32[4,16,128]{2,1,0:T(8,128)S(1)} %get-tuple-element.58), channel_id=1, source_target_pairs={{0,16},{8,24},{16,0},{24,8},{1,17},{9,25},{17,1},{25,9},{2,18},{10... | collective-permute-start | bytes 98312 | tf_op jit(solution)/shard_map/ppermute | solution.py:574
  37.6 0.9 %collective-permute-start.12 = (f32[4,24,128]{2,1,0:T(8,128)S(1)}, f32[4,24,128]{2,1,0:T(8,128)S(1)}, u32[]{:S(2)}, u32[]{:S(2)}) collective-permute-start(f32[4,24,128]{2,1,0:T(8,128)S(1)} %get-tuple-element.60), channel_id=1, source_target_pairs={{0,1},{1,0},{2,3},{3,2},{4,5},{5,4},{6,7},{7,6},{8,9},{9,8},{10,11... | collective-permute-start | bytes 147464 | tf_op jit(solution)/shard_map/ppermute | solution.py:574
  38.5 2.6 %all-to-all-start = ((f32[32,8,128]{2,1,0:T(8,128)}), f32[32,8,128]{2,1,0:T(8,128)S(1)}, u32[]{:S(2)}, u32[]{:S(2)}) async-start(f32[32,8,128]{2,1,0:T(8,128)} %get-tuple-element.56), calls=%async_computation | async-start | bytes 262144 | tf_op jit(solution)/shard_map/all_to_all | solution.py:637
  41.1 1.8 %collective-permute-start.17 = (f32[8,16,128]{2,1,0:T(8,128)S(1)}, f32[8,16,128]{2,1,0:T(8,128)S(1)}, u32[]{:S(2)}, u32[]{:S(2)}) collective-permute-start(f32[8,16,128]{2,1,0:T(8,128)S(1)} %pad_maximum_fusion.2), channel_id=1, source_target_pairs={{0,1},{1,0},{2,3},{3,2},{4,5},{5,4},{6,7},{7,6},{8,9},{9,8},{10,11... | collective-permute-start | bytes 196616 | tf_op jit(solution)/shard_map/ppermute | solution.py:574
  42.9 1.5 %collective-permute-start.13 = (f32[8,24,128]{2,1,0:T(8,128)S(1)}, f32[8,24,128]{2,1,0:T(8,128)S(1)}, u32[]{:S(2)}, u32[]{:S(2)}) collective-permute-start(f32[8,24,128]{2,1,0:T(8,128)S(1)} %pad_maximum_fusion), channel_id=1, source_target_pairs={{0,16},{8,24},{16,0},{24,8},{1,17},{9,25},{17,1},{25,9},{2,18},{10... | collective-permute-start | bytes 294920 | tf_op jit(solution)/shard_map/ppermute | solution.py:574
  44.5 0.2 collective-permute-start.14
  44.7 1.5 %collective-permute-done.17 = f32[8,16,128]{2,1,0:T(8,128)S(1)} collective-permute-done((f32[8,16,128]{2,1,0:T(8,128)S(1)}, f32[8,16,128]{2,1,0:T(8,128)S(1)}, u32[]{:S(2)}, u32[]{:S(2)}) %collective-permute-start.17) | collective-permute-done | bytes 65568 | tf_op jit(solution)/shard_map/ppermute | solution.py:574
  46.2 2.7 %collective-permute-done.13 = f32[8,24,128]{2,1,0:T(8,128)S(1)} collective-permute-done((f32[8,24,128]{2,1,0:T(8,128)S(1)}, f32[8,24,128]{2,1,0:T(8,128)S(1)}, u32[]{:S(2)}, u32[]{:S(2)}) %collective-permute-start.13) | collective-permute-done | bytes 98336 | tf_op jit(solution)/shard_map/ppermute | solution.py:574
  48.9 1.2 %collective-permute-done.15 = f32[8,24,128]{2,1,0:T(8,128)S(1)} collective-permute-done((f32[8,24,128]{2,1,0:T(8,128)S(1)}, f32[8,24,128]{2,1,0:T(8,128)S(1)}, u32[]{:S(2)}, u32[]{:S(2)}) %collective-permute-start.15) | collective-permute-done | bytes 98336 | tf_op jit(solution)/shard_map/ppermute | solution.py:574
  50.2 3.5 %solve.1 = f32[3,5,1,8]{3,2,1,0:T(1,128)} custom-call(f32[32,24,128]{2,1,0:T(8,128)S(1)} %constant_dynamic-update-slice_fusion.first, f32[32,16,128]{2,1,0:T(8,128)S(1)} %constant_dynamic-update-slice_fusion.5.second, f32[32,8,128]{2,1,0:T(8,128)S(1)} %all-to-all-done.load), custom_call_target="tpu_custom_call" | custom-call | bytes 12915000 | tf_op jit(solution)/shard_map/solve/pallas_call | solution.py:556
  (42 shorter events, 0.2 us)
Async XLA Ops:
  0.6 12.6 %copy-start = (bf16[64,16,128]{2,1,0:T(8,128)(2,1)S(1)}, bf16[64,16,128]{2,1,0:T(8,128)(2,1)}, u32[]{:S(2)}) copy-start(bf16[64,16,128]{2,1,0:T(8,128)(2,1)} %ref.5) | copy-start | bytes 786436
  3.0 7.7 %copy-start.5 = (f32[8,128]{1,0:T(8,128)S(1)}, f32[8,128]{1,0:T(8,128)}, u32[]{:S(2)}) copy-start(f32[8,128]{1,0:T(8,128)} %get-tuple-element.34) | copy-start | bytes 12292
  3.0 10.3 %collective-permute-start = (bf16[72,16,128]{2,1,0:T(8,128)(2,1)}, bf16[72,16,128]{2,1,0:T(8,128)(2,1)S(1)}, u32[]{:S(2)}, u32[]{:S(2)}) collective-permute-start(bf16[72,16,128]{2,1,0:T(8,128)(2,1)} %get-tuple-element.30), channel_id=1, source_target_pairs={{0,8},{8,0},{16,24},{24,16},{1,9},{9,1},{17,25},{25,17},{2,10},{10... | collective-permute-start | bytes 884744 | tf_op jit(solution)/shard_map/ppermute | solution.py:574
  3.4 9.8 %collective-permute-start.1 = (bf16[72,16,128]{2,1,0:T(8,128)(2,1)}, bf16[72,16,128]{2,1,0:T(8,128)(2,1)S(1)}, u32[]{:S(2)}, u32[]{:S(2)}) collective-permute-start(bf16[72,16,128]{2,1,0:T(8,128)(2,1)} %get-tuple-element.30), channel_id=1, source_target_pairs={{8,16},{16,8},{9,17},{17,9},{10,18},{18,10},{11,19},{19,11},{12,20... | collective-permute-start | bytes 884744 | tf_op jit(solution)/shard_map/ppermute | solution.py:574
  4.1 6.6 %collective-permute-start.3 = (f32[16,128]{1,0:T(8,128)}, f32[16,128]{1,0:T(8,128)S(1)}, u32[]{:S(2)}, u32[]{:S(2)}) collective-permute-start(f32[16,128]{1,0:T(8,128)} %get-tuple-element.32), channel_id=1, source_target_pairs={{0,1},{1,0},{2,3},{3,2},{4,5},{5,4},{6,7},{7,6},{8,9},{9,8},{10,11... | collective-permute-start | bytes 24584 | tf_op jit(solution)/shard_map/ppermute | solution.py:574
  6.7 4.0 %copy-start.4 = (s32[1,1,32,3]{2,1,3,0:T(1,128)S(1)}, s32[1,1,32,3]{2,1,3,0:T(1,128)}, u32[]{:S(2)}) copy-start(s32[1,1,32,3]{2,1,3,0:T(1,128)} %param.11) | copy-start | bytes 1156
  6.7 6.6 %collective-permute-start.4 = (f32[16,128]{1,0:T(8,128)}, f32[16,128]{1,0:T(8,128)S(1)}, u32[]{:S(2)}, u32[]{:S(2)}) collective-permute-start(f32[16,128]{1,0:T(8,128)} %get-tuple-element.33), channel_id=1, source_target_pairs={{0,7},{1,2},{2,1},{3,4},{4,3},{5,6},{6,5},{7,0},{8,15},{9,10},{10,... | collective-permute-start | bytes 24584 | tf_op jit(solution)/shard_map/ppermute | solution.py:574
  10.3 5.6 %collective-permute-start.2 = (f32[8,128]{1,0:T(8,128)}, f32[8,128]{1,0:T(8,128)S(1)}, u32[]{:S(2)}, u32[]{:S(2)}) collective-permute-start(f32[8,128]{1,0:T(8,128)} %get-tuple-element.31), channel_id=1, source_target_pairs={{0,6},{1,7},{2,4},{3,5},{4,2},{5,3},{6,0},{7,1},{8,14},{9,15},{10,... | collective-permute-start | bytes 12296 | tf_op jit(solution)/shard_map/ppermute | solution.py:574
  10.7 5.2 %collective-permute-start.5 = (f32[8,128]{1,0:T(8,128)S(1)}, f32[8,128]{1,0:T(8,128)S(1)}, u32[]{:S(2)}, u32[]{:S(2)}) collective-permute-start(f32[8,128]{1,0:T(8,128)S(1)} %copy-done.5), channel_id=1, source_target_pairs={{0,2},{1,3},{2,0},{3,1},{4,6},{5,7},{6,4},{7,5},{8,10},{9,11},{10,... | collective-permute-start | bytes 12296 | tf_op jit(solution)/shard_map/ppermute | solution.py:574
  13.3 2.6 %copy-start.1 = (bf16[64,16,128]{2,1,0:T(8,128)(2,1)S(1)}, bf16[64,16,128]{2,1,0:T(8,128)(2,1)}, u32[]{:S(2)}) copy-start(bf16[64,16,128]{2,1,0:T(8,128)(2,1)} %refs_0_.1) | copy-start | bytes 786436
  13.3 2.6 %copy-start.2 = (f32[8,128]{1,0:T(8,128)S(1)}, f32[8,128]{1,0:T(8,128)}, u32[]{:S(2)}) copy-start(f32[8,128]{1,0:T(8,128)} %get-tuple-element.35.refs_7_) | copy-start | bytes 12292
  18.5 5.9 %collective-permute-start.10 = (f32[1,40,128]{2,1,0:T(8,128)S(1)}, f32[1,40,128]{2,1,0:T(8,128)S(1)}, u32[]{:S(2)}, u32[]{:S(2)}) collective-permute-start(f32[1,40,128]{2,1,0:T(8,128)S(1)} %bitcast.6), channel_id=1, source_target_pairs={{0,2},{1,3},{2,0},{3,1},{4,6},{5,7},{6,4},{7,5},{8,10},{9,11},{10,... | collective-permute-start | bytes 61448 | tf_op jit(solution)/shard_map/ppermute | solution.py:574
  18.6 6.8 %collective-permute-start.6 = (bf16[16,16,128]{2,1,0:T(8,128)(2,1)S(1)}, bf16[16,16,128]{2,1,0:T(8,128)(2,1)S(1)}, u32[]{:S(2)}, u32[]{:S(2)}) collective-permute-start(bf16[16,16,128]{2,1,0:T(8,128)(2,1)S(1)} %get-tuple-element.36), channel_id=1, source_target_pairs={{0,6},{1,7},{2,4},{3,5},{4,2},{5,3},{6,0},{7,1},{8,14},{9,15},{10,... | collective-permute-start | bytes 196616 | tf_op jit(solution)/shard_map/ppermute | solution.py:574
  20.9 4.8 %collective-permute-start.7 = (bf16[16,16,128]{2,1,0:T(8,128)(2,1)S(1)}, bf16[16,16,128]{2,1,0:T(8,128)(2,1)S(1)}, u32[]{:S(2)}, u32[]{:S(2)}) collective-permute-start(bf16[16,16,128]{2,1,0:T(8,128)(2,1)S(1)} %get-tuple-element.37), channel_id=1, source_target_pairs={{0,1},{1,0},{2,3},{3,2},{4,5},{5,4},{6,7},{7,6},{8,9},{9,8},{10,11... | collective-permute-start | bytes 196616 | tf_op jit(solution)/shard_map/ppermute | solution.py:574
  22.2 7.7 %collective-permute-start.8 = (bf16[16,16,128]{2,1,0:T(8,128)(2,1)S(1)}, bf16[16,16,128]{2,1,0:T(8,128)(2,1)S(1)}, u32[]{:S(2)}, u32[]{:S(2)}) collective-permute-start(bf16[16,16,128]{2,1,0:T(8,128)(2,1)S(1)} %get-tuple-element.38), channel_id=1, source_target_pairs={{0,7},{1,2},{2,1},{3,4},{4,3},{5,6},{6,5},{7,0},{8,15},{9,10},{10,... | collective-permute-start | bytes 196616 | tf_op jit(solution)/shard_map/ppermute | solution.py:574
  23.9 5.9 %collective-permute-start.9 = (bf16[16,16,128]{2,1,0:T(8,128)(2,1)S(1)}, bf16[16,16,128]{2,1,0:T(8,128)(2,1)S(1)}, u32[]{:S(2)}, u32[]{:S(2)}) collective-permute-start(bf16[16,16,128]{2,1,0:T(8,128)(2,1)S(1)} %get-tuple-element.39), channel_id=1, source_target_pairs={{0,2},{1,3},{2,0},{3,1},{4,6},{5,7},{6,4},{7,5},{8,10},{9,11},{10,... | collective-permute-start | bytes 196616 | tf_op jit(solution)/shard_map/ppermute | solution.py:574
  24.4 5.4 %copy-start.3 = (s32[8,128]{1,0:T(8,128)S(1)}, s32[8,128]{1,0:T(8,128)}, u32[]{:S(2)}) copy-start(s32[8,128]{1,0:T(8,128)} %get-tuple-element.50.place) | copy-start | bytes 12292
  29.8 4.9 %collective-permute-start.11 = (f32[2,40,128]{2,1,0:T(8,128)S(1)}, f32[2,40,128]{2,1,0:T(8,128)S(1)}, u32[]{:S(2)}, u32[]{:S(2)}) collective-permute-start(f32[2,40,128]{2,1,0:T(8,128)S(1)} %pad_maximum_fusion.3), channel_id=1, source_target_pairs={{0,4},{1,5},{2,6},{3,7},{4,0},{5,1},{6,2},{7,3},{8,12},{9,13},{10,... | collective-permute-start | bytes 122888 | tf_op jit(solution)/shard_map/ppermute | solution.py:574
  34.8 6.3 %collective-permute-start.16 = (f32[4,16,128]{2,1,0:T(8,128)S(1)}, f32[4,16,128]{2,1,0:T(8,128)S(1)}, u32[]{:S(2)}, u32[]{:S(2)}) collective-permute-start(f32[4,16,128]{2,1,0:T(8,128)S(1)} %get-tuple-element.58), channel_id=1, source_target_pairs={{0,16},{8,24},{16,0},{24,8},{1,17},{9,25},{17,1},{25,9},{2,18},{10... | collective-permute-start | bytes 98312 | tf_op jit(solution)/shard_map/ppermute | solution.py:574
  37.6 5.4 %collective-permute-start.12 = (f32[4,24,128]{2,1,0:T(8,128)S(1)}, f32[4,24,128]{2,1,0:T(8,128)S(1)}, u32[]{:S(2)}, u32[]{:S(2)}) collective-permute-start(f32[4,24,128]{2,1,0:T(8,128)S(1)} %get-tuple-element.60), channel_id=1, source_target_pairs={{0,1},{1,0},{2,3},{3,2},{4,5},{5,4},{6,7},{7,6},{8,9},{9,8},{10,11... | collective-permute-start | bytes 147464 | tf_op jit(solution)/shard_map/ppermute | solution.py:574
  38.5 11.7 %all-to-all-start = ((f32[32,8,128]{2,1,0:T(8,128)}), f32[32,8,128]{2,1,0:T(8,128)S(1)}, u32[]{:S(2)}, u32[]{:S(2)}) async-start(f32[32,8,128]{2,1,0:T(8,128)} %get-tuple-element.56), calls=%async_computation | async-start | bytes 262144 | tf_op jit(solution)/shard_map/all_to_all | solution.py:637
  41.1 5.1 %collective-permute-start.17 = (f32[8,16,128]{2,1,0:T(8,128)S(1)}, f32[8,16,128]{2,1,0:T(8,128)S(1)}, u32[]{:S(2)}, u32[]{:S(2)}) collective-permute-start(f32[8,16,128]{2,1,0:T(8,128)S(1)} %pad_maximum_fusion.2), channel_id=1, source_target_pairs={{0,1},{1,0},{2,3},{3,2},{4,5},{5,4},{6,7},{7,6},{8,9},{9,8},{10,11... | collective-permute-start | bytes 196616 | tf_op jit(solution)/shard_map/ppermute | solution.py:574
  42.9 3.3 %collective-permute-start.18 = (f32[8,16,128]{2,1,0:T(8,128)S(1)}, f32[8,16,128]{2,1,0:T(8,128)S(1)}, u32[]{:S(2)}, u32[]{:S(2)}) collective-permute-start(f32[8,16,128]{2,1,0:T(8,128)S(1)} %pad_maximum_fusion.2), channel_id=1, source_target_pairs={{0,8},{8,0},{16,24},{24,16},{1,9},{9,1},{17,25},{25,17},{2,10},{10... | collective-permute-start | bytes 196616 | tf_op jit(solution)/shard_map/ppermute | solution.py:574
  42.9 5.9 %collective-permute-start.13 = (f32[8,24,128]{2,1,0:T(8,128)S(1)}, f32[8,24,128]{2,1,0:T(8,128)S(1)}, u32[]{:S(2)}, u32[]{:S(2)}) collective-permute-start(f32[8,24,128]{2,1,0:T(8,128)S(1)} %pad_maximum_fusion), channel_id=1, source_target_pairs={{0,16},{8,24},{16,0},{24,8},{1,17},{9,25},{17,1},{25,9},{2,18},{10... | collective-permute-start | bytes 294920 | tf_op jit(solution)/shard_map/ppermute | solution.py:574
  44.5 4.4 %collective-permute-start.14 = (f32[8,24,128]{2,1,0:T(8,128)S(1)}, f32[8,24,128]{2,1,0:T(8,128)S(1)}, u32[]{:S(2)}, u32[]{:S(2)}) collective-permute-start(f32[8,24,128]{2,1,0:T(8,128)S(1)} %pad_maximum_fusion), channel_id=1, source_target_pairs={{0,8},{8,0},{16,24},{24,16},{1,9},{9,1},{17,25},{25,17},{2,10},{10... | collective-permute-start | bytes 294920 | tf_op jit(solution)/shard_map/ppermute | solution.py:574
  46.2 2.8 %collective-permute-start.19 = (f32[8,16,128]{2,1,0:T(8,128)S(1)}, f32[8,16,128]{2,1,0:T(8,128)S(1)}, u32[]{:S(2)}, u32[]{:S(2)}) collective-permute-start(f32[8,16,128]{2,1,0:T(8,128)S(1)} %collective-permute-done.17), channel_id=1, source_target_pairs={{0,8},{8,0},{16,24},{24,16},{1,9},{9,1},{17,25},{25,17},{2,10},{10... | collective-permute-start | bytes 196616 | tf_op jit(solution)/shard_map/ppermute | solution.py:574
  48.9 1.3 %collective-permute-start.15 = (f32[8,24,128]{2,1,0:T(8,128)S(1)}, f32[8,24,128]{2,1,0:T(8,128)S(1)}, u32[]{:S(2)}, u32[]{:S(2)}) collective-permute-start(f32[8,24,128]{2,1,0:T(8,128)S(1)} %collective-permute-done.13), channel_id=1, source_target_pairs={{0,8},{8,0},{16,24},{24,16},{1,9},{9,1},{17,25},{25,17},{2,10},{10... | collective-permute-start | bytes 294920 | tf_op jit(solution)/shard_map/ppermute | solution.py:574

commit v4 on v3

--- a/solution.py
+++ b/solution.py
@@ -21,7 +21,6 @@
 
 PAIRS = ((0, 0), (0, 1), (0, 2), (1, 1), (1, 2), (2, 2))
 HROWS = 40
-SPLIT = 24
 KINDS = (3, 0, 1, 2)
 LIMIT = 32 * 1024 * 1024
 
@@ -225,7 +224,7 @@
     )(own, d0, d1, *asked)
 
 
-def moments_kernel(gy_count, r1, r0, a1, a0, ref, frac, grad, packed, extra, portions, side, slabs):
+def moments_kernel(gy_count, r0, r1, a1, a0, ref, frac, grad, packed, extra, portions, side, slabs):
     gx, gy = lax.axis_index("gx"), lax.axis_index("gy")
     gx_even, gy_even = even(gx), even(gy)
     side[...] = jnp.zeros((8, NZ * EDGE), F32)
@@ -290,7 +289,7 @@
     total = pltpu.roll(total, lax.rem(gx, 4) * NEL, 1)
     packed[...] = total[:HROWS]
     line = pltpu.roll(total[HROWS:], NEL, 1)[0:1] + pltpu.roll(total[HROWS:], 2 * NEL, 1)[1:2]
-    extra[...] = jnp.where(row == 6, line, 0.0)
+    extra[...] = jnp.where(row == 3, line, 0.0)
     element, lane_e = rows_of((EYD, 128)), lanes((EYD, 128))
     unfold = (lane_e // EDGE == element).astype(F32).astype(BF16)
     for ez in range(EZ):
@@ -315,7 +314,7 @@
         compiler_params=pltpu.CompilerParams(vmem_limit_bytes=LIMIT),
         cost_estimate=takes(2.2),
         name="moments",
-    )(faces_y[1], faces_y[0], faces_x[1], faces_x[0], ref, fractions)
+    )(faces_y[0], faces_y[1], faces_x[1], faces_x[0], ref, fractions)
 
 
 def warp_kernel(b0, b1, b2, b3, b4, place, ref, grad, portions, extra, mismatch, packed, bricks, tables, slabs, spots, sem):
@@ -357,11 +356,28 @@
                 slabs[start : start + EDGE, :] = collected[c][a]
     found = weighed_once(slabs[...], along_y(lambda group, at: hat_weight(lax.rem(group, 2), at), (0, 1, 2, 3)))
     across = hat_weight(lanes((EDGE, 128)) // (2 * NEL), rows_of((EDGE, 128)))
-    row8 = rows_of((8, 128))
+    row, lane = rows_of((8, 128)), lanes((8, 128))
+    group, in_z, in_y = lane // NEL, lax.rem(lane, NEL) // EYD, lax.rem(lane, EYD)
     total = jnp.zeros((8, 128), F32)
-    for slab in range(6):
-        total = jnp.where(row8 == slab, layered(found, slab, 6, across), total)
-    packed[...] = jnp.broadcast_to(pltpu.roll(total, lax.rem(gx, 4) * NEL, 1) + extra[...], packed.shape)
+    for c in range(3):
+        lower, upper = (layered(found, c * 2 + a, 6, across) for a in range(2))
+        lower, upper = (jnp.broadcast_to(line, (8, 128)) for line in (lower, upper))
+        level = lower + jnp.where(in_z > 0, pltpu.roll(upper, EYD, 1), 0.0)
+        top = jnp.where(in_z == EZ - 1, upper, 0.0)
+
+        def joined(line):
+            return line + jnp.where(in_y > 0, pltpu.roll(line, 128 - NEL + 1, 1), 0.0)
+
+        rim = jnp.where(in_y == EYD - 1, level, 0.0) + jnp.where(in_y == EYD - 2, pltpu.roll(top, 127, 1), 0.0)
+        main = jnp.where(lax.rem(group, 2) == 0, joined(level), rim)
+        total = jnp.where(row == c, main, total)
+        top = joined(top)
+        for bx in range(2):
+            start = 2 * NEL + (c * 2 + bx) * EYD
+            moved = pltpu.roll(top, (start - (bx * 2 * NEL + (EZ - 1) * EYD)) % 128, 1)
+            total = jnp.where((row == 3) & (lane // EYD == start // EYD), moved, total)
+    total = pltpu.roll(total, lax.rem(gx, 4) * NEL, 1) + extra[...]
+    packed[...] = jnp.broadcast_to(total[0:4], packed.shape)
 
 
 def warp(place, bricks, ref, grad, portions, extra):
@@ -369,7 +385,7 @@
     devices = lax.axis_size("gx") * lax.axis_size("gy")
     return pl.pallas_call(
         warp_kernel,
-        out_shape=(jax.ShapeDtypeStruct((NZ, EDGE, NY), F32), jax.ShapeDtypeStruct((devices, 8, 128), F32)),
+        out_shape=(jax.ShapeDtypeStruct((NZ, EDGE, NY), F32), jax.ShapeDtypeStruct((devices, 4, 128), F32)),
         in_specs=[vmem] * 10,
         out_specs=(vmem, vmem),
         scratch_shapes=[
@@ -398,17 +414,16 @@
             store(group, tile, pltpu.roll(merged, (128 - NEL * group) % 128, 1) if group else merged)
 
 
-def solve_kernel(gx_count, gy_count, first, second, load, out, coef, rhs):
+def solve_kernel(gx_count, gy_count, hess, load, out, coef, rhs):
     gx, gy = lax.axis_index("gx"), lax.axis_index("gy")
-    orders = gather_orders(gx_count, gy_count)
+    steps = gather_steps(gx_count, gy_count)
     tiles = -(-gx_count // 4)
     width = 128 * tiles
 
     def unpack(row, _):
         def hess_block(column):
             relative = dict(gx=jnp.bitwise_xor(gx, column), gy=jnp.bitwise_xor(gy, row))
-            parts = [half[block_index(order, relative)] for half, order in zip((first, second), orders)]
-            return jnp.concatenate(parts, axis=0)
+            return hess[block_index(steps, relative)]
 
         def store_hess(group, tile, value):
             coef[tile, pl.ds(row * 4 * HROWS + group * HROWS, HROWS), :] = value
@@ -417,7 +432,7 @@
             return load[column * gy_count + row]
 
         def store_load(group, tile, value):
-            rhs[tile, pl.ds(row * 32 + group * 8, 8), :] = value
+            rhs[tile, pl.ds(row * 16 + group * 4, 4), :] = value
 
         spread_groups(hess_block, 4, gx_count, store_hess)
         spread_groups(load_block, 4, gx_count, store_load)
@@ -476,7 +491,7 @@
         spare = wy * 14 + source - HROWS
         if spare < HROWS:
             return strided(coef, 3 * HROWS + spare, 4 * HROWS)
-        return strided(rhs, (spare - HROWS) * 8 + 6, 32)
+        return strided(rhs, (spare - HROWS) * 4 + 3, 16)
 
     pair_of = {}
     for p, (c, d) in enumerate(PAIRS):
@@ -519,8 +534,22 @@
 
     residual = []
     for c in range(3):
-        parts = [strided(rhs, (b * 2 + d) * 8 + c * 2 + a, 32) for a, b, d in bits]
-        residual.append(settle(parts))
+        main, top = None, None
+        for bx in range(2):
+            inside = strided(rhs, 2 * bx * 4 + c, 16)
+            rim = turn(strided(rhs, (2 * bx + 1) * 4 + c, 16), 1, 0)
+            spot = c * 2 + bx
+            upper = strided(rhs, (2 + spot // 4) * 4 + 3, 16)
+            upper = jnp.where(last_z, turn(upper, (EZ - 1 - spot % 4) * EYD, 1), 0.0)
+            reached = first_y & (row > 0)
+            inside = inside + jnp.where(reached, turn(rim, 1 - EYD, 1), 0.0)
+            upper = upper + jnp.where(reached & last_z, turn(rim, 2 - EYD, 1), 0.0)
+            if bx:
+                main = main + jnp.where(first_x, 0.0, turn(inside, NEL, 1))
+                top = top + jnp.where(first_x, 0.0, turn(upper, NEL, 1))
+            else:
+                main, top = inside, upper
+        residual.append((main, top))
     direction = residual
     increment = None
     norm_now = inner(residual, residual)
@@ -549,23 +578,23 @@
                 out[c, level] = short[0:1, start : start + EYD]
 
 
-def solve(first, second, load):
+def solve(hess, load):
     gx_count, gy_count = lax.axis_size("gx"), lax.axis_size("gy")
     tiles = -(-gx_count // 4)
     vmem = pl.BlockSpec(memory_space=pltpu.VMEM)
     return pl.pallas_call(
         functools.partial(solve_kernel, gx_count, gy_count),
         out_shape=jax.ShapeDtypeStruct((3, EZ + 1, 1, EYD), F32),
-        in_specs=[vmem] * 3,
+        in_specs=[vmem] * 2,
         out_specs=vmem,
         scratch_shapes=[
             pltpu.VMEM((tiles, gy_count * 4 * HROWS, 128), F32),
-            pltpu.VMEM((tiles, gy_count * 32, 128), F32),
+            pltpu.VMEM((tiles, gy_count * 16, 128), F32),
         ],
         compiler_params=pltpu.CompilerParams(vmem_limit_bytes=LIMIT),
         cost_estimate=takes(3.5),
         name="solve",
-    )(first, second, load)
+    )(hess, load)
 
 
 def swap(array, axis, partner):
@@ -596,11 +625,6 @@
     return [*far, ("gy", 1), *[("gx", 1 << k) for k in reversed(range(gx_count.bit_length() - 1))]]
 
 
-def gather_orders(gx_count, gy_count):
-    steps = gather_steps(gx_count, gy_count)
-    return steps, [*steps[:-3], steps[-2], steps[-3], steps[-1]]
-
-
 def block_index(steps, relative):
     found = 0
     for k, (axis, bit) in enumerate(steps):
@@ -608,11 +632,13 @@
     return found
 
 
-def doubled(known, step, pieces=1):
+def swapped(known, step):
     axis, bit = step
-    size = known.shape[0] // pieces
-    sent = [swap(known[i * size : (i + 1) * size], axis, lambda j: j ^ bit) for i in range(pieces)]
-    return jnp.concatenate([known, *sent], axis=0)
+    return swap(known, axis, lambda j: j ^ bit)
+
+
+def doubled(known, step):
+    return jnp.concatenate([known, swapped(known, step)], axis=0)
 
 
 def body(reference_image, deformed_image, route, within, xshift, fractions):
@@ -623,22 +649,24 @@
     q = {kind: swap_y(asks[kind], kind) for kind in KINDS}
     d1, d0 = swap_x(thick, 1), swap_x(thick, 0)
     grad, packed, extra, portions = moments(reference_image, (d0, d1), (q[0], q[1]), fractions.reshape(NEL, 3))
+    q[3], q[0], q[1], q[2], packed = lax.optimization_barrier((q[3], q[0], q[1], q[2], packed))
     *served, at_home = serve(deformed_image, d0, d1, [q[kind] for kind in KINDS] + [own], [8 * (k < 2) + k for k in KINDS] + [4])
-    known, at_home = lax.optimization_barrier((packed[None], at_home))
+    known = packed[None]
     bricks = [swap_y(block, kind) for kind, block in zip(KINDS, served)] + [at_home]
-    orders = gather_orders(lax.axis_size("gx"), lax.axis_size("gy"))
-    steps = orders[0]
-    for step in steps[:-4]:
+    steps = gather_steps(lax.axis_size("gx"), lax.axis_size("gy"))
+    for k, step in enumerate(steps[:-3]):
+        if k == 1:
+            known, at_home = lax.optimization_barrier((known, at_home))
         known = doubled(known, step)
+    bricks[-1] = at_home
     bricks, known = lax.optimization_barrier((bricks, known))
     mismatch, part = warp(place, bricks, reference_image, grad, portions, extra)
-    known = doubled(known, steps[-4])
-    known, part = lax.optimization_barrier((known, part))
+    beside, across = swapped(known, steps[-3]), swapped(known, steps[-2])
+    beside, across, _ = lax.optimization_barrier((beside, across, part))
     load = lax.all_to_all(part, ("gx", "gy"), 0, 0)
-    halves = [known[:, :SPLIT], known[:, SPLIT:]]
-    for k in (-3, -2, -1):
-        halves = [doubled(half, order[k], 2 if k == -1 else 1) for half, order in zip(halves, orders)]
-    return solve(*halves, load), mismatch
+    blocks = [known, beside, across, swapped(beside, steps[-2])]
+    blocks = blocks + [swapped(block, steps[-1]) for block in blocks]
+    return solve(jnp.concatenate(blocks, axis=0), load), mismatch
 
 
 def solution(mesh):

time: 53.9 us -> 51.4 us (0.954)
  waiting for transfers between devices: 16 us -> 13.4 us
    ppermute x20 -> x19, waiting for transfers between devices: 16 us -> 12.4 us  [swap(): lax.ppermute(array, axis, [(i, j) for i, j in pairs if 0 <= j < size])]
    all_to_all x1, starting transfers between devices: 2.58 us -> 3.75 us  [body(): load = lax.all_to_all(part, ('gx', 'gy'), 0, 0)]
    ppermute x20 -> x19, starting transfers between devices: 20.9 us -> 19.9 us  [swap(): lax.ppermute(array, axis, [(i, j) for i, j in pairs if 0 <= j < size])]
    all_to_all x1, waiting for transfers between devices: 0.01 us -> 0.94 us  [body(): load = lax.all_to_all(part, ('gx', 'gy'), 0, 0)]
  transfers between devices with their start and end apart: 21 -> 20, of which waited for: 9 -> 8; matrix products, arithmetic and copies ran while one was open for 0% -> 0% of each run, Pallas kernels for 9% -> 14%
where the time goes in v4:
time: 51.4 us; the launch traced here: 51.2 us
  starting transfers between devices  23.7 us (46%)
  waiting for transfers between devices  13.4 us (26%)
  Pallas kernels  13.1 us (25%)
  between operations  0.81 us (2%)
    ppermute x19, starting transfers between devices, swap(): lax.ppermute(array, axis, [(i, j) for i, j in pairs if 0 <= j < size])  19.9 us
    ppermute x19, waiting for transfers between devices, swap(): lax.ppermute(array, axis, [(i, j) for i, j in pairs if 0 <= j < size])  12.4 us
    all_to_all x1, starting transfers between devices, body(): load = lax.all_to_all(part, ('gx', 'gy'), 0, 0)  3.75 us
    pallas_call x1, Pallas kernels, solve(): pl.pallas_call(functools.partial(solve_kernel, gx_count, gy_count), out_s...  3.4 us
    pallas_call x1, Pallas kernels, warp(): pl.pallas_call(warp_kernel, out_shape=(jax.ShapeDtypeStruct((NZ, EDGE, NY...  2.84 us
    pallas_call x1, Pallas kernels, serve(): pl.pallas_call(functools.partial(serve_kernel, lines), out_shape=(jax.Sha...  2.6 us
    pallas_call x1, Pallas kernels, ask(): pl.pallas_call(functools.partial(ask_kernel, lax.axis_size('gx')), out_sh...  2.35 us
    pallas_call x1, Pallas kernels, moments(): pl.pallas_call(functools.partial(moments_kernel, lax.axis_size('gy')), ou...  1.94 us
  transfers between devices with their start and end apart: 20, of which 8 were waited for; matrix products, arithmetic and copies ran while one was open for 0% of the time, Pallas kernels for 14%

profile of v4, /device:TPU:0, one launch (start us, length us, event | category | flops | bytes accessed | tf_op | source)
XLA Modules:
  0.0 51.2 jit_solution(2284185690215959036)
XLA Ops:
  0.6 2.3 %ask.1 = (f32[16,128]{1,0:T(8,128)}, f32[16,128]{1,0:T(8,128)}, f32[8,128]{1,0:T(8,128)}, f32[8,128]{1,0:T(8,128)}, bf16[72,16,128]{2,1,0:T(8,128)(2,1)}, /*index=5*/f32[8,128]{1,0:T(8,128)}, s32[8,128]{1,0:T(8,128)}) custom-call(s32[32]{0:T(128)} %bitcast.8, s32[32]{0:T(128)} %bitcast.9, s32[32]{0:T(128)} %bitcast.10, bf16[64,16,128]{2,1,0:T(8,128)(2,1)} %ref.5, ...), custom_call_target="tpu_custom_call" | custom-call | bytes 7380000 | tf_op jit(solution)/shard_map/ask/pallas_call | solution.py:155
  3.0 0.5 collective-permute-start
  3.4 0.7 %collective-permute-start.1 = (bf16[72,16,128]{2,1,0:T(8,128)(2,1)}, bf16[72,16,128]{2,1,0:T(8,128)(2,1)S(1)}, u32[]{:S(2)}, u32[]{:S(2)}) collective-permute-start(bf16[72,16,128]{2,1,0:T(8,128)(2,1)} %get-tuple-element.35), channel_id=1, source_target_pairs={{8,16},{16,8},{9,17},{17,9},{10,18},{18,10},{11,19},{19,11},{12,20... | collective-permute-start | bytes 884744 | tf_op jit(solution)/shard_map/ppermute | solution.py:603
  4.1 2.6 %collective-permute-start.3 = (f32[16,128]{1,0:T(8,128)}, f32[16,128]{1,0:T(8,128)S(1)}, u32[]{:S(2)}, u32[]{:S(2)}) collective-permute-start(f32[16,128]{1,0:T(8,128)} %get-tuple-element.37), channel_id=1, source_target_pairs={{0,1},{1,0},{2,3},{3,2},{4,5},{5,4},{6,7},{7,6},{8,9},{9,8},{10,11... | collective-permute-start | bytes 24584 | tf_op jit(solution)/shard_map/ppermute | solution.py:603
  6.7 3.6 %collective-permute-start.4 = (f32[16,128]{1,0:T(8,128)}, f32[16,128]{1,0:T(8,128)S(1)}, u32[]{:S(2)}, u32[]{:S(2)}) collective-permute-start(f32[16,128]{1,0:T(8,128)} %get-tuple-element.38), channel_id=1, source_target_pairs={{0,7},{1,2},{2,1},{3,4},{4,3},{5,6},{6,5},{7,0},{8,15},{9,10},{10,... | collective-permute-start | bytes 24584 | tf_op jit(solution)/shard_map/ppermute | solution.py:603
  10.3 0.4 collective-permute-start.2
  10.7 0.0 collective-permute-done.3.r0.refs_4_
  10.7 0.1 copy.9
  10.8 2.4 %collective-permute-done.4.r1.refs_5_ = f32[16,128]{1,0:T(8,128)S(1)} collective-permute-done((f32[16,128]{1,0:T(8,128)}, f32[16,128]{1,0:T(8,128)S(1)}, u32[]{:S(2)}, u32[]{:S(2)}) %collective-permute-start.4) | collective-permute-done | bytes 8224 | tf_op jit(solution)/shard_map/ppermute | solution.py:603
  13.3 0.0 copy-start.1
  13.3 1.9 %moments.1 = (bf16[3,64,16,128]{3,2,1,0:T(8,128)(2,1)S(1)}, f32[40,128]{1,0:T(8,128)S(1)}, f32[8,128]{1,0:T(8,128)S(1)}, f32[4,8,128]{2,1,0:T(8,128)S(1)}) custom-call(f32[16,128]{1,0:T(8,128)S(1)} %collective-permute-done.3.r0.refs_4_, f32[16,128]{1,0:T(8,128)S(1)} %collective-permute-done.4.r1.refs_5_, ...), custom_call_target="tpu_custom_call" | custom-call | bytes 8118000 | tf_op jit(solution)/shard_map/moments/pallas_call | solution.py:303
  15.2 0.7 %collective-permute-done.2.refs_3_ = f32[8,128]{1,0:T(8,128)S(1)} collective-permute-done((f32[8,128]{1,0:T(8,128)}, f32[8,128]{1,0:T(8,128)S(1)}, u32[]{:S(2)}, u32[]{:S(2)}) %collective-permute-start.2) | collective-permute-done | bytes 4128 | tf_op jit(solution)/shard_map/ppermute | solution.py:603
  15.9 0.0 copy-done.2
  15.9 2.6 %serve.1 = (bf16[16,16,128]{2,1,0:T(8,128)(2,1)S(1)}, bf16[16,16,128]{2,1,0:T(8,128)(2,1)S(1)}, bf16[16,16,128]{2,1,0:T(8,128)(2,1)S(1)}, bf16[16,16,128]{2,1,0:T(8,128)(2,1)S(1)}, bf16[16,16,128]{2,1,0:T(8,128)(2,1)S(1)}) custom-call(bf16[64,16,128]{2,1,0:T(8,128)(2,1)S(1)} %copy-done.1, bf16[72,16,128]{2,1,0:T(8,128)(2,1)S(1)} %collective-permute-done.a0.refs_1_, ...), custom_call_target="tpu_custom_call" | custom-call | bytes 7380000 | tf_op jit(solution)/shard_map/serve/pallas_call | solution.py:210
  18.5 1.2 %collective-permute-done.10 = f32[1,40,128]{2,1,0:T(8,128)S(1)} collective-permute-done((f32[1,40,128]{2,1,0:T(8,128)S(1)}, f32[1,40,128]{2,1,0:T(8,128)S(1)}, u32[]{:S(2)}, u32[]{:S(2)}) %collective-permute-start.10) | collective-permute-done | bytes 20512 | tf_op jit(solution)/shard_map/ppermute | solution.py:603
  19.7 1.3 %collective-permute-start.11 = (f32[2,40,128]{2,1,0:T(8,128)S(1)}, f32[2,40,128]{2,1,0:T(8,128)S(1)}, u32[]{:S(2)}, u32[]{:S(2)}) collective-permute-start(f32[2,40,128]{2,1,0:T(8,128)S(1)} %pad_maximum_fusion.1), channel_id=1, source_target_pairs={{0,4},{1,5},{2,6},{3,7},{4,0},{5,1},{6,2},{7,3},{8,12},{9,13},{10,... | collective-permute-start | bytes 122888 | tf_op jit(solution)/shard_map/ppermute | solution.py:603
  21.0 2.0 %collective-permute-start.6 = (bf16[16,16,128]{2,1,0:T(8,128)(2,1)S(1)}, bf16[16,16,128]{2,1,0:T(8,128)(2,1)S(1)}, u32[]{:S(2)}, u32[]{:S(2)}) collective-permute-start(bf16[16,16,128]{2,1,0:T(8,128)(2,1)S(1)} %get-tuple-element.46), channel_id=1, source_target_pairs={{0,6},{1,7},{2,4},{3,5},{4,2},{5,3},{6,0},{7,1},{8,14},{9,15},{10,... | collective-permute-start | bytes 196616 | tf_op jit(solution)/shard_map/ppermute | solution.py:603
  23.0 0.3 collective-permute-start.7
  23.3 3.0 %collective-permute-start.8 = (bf16[16,16,128]{2,1,0:T(8,128)(2,1)S(1)}, bf16[16,16,128]{2,1,0:T(8,128)(2,1)S(1)}, u32[]{:S(2)}, u32[]{:S(2)}) collective-permute-start(bf16[16,16,128]{2,1,0:T(8,128)(2,1)S(1)} %get-tuple-element.48), channel_id=1, source_target_pairs={{0,7},{1,2},{2,1},{3,4},{4,3},{5,6},{6,5},{7,0},{8,15},{9,10},{10,... | collective-permute-start | bytes 196616 | tf_op jit(solution)/shard_map/ppermute | solution.py:603
  26.3 0.2 collective-permute-start.9
  26.5 1.0 %collective-permute-done.6.b0 = bf16[16,16,128]{2,1,0:T(8,128)(2,1)S(1)} collective-permute-done((bf16[16,16,128]{2,1,0:T(8,128)(2,1)S(1)}, bf16[16,16,128]{2,1,0:T(8,128)(2,1)S(1)}, u32[]{:S(2)}, u32[]{:S(2)}) %collective-permute-start.6) | collective-permute-done | bytes 65568 | tf_op jit(solution)/shard_map/ppermute | solution.py:603
  27.5 3.3 %collective-permute-done.8.b2 = bf16[16,16,128]{2,1,0:T(8,128)(2,1)S(1)} collective-permute-done((bf16[16,16,128]{2,1,0:T(8,128)(2,1)S(1)}, bf16[16,16,128]{2,1,0:T(8,128)(2,1)S(1)}, u32[]{:S(2)}, u32[]{:S(2)}) %collective-permute-start.8) | collective-permute-done | bytes 65568 | tf_op jit(solution)/shard_map/ppermute | solution.py:603
  30.8 1.4 %collective-permute-start.12 = (f32[4,40,128]{2,1,0:T(8,128)S(1)}, f32[4,40,128]{2,1,0:T(8,128)S(1)}, u32[]{:S(2)}, u32[]{:S(2)}) collective-permute-start(f32[4,40,128]{2,1,0:T(8,128)S(1)} %pad_maximum_fusion), channel_id=1, source_target_pairs={{0,1},{1,0},{2,3},{3,2},{4,5},{5,4},{6,7},{7,6},{8,9},{9,8},{10,11... | collective-permute-start | bytes 245768 | tf_op jit(solution)/shard_map/ppermute | solution.py:603
  32.2 1.7 %collective-permute-start.13 = (f32[4,40,128]{2,1,0:T(8,128)S(1)}, f32[4,40,128]{2,1,0:T(8,128)S(1)}, u32[]{:S(2)}, u32[]{:S(2)}) collective-permute-start(f32[4,40,128]{2,1,0:T(8,128)S(1)} %pad_maximum_fusion), channel_id=1, source_target_pairs={{0,16},{8,24},{16,0},{24,8},{1,17},{9,25},{17,1},{25,9},{2,18},{10... | collective-permute-start | bytes 245768 | tf_op jit(solution)/shard_map/ppermute | solution.py:603
  33.9 2.8 %warp.1 = (f32[64,16,128]{2,1,0:T(8,128)}, f32[32,4,128]{2,1,0:T(4,128)}) custom-call(bf16[16,16,128]{2,1,0:T(8,128)(2,1)S(1)} %collective-permute-done.6.b0, bf16[16,16,128]{2,1,0:T(8,128)(2,1)S(1)} %collective-permute-done.7.b1, bf16[16,16,128]{2,1,0:T(8,128)(2,1)S(1)} %collective-permute-done.8.b2, bf16[16,16,128]{2,1,0:T(8,128)(2,1)S(1)} %collective-permute-done.9.b3, ...), custom_call_target="tpu_custom_call" | custom-call | bytes 14760000 | tf_op jit(solution)/shard_map/warp/pallas_call | solution.py:386
  36.7 3.7 %all-to-all-start = ((f32[32,4,128]{2,1,0:T(4,128)}), f32[32,4,128]{2,1,0:T(4,128)S(1)}, u32[]{:S(2)}, u32[]{:S(2)}) async-start(f32[32,4,128]{2,1,0:T(4,128)} %get-tuple-element.64), calls=%async_computation | async-start | bytes 131072 | tf_op jit(solution)/shard_map/all_to_all | solution.py:666
  40.5 1.8 %collective-permute-start.14 = (f32[4,40,128]{2,1,0:T(8,128)S(1)}, f32[4,40,128]{2,1,0:T(8,128)S(1)}, u32[]{:S(2)}, u32[]{:S(2)}) collective-permute-start(f32[4,40,128]{2,1,0:T(8,128)S(1)} %collective-permute-done.12), channel_id=1, source_target_pairs={{0,16},{8,24},{16,0},{24,8},{1,17},{9,25},{17,1},{25,9},{2,18},{10... | collective-permute-start | bytes 245768 | tf_op jit(solution)/shard_map/ppermute | solution.py:603
  42.4 0.5 collective-permute-start.17
  42.9 2.7 %collective-permute-done.14 = f32[4,40,128]{2,1,0:T(8,128)S(1)} collective-permute-done((f32[4,40,128]{2,1,0:T(8,128)S(1)}, f32[4,40,128]{2,1,0:T(8,128)S(1)}, u32[]{:S(2)}, u32[]{:S(2)}) %collective-permute-start.14) | collective-permute-done | bytes 81952 | tf_op jit(solution)/shard_map/ppermute | solution.py:603
  45.6 1.2 %collective-permute-done.18 = f32[4,40,128]{2,1,0:T(8,128)S(1)} collective-permute-done((f32[4,40,128]{2,1,0:T(8,128)S(1)}, f32[4,40,128]{2,1,0:T(8,128)S(1)}, u32[]{:S(2)}, u32[]{:S(2)}) %collective-permute-start.18) | collective-permute-done | bytes 81952 | tf_op jit(solution)/shard_map/ppermute | solution.py:603
  46.8 0.9 %all-to-all-done.load = f32[32,4,128]{2,1,0:T(4,128)S(1)} async-done(((f32[32,4,128]{2,1,0:T(4,128)}), f32[32,4,128]{2,1,0:T(4,128)S(1)}, u32[]{:S(2)}, u32[]{:S(2)}) %all-to-all-start) | async-done | bytes 65568 | tf_op jit(solution)/shard_map/all_to_all | solution.py:666
  47.8 3.4 %solve.1 = f32[3,5,1,8]{3,2,1,0:T(1,128)} custom-call(f32[32,40,128]{2,1,0:T(8,128)S(1)} %constant_dynamic-update-slice_fusion.hess, f32[32,4,128]{2,1,0:T(4,128)S(1)} %all-to-all-done.load), custom_call_target="tpu_custom_call" | custom-call | bytes 12915000 | tf_op jit(solution)/shard_map/solve/pallas_call | solution.py:585
  (36 shorter events, 0.1 us)
Async XLA Ops:
  0.6 12.6 %copy-start = (bf16[64,16,128]{2,1,0:T(8,128)(2,1)S(1)}, bf16[64,16,128]{2,1,0:T(8,128)(2,1)}, u32[]{:S(2)}) copy-start(bf16[64,16,128]{2,1,0:T(8,128)(2,1)} %ref.5) | copy-start | bytes 786436
  3.0 7.7 %copy-start.5 = (f32[8,128]{1,0:T(8,128)S(1)}, f32[8,128]{1,0:T(8,128)}, u32[]{:S(2)}) copy-start(f32[8,128]{1,0:T(8,128)} %get-tuple-element.39) | copy-start | bytes 12292
  3.0 10.3 %collective-permute-start = (bf16[72,16,128]{2,1,0:T(8,128)(2,1)}, bf16[72,16,128]{2,1,0:T(8,128)(2,1)S(1)}, u32[]{:S(2)}, u32[]{:S(2)}) collective-permute-start(bf16[72,16,128]{2,1,0:T(8,128)(2,1)} %get-tuple-element.35), channel_id=1, source_target_pairs={{0,8},{8,0},{16,24},{24,16},{1,9},{9,1},{17,25},{25,17},{2,10},{10... | collective-permute-start | bytes 884744 | tf_op jit(solution)/shard_map/ppermute | solution.py:603
  3.4 9.8 %collective-permute-start.1 = (bf16[72,16,128]{2,1,0:T(8,128)(2,1)}, bf16[72,16,128]{2,1,0:T(8,128)(2,1)S(1)}, u32[]{:S(2)}, u32[]{:S(2)}) collective-permute-start(bf16[72,16,128]{2,1,0:T(8,128)(2,1)} %get-tuple-element.35), channel_id=1, source_target_pairs={{8,16},{16,8},{9,17},{17,9},{10,18},{18,10},{11,19},{19,11},{12,20... | collective-permute-start | bytes 884744 | tf_op jit(solution)/shard_map/ppermute | solution.py:603
  4.1 6.6 %collective-permute-start.3 = (f32[16,128]{1,0:T(8,128)}, f32[16,128]{1,0:T(8,128)S(1)}, u32[]{:S(2)}, u32[]{:S(2)}) collective-permute-start(f32[16,128]{1,0:T(8,128)} %get-tuple-element.37), channel_id=1, source_target_pairs={{0,1},{1,0},{2,3},{3,2},{4,5},{5,4},{6,7},{7,6},{8,9},{9,8},{10,11... | collective-permute-start | bytes 24584 | tf_op jit(solution)/shard_map/ppermute | solution.py:603
  6.7 4.0 %copy-start.4 = (s32[1,1,32,3]{2,1,3,0:T(1,128)S(1)}, s32[1,1,32,3]{2,1,3,0:T(1,128)}, u32[]{:S(2)}) copy-start(s32[1,1,32,3]{2,1,3,0:T(1,128)} %param.11) | copy-start | bytes 1156
  6.7 6.6 %collective-permute-start.4 = (f32[16,128]{1,0:T(8,128)}, f32[16,128]{1,0:T(8,128)S(1)}, u32[]{:S(2)}, u32[]{:S(2)}) collective-permute-start(f32[16,128]{1,0:T(8,128)} %get-tuple-element.38), channel_id=1, source_target_pairs={{0,7},{1,2},{2,1},{3,4},{4,3},{5,6},{6,5},{7,0},{8,15},{9,10},{10,... | collective-permute-start | bytes 24584 | tf_op jit(solution)/shard_map/ppermute | solution.py:603
  10.3 5.6 %collective-permute-start.2 = (f32[8,128]{1,0:T(8,128)}, f32[8,128]{1,0:T(8,128)S(1)}, u32[]{:S(2)}, u32[]{:S(2)}) collective-permute-start(f32[8,128]{1,0:T(8,128)} %get-tuple-element.36), channel_id=1, source_target_pairs={{0,6},{1,7},{2,4},{3,5},{4,2},{5,3},{6,0},{7,1},{8,14},{9,15},{10,... | collective-permute-start | bytes 12296 | tf_op jit(solution)/shard_map/ppermute | solution.py:603
  10.7 5.2 %collective-permute-start.5 = (f32[8,128]{1,0:T(8,128)S(1)}, f32[8,128]{1,0:T(8,128)S(1)}, u32[]{:S(2)}, u32[]{:S(2)}) collective-permute-start(f32[8,128]{1,0:T(8,128)S(1)} %copy-done.5), channel_id=1, source_target_pairs={{0,2},{1,3},{2,0},{3,1},{4,6},{5,7},{6,4},{7,5},{8,10},{9,11},{10,... | collective-permute-start | bytes 12296 | tf_op jit(solution)/shard_map/ppermute | solution.py:603
  13.3 2.6 %copy-start.1 = (bf16[64,16,128]{2,1,0:T(8,128)(2,1)S(1)}, bf16[64,16,128]{2,1,0:T(8,128)(2,1)}, u32[]{:S(2)}) copy-start(bf16[64,16,128]{2,1,0:T(8,128)(2,1)} %refs_0_.1) | copy-start | bytes 786436
  15.2 0.7 %copy-start.2 = (f32[8,128]{1,0:T(8,128)S(1)}, f32[8,128]{1,0:T(8,128)}, u32[]{:S(2)}) copy-start(f32[8,128]{1,0:T(8,128)} %get-tuple-element.45.refs_7_) | copy-start | bytes 12292
  15.9 3.8 %collective-permute-start.10 = (f32[1,40,128]{2,1,0:T(8,128)S(1)}, f32[1,40,128]{2,1,0:T(8,128)S(1)}, u32[]{:S(2)}, u32[]{:S(2)}) collective-permute-start(f32[1,40,128]{2,1,0:T(8,128)S(1)} %bitcast.6), channel_id=1, source_target_pairs={{0,2},{1,3},{2,0},{3,1},{4,6},{5,7},{6,4},{7,5},{8,10},{9,11},{10,... | collective-permute-start | bytes 61448 | tf_op jit(solution)/shard_map/ppermute | solution.py:603
  19.7 6.8 %collective-permute-start.11 = (f32[2,40,128]{2,1,0:T(8,128)S(1)}, f32[2,40,128]{2,1,0:T(8,128)S(1)}, u32[]{:S(2)}, u32[]{:S(2)}) collective-permute-start(f32[2,40,128]{2,1,0:T(8,128)S(1)} %pad_maximum_fusion.1), channel_id=1, source_target_pairs={{0,4},{1,5},{2,6},{3,7},{4,0},{5,1},{6,2},{7,3},{8,12},{9,13},{10,... | collective-permute-start | bytes 122888 | tf_op jit(solution)/shard_map/ppermute | solution.py:603
  21.0 6.6 %collective-permute-start.6 = (bf16[16,16,128]{2,1,0:T(8,128)(2,1)S(1)}, bf16[16,16,128]{2,1,0:T(8,128)(2,1)S(1)}, u32[]{:S(2)}, u32[]{:S(2)}) collective-permute-start(bf16[16,16,128]{2,1,0:T(8,128)(2,1)S(1)} %get-tuple-element.46), channel_id=1, source_target_pairs={{0,6},{1,7},{2,4},{3,5},{4,2},{5,3},{6,0},{7,1},{8,14},{9,15},{10,... | collective-permute-start | bytes 196616 | tf_op jit(solution)/shard_map/ppermute | solution.py:603
  23.0 4.5 %collective-permute-start.7 = (bf16[16,16,128]{2,1,0:T(8,128)(2,1)S(1)}, bf16[16,16,128]{2,1,0:T(8,128)(2,1)S(1)}, u32[]{:S(2)}, u32[]{:S(2)}) collective-permute-start(bf16[16,16,128]{2,1,0:T(8,128)(2,1)S(1)} %get-tuple-element.47), channel_id=1, source_target_pairs={{0,1},{1,0},{2,3},{3,2},{4,5},{5,4},{6,7},{7,6},{8,9},{9,8},{10,11... | collective-permute-start | bytes 196616 | tf_op jit(solution)/shard_map/ppermute | solution.py:603
  23.3 7.5 %collective-permute-start.8 = (bf16[16,16,128]{2,1,0:T(8,128)(2,1)S(1)}, bf16[16,16,128]{2,1,0:T(8,128)(2,1)S(1)}, u32[]{:S(2)}, u32[]{:S(2)}) collective-permute-start(bf16[16,16,128]{2,1,0:T(8,128)(2,1)S(1)} %get-tuple-element.48), channel_id=1, source_target_pairs={{0,7},{1,2},{2,1},{3,4},{4,3},{5,6},{6,5},{7,0},{8,15},{9,10},{10,... | collective-permute-start | bytes 196616 | tf_op jit(solution)/shard_map/ppermute | solution.py:603
  26.3 4.5 %collective-permute-start.9 = (bf16[16,16,128]{2,1,0:T(8,128)(2,1)S(1)}, bf16[16,16,128]{2,1,0:T(8,128)(2,1)S(1)}, u32[]{:S(2)}, u32[]{:S(2)}) collective-permute-start(bf16[16,16,128]{2,1,0:T(8,128)(2,1)S(1)} %get-tuple-element.49), channel_id=1, source_target_pairs={{0,2},{1,3},{2,0},{3,1},{4,6},{5,7},{6,4},{7,5},{8,10},{9,11},{10,... | collective-permute-start | bytes 196616 | tf_op jit(solution)/shard_map/ppermute | solution.py:603
  26.5 7.4 %copy-start.3 = (s32[8,128]{1,0:T(8,128)S(1)}, s32[8,128]{1,0:T(8,128)}, u32[]{:S(2)}) copy-start(s32[8,128]{1,0:T(8,128)} %get-tuple-element.60.place) | copy-start | bytes 12292
  30.8 9.7 %collective-permute-start.12 = (f32[4,40,128]{2,1,0:T(8,128)S(1)}, f32[4,40,128]{2,1,0:T(8,128)S(1)}, u32[]{:S(2)}, u32[]{:S(2)}) collective-permute-start(f32[4,40,128]{2,1,0:T(8,128)S(1)} %pad_maximum_fusion), channel_id=1, source_target_pairs={{0,1},{1,0},{2,3},{3,2},{4,5},{5,4},{6,7},{7,6},{8,9},{9,8},{10,11... | collective-permute-start | bytes 245768 | tf_op jit(solution)/shard_map/ppermute | solution.py:603
  32.2 8.3 %collective-permute-start.13 = (f32[4,40,128]{2,1,0:T(8,128)S(1)}, f32[4,40,128]{2,1,0:T(8,128)S(1)}, u32[]{:S(2)}, u32[]{:S(2)}) collective-permute-start(f32[4,40,128]{2,1,0:T(8,128)S(1)} %pad_maximum_fusion), channel_id=1, source_target_pairs={{0,16},{8,24},{16,0},{24,8},{1,17},{9,25},{17,1},{25,9},{2,18},{10... | collective-permute-start | bytes 245768 | tf_op jit(solution)/shard_map/ppermute | solution.py:603
  33.9 11.7 %collective-permute-start.15 = (f32[4,40,128]{2,1,0:T(8,128)S(1)}, f32[4,40,128]{2,1,0:T(8,128)S(1)}, u32[]{:S(2)}, u32[]{:S(2)}) collective-permute-start(f32[4,40,128]{2,1,0:T(8,128)S(1)} %pad_maximum_fusion), channel_id=1, source_target_pairs={{0,8},{8,0},{16,24},{24,16},{1,9},{9,1},{17,25},{25,17},{2,10},{10... | collective-permute-start | bytes 245768 | tf_op jit(solution)/shard_map/ppermute | solution.py:603
  36.7 11.0 %all-to-all-start = ((f32[32,4,128]{2,1,0:T(4,128)}), f32[32,4,128]{2,1,0:T(4,128)S(1)}, u32[]{:S(2)}, u32[]{:S(2)}) async-start(f32[32,4,128]{2,1,0:T(4,128)} %get-tuple-element.64), calls=%async_computation | async-start | bytes 131072 | tf_op jit(solution)/shard_map/all_to_all | solution.py:666
  40.5 5.0 %collective-permute-start.14 = (f32[4,40,128]{2,1,0:T(8,128)S(1)}, f32[4,40,128]{2,1,0:T(8,128)S(1)}, u32[]{:S(2)}, u32[]{:S(2)}) collective-permute-start(f32[4,40,128]{2,1,0:T(8,128)S(1)} %collective-permute-done.12), channel_id=1, source_target_pairs={{0,16},{8,24},{16,0},{24,8},{1,17},{9,25},{17,1},{25,9},{2,18},{10... | collective-permute-start | bytes 245768 | tf_op jit(solution)/shard_map/ppermute | solution.py:603
  42.3 3.2 %collective-permute-start.16 = (f32[4,40,128]{2,1,0:T(8,128)S(1)}, f32[4,40,128]{2,1,0:T(8,128)S(1)}, u32[]{:S(2)}, u32[]{:S(2)}) collective-permute-start(f32[4,40,128]{2,1,0:T(8,128)S(1)} %collective-permute-done.12), channel_id=1, source_target_pairs={{0,8},{8,0},{16,24},{24,16},{1,9},{9,1},{17,25},{25,17},{2,10},{10... | collective-permute-start | bytes 245768 | tf_op jit(solution)/shard_map/ppermute | solution.py:603
  42.4 3.2 %collective-permute-start.17 = (f32[4,40,128]{2,1,0:T(8,128)S(1)}, f32[4,40,128]{2,1,0:T(8,128)S(1)}, u32[]{:S(2)}, u32[]{:S(2)}) collective-permute-start(f32[4,40,128]{2,1,0:T(8,128)S(1)} %collective-permute-done.13), channel_id=1, source_target_pairs={{0,8},{8,0},{16,24},{24,16},{1,9},{9,1},{17,25},{25,17},{2,10},{10... | collective-permute-start | bytes 245768 | tf_op jit(solution)/shard_map/ppermute | solution.py:603
  45.5 1.3 %collective-permute-start.18 = (f32[4,40,128]{2,1,0:T(8,128)S(1)}, f32[4,40,128]{2,1,0:T(8,128)S(1)}, u32[]{:S(2)}, u32[]{:S(2)}) collective-permute-start(f32[4,40,128]{2,1,0:T(8,128)S(1)} %collective-permute-done.14), channel_id=1, source_target_pairs={{0,8},{8,0},{16,24},{24,16},{1,9},{9,1},{17,25},{25,17},{2,10},{10... | collective-permute-start | bytes 245768 | tf_op jit(solution)/shard_map/ppermute | solution.py:603

commit v5 on v4

--- a/solution.py
+++ b/solution.py
@@ -105,31 +105,32 @@
     return pl.CostEstimate(flops=0, bytes_accessed=int(microseconds * 3.69e6), transcendentals=0)
 
 
-def ask_kernel(gx_count, route, within, xshift, ref, deformed, m0, m1, m2, m3, thick, own, place, count):
+def ask_kernel(gx_count, route, within, xshift, ref, deformed, m0, m1, m2, m3, thick, own, place):
     gx, gy = lax.axis_index("gx"), lax.axis_index("gy")
-    for j in range(5):
-        count[j] = 0
     gx_even, gy_even, half_even = even(gx), even(gy), even(gy // 2)
     row, lane = rows_of((8, 128)), lanes((8, 128))
-
-    def visit(e, found):
-        offset = route[e] - SPAN
-        moved = jnp.clip(gx + xshift[e] - 1, 0, gx_count - 1) - gx
-        ahead = jnp.where(gx_even, 1, 2)
-        bank = jnp.where(moved == 0, 0, jnp.where(moved == 1, ahead, 3 - ahead))
-        code = bank * NEL + (e // EYD) * EYD + within[e]
-        near = jnp.where((offset == 1) == gy_even, 0, 1)
-        far = jnp.where((offset == 2) == half_even, 2, 3)
-        j = jnp.where(offset == 0, 4, jnp.where(jnp.abs(offset) == 1, near, far))
-        slot = count[j]
-        count[j] = slot + 1
-        asked, places = found
-        asked = jnp.where((row == j) & (lane == slot), code.astype(F32), asked)
-        return asked, jnp.where(lane == e, j * 8 + slot, places)
-
-    zero = jnp.zeros((8, 128), jnp.int32)
-    asked, places = lax.fori_loop(0, NEL, visit, (zero.astype(F32), zero), unroll=True)
-    place[...] = places
+    wide = (8, NEL)
+    offset = jnp.broadcast_to(route[...], wide) - SPAN
+    moved = jnp.clip(gx + jnp.broadcast_to(xshift[...], wide) - 1, 0, gx_count - 1) - gx
+    ahead = jnp.where(gx_even, 1, 2)
+    bank = jnp.where(moved == 0, 0, jnp.where(moved == 1, ahead, 3 - ahead))
+    code = bank * NEL + lanes(wide) // EYD * EYD + jnp.broadcast_to(within[...], wide)
+    plus = jnp.where(gy_even, 0, 1)
+    twice = jnp.where(half_even, 2, 3)
+    j = jnp.where(offset == 1, plus, jnp.where(offset == -1, 1 - plus, jnp.where(offset == 2, twice, 5 - twice)))
+    j = jnp.where(offset == 0, 4, j)
+    mine = (rows_of(wide) == j).astype(F32)
+    square = (NEL, NEL)
+    earlier = (rows_of(square) < lanes(square)).astype(F32).astype(BF16)
+    ahead_of = jnp.dot(mine.astype(BF16), earlier, preferred_element_type=F32)
+    slot = jnp.sum(mine * ahead_of, axis=0, keepdims=True)
+    place[...] = jnp.zeros((8, 128), jnp.int32)
+    place[0:1, 0:NEL] = j[0:1] * 8 + slot.astype(jnp.int32)
+    tall = (128, NEL)
+    taken = (rows_of(tall) == jnp.broadcast_to(slot, tall).astype(jnp.int32)).astype(F32).astype(BF16)
+    asked = lax.dot_general(
+        (mine * code.astype(F32)).astype(BF16), taken, (((1,), (1,)), ((), ())), preferred_element_type=F32
+    )
     own[...] = asked
     m2[...] = asked
     m3[...] = asked
@@ -163,9 +164,8 @@
             jax.ShapeDtypeStruct((8, 128), F32),
             jax.ShapeDtypeStruct((8, 128), jnp.int32),
         ),
-        in_specs=[smem] * 3 + [vmem] * 2,
+        in_specs=[vmem] * 5,
         out_specs=(vmem,) * 7,
-        scratch_shapes=[pltpu.SMEM((8,), jnp.int32)],
         cost_estimate=takes(2.0),
         name="ask",
     )(route, within, xshift, ref, deformed)
@@ -184,38 +184,39 @@
 def serve_kernel(lines, *refs):
     count = len(lines)
     asked, outs = refs[3 : 3 + count], refs[3 + count : 3 + 2 * count]
-    banks, tables, last, sem = refs[3 + 2 * count :]
-    copy = pltpu.make_async_copy(asked[-1], last, sem)
+    banks, tables, codes, scalars, sem = refs[3 + 2 * count :]
+    for j in range(count):
+        codes[j] = asked[j][lines[j] // 8 * 8 : lines[j] // 8 * 8 + 8].astype(jnp.int32)
+    copy = pltpu.make_async_copy(codes, scalars, sem)
     copy.start()
-    asked = (*asked[:-1], last)
     for i in range(3):
         banks[i] = refs[i][0:NZ]
+    copy.wait()
     for j in range(count):
         slabs, columns = [], []
-        if j == count - 1:
-            copy.wait()
         for slot in range(8):
-            code = asked[j][lines[j], slot].astype(jnp.int32)
-            slab = banks[code // NEL, pl.ds(lax.rem(code, NEL) // EYD * EDGE, EDGE)]
+            code = scalars[j, lines[j] % 8, slot]
+            start = jnp.bitwise_and(code, NEL - EYD) * (EDGE // EYD)
+            slab = banks[lax.shift_right_logical(code, 5), pl.ds(start, EDGE)]
             slabs.append(slab.reshape(EDGE * EDGE, NY))
-            columns.append(lax.rem(code, EYD))
+            columns.append(jnp.bitwise_and(code, EYD - 1))
         packed = gather_columns(tables.at[j], slabs, columns, range(8))
         outs[j][...] = packed.reshape(EDGE, EDGE, NY).astype(BF16)
 
 
 def serve(own, d0, d1, asked, lines):
-    smem = pl.BlockSpec(memory_space=pltpu.SMEM)
     vmem = pl.BlockSpec(memory_space=pltpu.VMEM)
     count = len(lines)
     return pl.pallas_call(
         functools.partial(serve_kernel, lines),
         out_shape=(jax.ShapeDtypeStruct((EDGE, EDGE, NY), BF16),) * count,
-        in_specs=[vmem] * 3 + [smem] * (count - 1) + [vmem],
+        in_specs=[vmem] * 3 + [vmem] * count,
         out_specs=(vmem,) * count,
         scratch_shapes=[
             pltpu.VMEM((3, NZ, EDGE, NY), BF16),
             pltpu.VMEM((count, 8 * NY, NY), BF16),
-            pltpu.SMEM((8, 128), F32),
+            pltpu.VMEM((count, 8, 128), jnp.int32),
+            pltpu.SMEM((count, 8, 128), jnp.int32),
             pltpu.SemaphoreType.DMA,
         ],
         compiler_params=pltpu.CompilerParams(vmem_limit_bytes=LIMIT),
@@ -330,8 +331,8 @@
     at_y_rim = lax.rem(lane, EDGE) == EDGE - 1
     for ez in range(EZ):
         codes = [spots[0, ez * EYD + b] for b in range(EYD)]
-        found = [bricks[code // 8].reshape(flat) for code in codes]
-        blended = gather_columns(tables.at[ez], found, [lax.rem(code, 8) for code in codes], range(EYD))
+        found = [bricks[lax.shift_right_logical(code, 3)].reshape(flat) for code in codes]
+        blended = gather_columns(tables.at[ez], found, [jnp.bitwise_and(code, 7) for code in codes], range(EYD))
         portion = portions[ez]
         ty, tx, tz = portion[2:3, :], portion[1:2, :], portion[0:1, :]
         shifted = jnp.where(at_y_rim, blended, pltpu.roll(blended, NY - 1, 1))
@@ -426,7 +427,7 @@
             return hess[block_index(steps, relative)]
 
         def store_hess(group, tile, value):
-            coef[tile, pl.ds(row * 4 * HROWS + group * HROWS, HROWS), :] = value
+            coef[tile, pl.ds(group * HROWS * gy_count + row, HROWS, stride=gy_count), :] = value
 
         def load_block(column):
             return load[column * gy_count + row]
@@ -438,7 +439,7 @@
         spread_groups(load_block, 4, gx_count, store_load)
         return 0
 
-    lax.fori_loop(0, gy_count, unpack, 0)
+    lax.fori_loop(0, gy_count, unpack, 0, unroll=8)
     shape = (gy_count, width)
     lane, row = lanes(shape), rows_of(shape)
     in_z, in_y, in_x = lax.rem(lane, NEL) // EYD, lax.rem(lane, EYD), lane // NEL
@@ -484,13 +485,17 @@
         found = [ref[tile, pl.ds(start, gy_count, stride=stride), :] for tile in range(tiles)]
         return found[0] if tiles == 1 else jnp.concatenate(found, axis=1)
 
+    def held(ref, index):
+        found = [ref[tile, index * gy_count : (index + 1) * gy_count, :] for tile in range(tiles)]
+        return found[0] if tiles == 1 else jnp.concatenate(found, axis=1)
+
     def channel(p, wz, wx, wy):
         source = (p * 3 + wz) * 3 + wx
         if source < HROWS:
-            return strided(coef, wy * HROWS + source, 4 * HROWS)
+            return held(coef, wy * HROWS + source)
         spare = wy * 14 + source - HROWS
         if spare < HROWS:
-            return strided(coef, 3 * HROWS + spare, 4 * HROWS)
+            return held(coef, 3 * HROWS + spare)
         return strided(rhs, (spare - HROWS) * 4 + 3, 16)
 
     pair_of = {}
@@ -643,7 +648,7 @@
 
 def body(reference_image, deformed_image, route, within, xshift, fractions):
     m0, m1, m2, m3, thick, own, place = ask(
-        route.reshape(NEL), within.reshape(NEL), xshift.reshape(NEL), reference_image, deformed_image
+        route.reshape(1, NEL), within.reshape(1, NEL), xshift.reshape(1, NEL), reference_image, deformed_image
     )
     asks = (m0, m1, m2, m3)
     q = {kind: swap_y(asks[kind], kind) for kind in KINDS}
@@ -662,7 +667,7 @@
     bricks, known = lax.optimization_barrier((bricks, known))
     mismatch, part = warp(place, bricks, reference_image, grad, portions, extra)
     beside, across = swapped(known, steps[-3]), swapped(known, steps[-2])
-    beside, across, _ = lax.optimization_barrier((beside, across, part))
+    known, beside, across, _ = lax.optimization_barrier((known, beside, across, part))
     load = lax.all_to_all(part, ("gx", "gy"), 0, 0)
     blocks = [known, beside, across, swapped(beside, steps[-2])]
     blocks = blocks + [swapped(block, steps[-1]) for block in blocks]

time: 51.4 us -> 50.2 us (0.977)
  Pallas kernels: 13.1 us -> 11.5 us
  waiting for transfers between devices: 13.4 us -> 14.6 us
  starting transfers between devices: 23.7 us -> 23 us
    ppermute x19, waiting for transfers between devices: 12.4 us -> 13.9 us  [swap(): lax.ppermute(array, axis, [(i, j) for i, j in pairs if 0 <= j < size])]
    pallas_call x1, Pallas kernels: 3.4 us -> 2.56 us  [solve(): pl.pallas_call(functools.partial(solve_kernel, gx_count, gy_count), out_s...]
    pallas_call x1, Pallas kernels: 2.6 us -> 1.89 us  [serve(): pl.pallas_call(functools.partial(serve_kernel, lines), out_shape=(jax.Sha...]
where the time goes in v5:
time: 50.2 us; the launch traced here: 50 us
  starting transfers between devices  23 us (46%)
  waiting for transfers between devices  14.6 us (29%)
  Pallas kernels  11.5 us (23%)
  between operations  0.81 us (2%)
    ppermute x19, starting transfers between devices, swap(): lax.ppermute(array, axis, [(i, j) for i, j in pairs if 0 <= j < size])  19.4 us
    ppermute x19, waiting for transfers between devices, swap(): lax.ppermute(array, axis, [(i, j) for i, j in pairs if 0 <= j < size])  13.9 us
    all_to_all x1, starting transfers between devices, body(): load = lax.all_to_all(part, ('gx', 'gy'), 0, 0)  3.51 us
    pallas_call x1, Pallas kernels, warp(): pl.pallas_call(warp_kernel, out_shape=(jax.ShapeDtypeStruct((NZ, EDGE, NY...  2.92 us
    pallas_call x1, Pallas kernels, solve(): pl.pallas_call(functools.partial(solve_kernel, gx_count, gy_count), out_s...  2.56 us
    pallas_call x1, Pallas kernels, ask(): pl.pallas_call(functools.partial(ask_kernel, lax.axis_size('gx')), out_sh...  2.14 us
    pallas_call x1, Pallas kernels, moments(): pl.pallas_call(functools.partial(moments_kernel, lax.axis_size('gy')), ou...  1.94 us
    pallas_call x1, Pallas kernels, serve(): pl.pallas_call(functools.partial(serve_kernel, lines), out_shape=(jax.Sha...  1.89 us
  transfers between devices with their start and end apart: 20, of which 8 were waited for; matrix products, arithmetic and copies ran while one was open for 0% of the time, Pallas kernels for 14%

profile of v5, /device:TPU:0, one launch (start us, length us, event | category | flops | bytes accessed | tf_op | source)
XLA Modules:
  0.0 50.0 jit_solution(14507442612355983708)
XLA Ops:
  0.6 2.1 %ask.1 = (f32[16,128]{1,0:T(8,128)}, f32[16,128]{1,0:T(8,128)}, f32[8,128]{1,0:T(8,128)}, f32[8,128]{1,0:T(8,128)}, bf16[72,16,128]{2,1,0:T(8,128)(2,1)}, /*index=5*/f32[8,128]{1,0:T(8,128)}, s32[8,128]{1,0:T(8,128)}) custom-call(s32[1,32]{1,0:T(1,128)} %bitcast.8, s32[1,32]{1,0:T(1,128)} %bitcast.9, s32[1,32]{1,0:T(1,128)} %bitcast.10, ...), custom_call_target="tpu_custom_call" | custom-call | bytes 7380000 | tf_op jit(solution)/shard_map/ask/pallas_call | solution.py:156
  2.8 0.5 %collective-permute-start = (bf16[72,16,128]{2,1,0:T(8,128)(2,1)}, bf16[72,16,128]{2,1,0:T(8,128)(2,1)S(1)}, u32[]{:S(2)}, u32[]{:S(2)}) collective-permute-start(bf16[72,16,128]{2,1,0:T(8,128)(2,1)} %get-tuple-element.36), channel_id=1, source_target_pairs={{0,8},{8,0},{16,24},{24,16},{1,9},{9,1},{17,25},{25,17},{2,10},{10... | collective-permute-start | bytes 884744 | tf_op jit(solution)/shard_map/ppermute | solution.py:608
  3.3 0.7 %collective-permute-start.1 = (bf16[72,16,128]{2,1,0:T(8,128)(2,1)}, bf16[72,16,128]{2,1,0:T(8,128)(2,1)S(1)}, u32[]{:S(2)}, u32[]{:S(2)}) collective-permute-start(bf16[72,16,128]{2,1,0:T(8,128)(2,1)} %get-tuple-element.36), channel_id=1, source_target_pairs={{8,16},{16,8},{9,17},{17,9},{10,18},{18,10},{11,19},{19,11},{12,20... | collective-permute-start | bytes 884744 | tf_op jit(solution)/shard_map/ppermute | solution.py:608
  4.0 2.6 %collective-permute-start.3 = (f32[16,128]{1,0:T(8,128)}, f32[16,128]{1,0:T(8,128)S(1)}, u32[]{:S(2)}, u32[]{:S(2)}) collective-permute-start(f32[16,128]{1,0:T(8,128)} %get-tuple-element.38), channel_id=1, source_target_pairs={{0,1},{1,0},{2,3},{3,2},{4,5},{5,4},{6,7},{7,6},{8,9},{9,8},{10,11... | collective-permute-start | bytes 24584 | tf_op jit(solution)/shard_map/ppermute | solution.py:608
  6.5 3.6 %collective-permute-start.4 = (f32[16,128]{1,0:T(8,128)}, f32[16,128]{1,0:T(8,128)S(1)}, u32[]{:S(2)}, u32[]{:S(2)}) collective-permute-start(f32[16,128]{1,0:T(8,128)} %get-tuple-element.39), channel_id=1, source_target_pairs={{0,7},{1,2},{2,1},{3,4},{4,3},{5,6},{6,5},{7,0},{8,15},{9,10},{10,... | collective-permute-start | bytes 24584 | tf_op jit(solution)/shard_map/ppermute | solution.py:608
  10.1 0.4 collective-permute-start.2
  10.6 0.1 copy.9
  10.7 2.4 %collective-permute-done.4.r1.refs_5_ = f32[16,128]{1,0:T(8,128)S(1)} collective-permute-done((f32[16,128]{1,0:T(8,128)}, f32[16,128]{1,0:T(8,128)S(1)}, u32[]{:S(2)}, u32[]{:S(2)}) %collective-permute-start.4) | collective-permute-done | bytes 8224 | tf_op jit(solution)/shard_map/ppermute | solution.py:608
  13.1 0.0 copy-start.1
  13.1 1.9 %moments.1 = (bf16[3,64,16,128]{3,2,1,0:T(8,128)(2,1)S(1)}, f32[40,128]{1,0:T(8,128)S(1)}, f32[8,128]{1,0:T(8,128)S(1)}, f32[4,8,128]{2,1,0:T(8,128)S(1)}) custom-call(f32[16,128]{1,0:T(8,128)S(1)} %collective-permute-done.3.r0.refs_4_, f32[16,128]{1,0:T(8,128)S(1)} %collective-permute-done.4.r1.refs_5_, ...), custom_call_target="tpu_custom_call" | custom-call | bytes 8118000 | tf_op jit(solution)/shard_map/moments/pallas_call | solution.py:304
  15.1 0.7 %collective-permute-done.2.refs_3_ = f32[8,128]{1,0:T(8,128)S(1)} collective-permute-done((f32[8,128]{1,0:T(8,128)}, f32[8,128]{1,0:T(8,128)S(1)}, u32[]{:S(2)}, u32[]{:S(2)}) %collective-permute-start.2) | collective-permute-done | bytes 4128 | tf_op jit(solution)/shard_map/ppermute | solution.py:608
  15.7 0.0 copy-done.2
  15.8 1.9 %serve.1 = (bf16[16,16,128]{2,1,0:T(8,128)(2,1)S(1)}, bf16[16,16,128]{2,1,0:T(8,128)(2,1)S(1)}, bf16[16,16,128]{2,1,0:T(8,128)(2,1)S(1)}, bf16[16,16,128]{2,1,0:T(8,128)(2,1)S(1)}, bf16[16,16,128]{2,1,0:T(8,128)(2,1)S(1)}) custom-call(bf16[64,16,128]{2,1,0:T(8,128)(2,1)S(1)} %copy-done.1, bf16[72,16,128]{2,1,0:T(8,128)(2,1)S(1)} %collective-permute-done.a0.refs_1_, ...), custom_call_target="tpu_custom_call" | custom-call | bytes 7380000 | tf_op jit(solution)/shard_map/serve/pallas_call | solution.py:210
  17.7 1.9 %collective-permute-done.10 = f32[1,40,128]{2,1,0:T(8,128)S(1)} collective-permute-done((f32[1,40,128]{2,1,0:T(8,128)S(1)}, f32[1,40,128]{2,1,0:T(8,128)S(1)}, u32[]{:S(2)}, u32[]{:S(2)}) %collective-permute-start.10) | collective-permute-done | bytes 20512 | tf_op jit(solution)/shard_map/ppermute | solution.py:608
  19.6 0.9 %collective-permute-start.11 = (f32[2,40,128]{2,1,0:T(8,128)S(1)}, f32[2,40,128]{2,1,0:T(8,128)S(1)}, u32[]{:S(2)}, u32[]{:S(2)}) collective-permute-start(f32[2,40,128]{2,1,0:T(8,128)S(1)} %pad_maximum_fusion.1), channel_id=1, source_target_pairs={{0,4},{1,5},{2,6},{3,7},{4,0},{5,1},{6,2},{7,3},{8,12},{9,13},{10,... | collective-permute-start | bytes 122888 | tf_op jit(solution)/shard_map/ppermute | solution.py:608
  20.5 1.7 %collective-permute-start.6 = (bf16[16,16,128]{2,1,0:T(8,128)(2,1)S(1)}, bf16[16,16,128]{2,1,0:T(8,128)(2,1)S(1)}, u32[]{:S(2)}, u32[]{:S(2)}) collective-permute-start(bf16[16,16,128]{2,1,0:T(8,128)(2,1)S(1)} %get-tuple-element.47), channel_id=1, source_target_pairs={{0,6},{1,7},{2,4},{3,5},{4,2},{5,3},{6,0},{7,1},{8,14},{9,15},{10,... | collective-permute-start | bytes 196616 | tf_op jit(solution)/shard_map/ppermute | solution.py:608
  22.1 1.0 %collective-permute-start.7 = (bf16[16,16,128]{2,1,0:T(8,128)(2,1)S(1)}, bf16[16,16,128]{2,1,0:T(8,128)(2,1)S(1)}, u32[]{:S(2)}, u32[]{:S(2)}) collective-permute-start(bf16[16,16,128]{2,1,0:T(8,128)(2,1)S(1)} %get-tuple-element.48), channel_id=1, source_target_pairs={{0,1},{1,0},{2,3},{3,2},{4,5},{5,4},{6,7},{7,6},{8,9},{9,8},{10,11... | collective-permute-start | bytes 196616 | tf_op jit(solution)/shard_map/ppermute | solution.py:608
  23.1 2.6 %collective-permute-start.8 = (bf16[16,16,128]{2,1,0:T(8,128)(2,1)S(1)}, bf16[16,16,128]{2,1,0:T(8,128)(2,1)S(1)}, u32[]{:S(2)}, u32[]{:S(2)}) collective-permute-start(bf16[16,16,128]{2,1,0:T(8,128)(2,1)S(1)} %get-tuple-element.49), channel_id=1, source_target_pairs={{0,7},{1,2},{2,1},{3,4},{4,3},{5,6},{6,5},{7,0},{8,15},{9,10},{10,... | collective-permute-start | bytes 196616 | tf_op jit(solution)/shard_map/ppermute | solution.py:608
  25.7 1.0 %collective-permute-done.11 = f32[2,40,128]{2,1,0:T(8,128)S(1)} collective-permute-done((f32[2,40,128]{2,1,0:T(8,128)S(1)}, f32[2,40,128]{2,1,0:T(8,128)S(1)}, u32[]{:S(2)}, u32[]{:S(2)}) %collective-permute-start.11) | collective-permute-done | bytes 40992 | tf_op jit(solution)/shard_map/ppermute | solution.py:608
  26.8 3.9 %collective-permute-done.8.b2 = bf16[16,16,128]{2,1,0:T(8,128)(2,1)S(1)} collective-permute-done((bf16[16,16,128]{2,1,0:T(8,128)(2,1)S(1)}, bf16[16,16,128]{2,1,0:T(8,128)(2,1)S(1)}, u32[]{:S(2)}, u32[]{:S(2)}) %collective-permute-start.8) | collective-permute-done | bytes 65568 | tf_op jit(solution)/shard_map/ppermute | solution.py:608
  30.7 0.6 %collective-permute-start.12 = (f32[4,40,128]{2,1,0:T(8,128)S(1)}, f32[4,40,128]{2,1,0:T(8,128)S(1)}, u32[]{:S(2)}, u32[]{:S(2)}) collective-permute-start(f32[4,40,128]{2,1,0:T(8,128)S(1)} %pad_maximum_fusion), channel_id=1, source_target_pairs={{0,1},{1,0},{2,3},{3,2},{4,5},{5,4},{6,7},{7,6},{8,9},{9,8},{10,11... | collective-permute-start | bytes 245768 | tf_op jit(solution)/shard_map/ppermute | solution.py:608
  31.3 2.3 %collective-permute-start.13 = (f32[4,40,128]{2,1,0:T(8,128)S(1)}, f32[4,40,128]{2,1,0:T(8,128)S(1)}, u32[]{:S(2)}, u32[]{:S(2)}) collective-permute-start(f32[4,40,128]{2,1,0:T(8,128)S(1)} %pad_maximum_fusion), channel_id=1, source_target_pairs={{0,16},{8,24},{16,0},{24,8},{1,17},{9,25},{17,1},{25,9},{2,18},{10... | collective-permute-start | bytes 245768 | tf_op jit(solution)/shard_map/ppermute | solution.py:608
  33.7 2.9 %warp.1 = (f32[64,16,128]{2,1,0:T(8,128)}, f32[32,4,128]{2,1,0:T(4,128)}) custom-call(bf16[16,16,128]{2,1,0:T(8,128)(2,1)S(1)} %collective-permute-done.6.b0, bf16[16,16,128]{2,1,0:T(8,128)(2,1)S(1)} %collective-permute-done.7.b1, bf16[16,16,128]{2,1,0:T(8,128)(2,1)S(1)} %collective-permute-done.8.b2, bf16[16,16,128]{2,1,0:T(8,128)(2,1)S(1)} %collective-permute-done.9.b3, ...), custom_call_target="tpu_custom_call" | custom-call | bytes 14760000 | tf_op jit(solution)/shard_map/warp/pallas_call | solution.py:387
  36.6 3.5 %all-to-all-start = ((f32[32,4,128]{2,1,0:T(4,128)}), f32[32,4,128]{2,1,0:T(4,128)S(1)}, u32[]{:S(2)}, u32[]{:S(2)}) async-start(f32[32,4,128]{2,1,0:T(4,128)} %get-tuple-element.65), calls=%async_computation | async-start | bytes 131072 | tf_op jit(solution)/shard_map/all_to_all | solution.py:671
  40.2 0.3 collective-permute-start.15
  40.5 1.7 %collective-permute-start.14 = (f32[4,40,128]{2,1,0:T(8,128)S(1)}, f32[4,40,128]{2,1,0:T(8,128)S(1)}, u32[]{:S(2)}, u32[]{:S(2)}) collective-permute-start(f32[4,40,128]{2,1,0:T(8,128)S(1)} %collective-permute-done.12), channel_id=1, source_target_pairs={{0,16},{8,24},{16,0},{24,8},{1,17},{9,25},{17,1},{25,9},{2,18},{10... | collective-permute-start | bytes 245768 | tf_op jit(solution)/shard_map/ppermute | solution.py:608
  42.2 0.1 collective-permute-start.16
  42.3 0.4 collective-permute-start.17
  42.7 2.7 %collective-permute-done.14 = f32[4,40,128]{2,1,0:T(8,128)S(1)} collective-permute-done((f32[4,40,128]{2,1,0:T(8,128)S(1)}, f32[4,40,128]{2,1,0:T(8,128)S(1)}, u32[]{:S(2)}, u32[]{:S(2)}) %collective-permute-start.14) | collective-permute-done | bytes 81952 | tf_op jit(solution)/shard_map/ppermute | solution.py:608
  45.5 1.2 %collective-permute-done.18 = f32[4,40,128]{2,1,0:T(8,128)S(1)} collective-permute-done((f32[4,40,128]{2,1,0:T(8,128)S(1)}, f32[4,40,128]{2,1,0:T(8,128)S(1)}, u32[]{:S(2)}, u32[]{:S(2)}) %collective-permute-start.18) | collective-permute-done | bytes 81952 | tf_op jit(solution)/shard_map/ppermute | solution.py:608
  46.7 0.7 %all-to-all-done.load = f32[32,4,128]{2,1,0:T(4,128)S(1)} async-done(((f32[32,4,128]{2,1,0:T(4,128)}), f32[32,4,128]{2,1,0:T(4,128)S(1)}, u32[]{:S(2)}, u32[]{:S(2)}) %all-to-all-start) | async-done | bytes 65568 | tf_op jit(solution)/shard_map/all_to_all | solution.py:671
  47.4 2.6 %solve.1 = f32[3,5,1,8]{3,2,1,0:T(1,128)} custom-call(f32[32,40,128]{2,1,0:T(8,128)S(1)} %constant_dynamic-update-slice_fusion.hess, f32[32,4,128]{2,1,0:T(4,128)S(1)} %all-to-all-done.load), custom_call_target="tpu_custom_call" | custom-call | bytes 12915000 | tf_op jit(solution)/shard_map/solve/pallas_call | solution.py:590
  (36 shorter events, 0.1 us)
Async XLA Ops:
  0.6 12.5 %copy-start = (bf16[64,16,128]{2,1,0:T(8,128)(2,1)S(1)}, bf16[64,16,128]{2,1,0:T(8,128)(2,1)}, u32[]{:S(2)}) copy-start(bf16[64,16,128]{2,1,0:T(8,128)(2,1)} %ref.5) | copy-start | bytes 786436
  2.8 7.8 %copy-start.5 = (f32[8,128]{1,0:T(8,128)S(1)}, f32[8,128]{1,0:T(8,128)}, u32[]{:S(2)}) copy-start(f32[8,128]{1,0:T(8,128)} %get-tuple-element.40) | copy-start | bytes 12292
  2.8 10.3 %collective-permute-start = (bf16[72,16,128]{2,1,0:T(8,128)(2,1)}, bf16[72,16,128]{2,1,0:T(8,128)(2,1)S(1)}, u32[]{:S(2)}, u32[]{:S(2)}) collective-permute-start(bf16[72,16,128]{2,1,0:T(8,128)(2,1)} %get-tuple-element.36), channel_id=1, source_target_pairs={{0,8},{8,0},{16,24},{24,16},{1,9},{9,1},{17,25},{25,17},{2,10},{10... | collective-permute-start | bytes 884744 | tf_op jit(solution)/shard_map/ppermute | solution.py:608
  3.3 9.8 %collective-permute-start.1 = (bf16[72,16,128]{2,1,0:T(8,128)(2,1)}, bf16[72,16,128]{2,1,0:T(8,128)(2,1)S(1)}, u32[]{:S(2)}, u32[]{:S(2)}) collective-permute-start(bf16[72,16,128]{2,1,0:T(8,128)(2,1)} %get-tuple-element.36), channel_id=1, source_target_pairs={{8,16},{16,8},{9,17},{17,9},{10,18},{18,10},{11,19},{19,11},{12,20... | collective-permute-start | bytes 884744 | tf_op jit(solution)/shard_map/ppermute | solution.py:608
  4.0 6.6 %collective-permute-start.3 = (f32[16,128]{1,0:T(8,128)}, f32[16,128]{1,0:T(8,128)S(1)}, u32[]{:S(2)}, u32[]{:S(2)}) collective-permute-start(f32[16,128]{1,0:T(8,128)} %get-tuple-element.38), channel_id=1, source_target_pairs={{0,1},{1,0},{2,3},{3,2},{4,5},{5,4},{6,7},{7,6},{8,9},{9,8},{10,11... | collective-permute-start | bytes 24584 | tf_op jit(solution)/shard_map/ppermute | solution.py:608
  6.5 4.0 %copy-start.4 = (s32[1,1,32,3]{2,1,3,0:T(1,128)S(1)}, s32[1,1,32,3]{2,1,3,0:T(1,128)}, u32[]{:S(2)}) copy-start(s32[1,1,32,3]{2,1,3,0:T(1,128)} %param.11) | copy-start | bytes 1156
  6.5 6.6 %collective-permute-start.4 = (f32[16,128]{1,0:T(8,128)}, f32[16,128]{1,0:T(8,128)S(1)}, u32[]{:S(2)}, u32[]{:S(2)}) collective-permute-start(f32[16,128]{1,0:T(8,128)} %get-tuple-element.39), channel_id=1, source_target_pairs={{0,7},{1,2},{2,1},{3,4},{4,3},{5,6},{6,5},{7,0},{8,15},{9,10},{10,... | collective-permute-start | bytes 24584 | tf_op jit(solution)/shard_map/ppermute | solution.py:608
  10.1 5.6 %collective-permute-start.2 = (f32[8,128]{1,0:T(8,128)}, f32[8,128]{1,0:T(8,128)S(1)}, u32[]{:S(2)}, u32[]{:S(2)}) collective-permute-start(f32[8,128]{1,0:T(8,128)} %get-tuple-element.37), channel_id=1, source_target_pairs={{0,6},{1,7},{2,4},{3,5},{4,2},{5,3},{6,0},{7,1},{8,14},{9,15},{10,... | collective-permute-start | bytes 12296 | tf_op jit(solution)/shard_map/ppermute | solution.py:608
  10.6 5.2 %collective-permute-start.5 = (f32[8,128]{1,0:T(8,128)S(1)}, f32[8,128]{1,0:T(8,128)S(1)}, u32[]{:S(2)}, u32[]{:S(2)}) collective-permute-start(f32[8,128]{1,0:T(8,128)S(1)} %copy-done.5), channel_id=1, source_target_pairs={{0,2},{1,3},{2,0},{3,1},{4,6},{5,7},{6,4},{7,5},{8,10},{9,11},{10,... | collective-permute-start | bytes 12296 | tf_op jit(solution)/shard_map/ppermute | solution.py:608
  13.1 2.6 %copy-start.1 = (bf16[64,16,128]{2,1,0:T(8,128)(2,1)S(1)}, bf16[64,16,128]{2,1,0:T(8,128)(2,1)}, u32[]{:S(2)}) copy-start(bf16[64,16,128]{2,1,0:T(8,128)(2,1)} %refs_0_.1) | copy-start | bytes 786436
  15.1 0.7 %copy-start.2 = (f32[8,128]{1,0:T(8,128)S(1)}, f32[8,128]{1,0:T(8,128)}, u32[]{:S(2)}) copy-start(f32[8,128]{1,0:T(8,128)} %get-tuple-element.46.refs_7_) | copy-start | bytes 12292
  15.7 3.8 %collective-permute-start.10 = (f32[1,40,128]{2,1,0:T(8,128)S(1)}, f32[1,40,128]{2,1,0:T(8,128)S(1)}, u32[]{:S(2)}, u32[]{:S(2)}) collective-permute-start(f32[1,40,128]{2,1,0:T(8,128)S(1)} %bitcast.6), channel_id=1, source_target_pairs={{0,2},{1,3},{2,0},{3,1},{4,6},{5,7},{6,4},{7,5},{8,10},{9,11},{10,... | collective-permute-start | bytes 61448 | tf_op jit(solution)/shard_map/ppermute | solution.py:608
  19.6 7.2 %collective-permute-start.11 = (f32[2,40,128]{2,1,0:T(8,128)S(1)}, f32[2,40,128]{2,1,0:T(8,128)S(1)}, u32[]{:S(2)}, u32[]{:S(2)}) collective-permute-start(f32[2,40,128]{2,1,0:T(8,128)S(1)} %pad_maximum_fusion.1), channel_id=1, source_target_pairs={{0,4},{1,5},{2,6},{3,7},{4,0},{5,1},{6,2},{7,3},{8,12},{9,13},{10,... | collective-permute-start | bytes 122888 | tf_op jit(solution)/shard_map/ppermute | solution.py:608
  20.5 6.3 %collective-permute-start.6 = (bf16[16,16,128]{2,1,0:T(8,128)(2,1)S(1)}, bf16[16,16,128]{2,1,0:T(8,128)(2,1)S(1)}, u32[]{:S(2)}, u32[]{:S(2)}) collective-permute-start(bf16[16,16,128]{2,1,0:T(8,128)(2,1)S(1)} %get-tuple-element.47), channel_id=1, source_target_pairs={{0,6},{1,7},{2,4},{3,5},{4,2},{5,3},{6,0},{7,1},{8,14},{9,15},{10,... | collective-permute-start | bytes 196616 | tf_op jit(solution)/shard_map/ppermute | solution.py:608
  22.1 4.7 %collective-permute-start.7 = (bf16[16,16,128]{2,1,0:T(8,128)(2,1)S(1)}, bf16[16,16,128]{2,1,0:T(8,128)(2,1)S(1)}, u32[]{:S(2)}, u32[]{:S(2)}) collective-permute-start(bf16[16,16,128]{2,1,0:T(8,128)(2,1)S(1)} %get-tuple-element.48), channel_id=1, source_target_pairs={{0,1},{1,0},{2,3},{3,2},{4,5},{5,4},{6,7},{7,6},{8,9},{9,8},{10,11... | collective-permute-start | bytes 196616 | tf_op jit(solution)/shard_map/ppermute | solution.py:608
  23.1 7.6 %collective-permute-start.8 = (bf16[16,16,128]{2,1,0:T(8,128)(2,1)S(1)}, bf16[16,16,128]{2,1,0:T(8,128)(2,1)S(1)}, u32[]{:S(2)}, u32[]{:S(2)}) collective-permute-start(bf16[16,16,128]{2,1,0:T(8,128)(2,1)S(1)} %get-tuple-element.49), channel_id=1, source_target_pairs={{0,7},{1,2},{2,1},{3,4},{4,3},{5,6},{6,5},{7,0},{8,15},{9,10},{10,... | collective-permute-start | bytes 196616 | tf_op jit(solution)/shard_map/ppermute | solution.py:608
  25.7 5.0 %collective-permute-start.9 = (bf16[16,16,128]{2,1,0:T(8,128)(2,1)S(1)}, bf16[16,16,128]{2,1,0:T(8,128)(2,1)S(1)}, u32[]{:S(2)}, u32[]{:S(2)}) collective-permute-start(bf16[16,16,128]{2,1,0:T(8,128)(2,1)S(1)} %get-tuple-element.50), channel_id=1, source_target_pairs={{0,2},{1,3},{2,0},{3,1},{4,6},{5,7},{6,4},{7,5},{8,10},{9,11},{10,... | collective-permute-start | bytes 196616 | tf_op jit(solution)/shard_map/ppermute | solution.py:608
  26.8 6.9 %copy-start.3 = (s32[8,128]{1,0:T(8,128)S(1)}, s32[8,128]{1,0:T(8,128)}, u32[]{:S(2)}) copy-start(s32[8,128]{1,0:T(8,128)} %get-tuple-element.61.place) | copy-start | bytes 12292
  30.7 9.4 %collective-permute-start.12 = (f32[4,40,128]{2,1,0:T(8,128)S(1)}, f32[4,40,128]{2,1,0:T(8,128)S(1)}, u32[]{:S(2)}, u32[]{:S(2)}) collective-permute-start(f32[4,40,128]{2,1,0:T(8,128)S(1)} %pad_maximum_fusion), channel_id=1, source_target_pairs={{0,1},{1,0},{2,3},{3,2},{4,5},{5,4},{6,7},{7,6},{8,9},{9,8},{10,11... | collective-permute-start | bytes 245768 | tf_op jit(solution)/shard_map/ppermute | solution.py:608
  31.3 8.8 %collective-permute-start.13 = (f32[4,40,128]{2,1,0:T(8,128)S(1)}, f32[4,40,128]{2,1,0:T(8,128)S(1)}, u32[]{:S(2)}, u32[]{:S(2)}) collective-permute-start(f32[4,40,128]{2,1,0:T(8,128)S(1)} %pad_maximum_fusion), channel_id=1, source_target_pairs={{0,16},{8,24},{16,0},{24,8},{1,17},{9,25},{17,1},{25,9},{2,18},{10... | collective-permute-start | bytes 245768 | tf_op jit(solution)/shard_map/ppermute | solution.py:608
  36.6 10.8 %all-to-all-start = ((f32[32,4,128]{2,1,0:T(4,128)}), f32[32,4,128]{2,1,0:T(4,128)S(1)}, u32[]{:S(2)}, u32[]{:S(2)}) async-start(f32[32,4,128]{2,1,0:T(4,128)} %get-tuple-element.65), calls=%async_computation | async-start | bytes 131072 | tf_op jit(solution)/shard_map/all_to_all | solution.py:671
  40.2 5.3 %collective-permute-start.15 = (f32[4,40,128]{2,1,0:T(8,128)S(1)}, f32[4,40,128]{2,1,0:T(8,128)S(1)}, u32[]{:S(2)}, u32[]{:S(2)}) collective-permute-start(f32[4,40,128]{2,1,0:T(8,128)S(1)} %pad_maximum_fusion), channel_id=1, source_target_pairs={{0,8},{8,0},{16,24},{24,16},{1,9},{9,1},{17,25},{25,17},{2,10},{10... | collective-permute-start | bytes 245768 | tf_op jit(solution)/shard_map/ppermute | solution.py:608
  40.5 4.9 %collective-permute-start.14 = (f32[4,40,128]{2,1,0:T(8,128)S(1)}, f32[4,40,128]{2,1,0:T(8,128)S(1)}, u32[]{:S(2)}, u32[]{:S(2)}) collective-permute-start(f32[4,40,128]{2,1,0:T(8,128)S(1)} %collective-permute-done.12), channel_id=1, source_target_pairs={{0,16},{8,24},{16,0},{24,8},{1,17},{9,25},{17,1},{25,9},{2,18},{10... | collective-permute-start | bytes 245768 | tf_op jit(solution)/shard_map/ppermute | solution.py:608
  42.2 3.3 %collective-permute-start.16 = (f32[4,40,128]{2,1,0:T(8,128)S(1)}, f32[4,40,128]{2,1,0:T(8,128)S(1)}, u32[]{:S(2)}, u32[]{:S(2)}) collective-permute-start(f32[4,40,128]{2,1,0:T(8,128)S(1)} %collective-permute-done.12), channel_id=1, source_target_pairs={{0,8},{8,0},{16,24},{24,16},{1,9},{9,1},{17,25},{25,17},{2,10},{10... | collective-permute-start | bytes 245768 | tf_op jit(solution)/shard_map/ppermute | solution.py:608
  42.3 3.3 %collective-permute-start.17 = (f32[4,40,128]{2,1,0:T(8,128)S(1)}, f32[4,40,128]{2,1,0:T(8,128)S(1)}, u32[]{:S(2)}, u32[]{:S(2)}) collective-permute-start(f32[4,40,128]{2,1,0:T(8,128)S(1)} %collective-permute-done.13), channel_id=1, source_target_pairs={{0,8},{8,0},{16,24},{24,16},{1,9},{9,1},{17,25},{25,17},{2,10},{10... | collective-permute-start | bytes 245768 | tf_op jit(solution)/shard_map/ppermute | solution.py:608
  45.4 1.3 %collective-permute-start.18 = (f32[4,40,128]{2,1,0:T(8,128)S(1)}, f32[4,40,128]{2,1,0:T(8,128)S(1)}, u32[]{:S(2)}, u32[]{:S(2)}) collective-permute-start(f32[4,40,128]{2,1,0:T(8,128)S(1)} %collective-permute-done.14), channel_id=1, source_target_pairs={{0,8},{8,0},{16,24},{24,16},{1,9},{9,1},{17,25},{25,17},{2,10},{10... | collective-permute-start | bytes 245768 | tf_op jit(solution)/shard_map/ppermute | solution.py:608

commit v6 on v5

--- a/solution.py
+++ b/solution.py
@@ -124,8 +124,14 @@
     earlier = (rows_of(square) < lanes(square)).astype(F32).astype(BF16)
     ahead_of = jnp.dot(mine.astype(BF16), earlier, preferred_element_type=F32)
     slot = jnp.sum(mine * ahead_of, axis=0, keepdims=True)
-    place[...] = jnp.zeros((8, 128), jnp.int32)
-    place[0:1, 0:NEL] = j[0:1] * 8 + slot.astype(jnp.int32)
+    order = jnp.full(wide, 4, jnp.int32)
+    for at, kind in enumerate(KINDS):
+        order = jnp.where(j == kind, at, order)
+    found = jnp.where(rows_of(wide) == lanes(wide) // EYD, order.astype(F32) * 8.0 + slot, 0.0)
+    long = (NEL, 128)
+    widen = (lax.rem(rows_of(long), EYD) == lanes(long) // EDGE).astype(F32).astype(BF16)
+    found = jnp.dot(found.astype(BF16), widen, preferred_element_type=F32)
+    place[...] = found.astype(jnp.int32) * EDGE + lax.rem(lane, EDGE)
     tall = (128, NEL)
     taken = (rows_of(tall) == jnp.broadcast_to(slot, tall).astype(jnp.int32)).astype(F32).astype(BF16)
     asked = lax.dot_general(
@@ -318,21 +324,21 @@
     )(faces_y[0], faces_y[1], faces_x[1], faces_x[0], ref, fractions)
 
 
-def warp_kernel(b0, b1, b2, b3, b4, place, ref, grad, portions, extra, mismatch, packed, bricks, tables, slabs, spots, sem):
+def warp_kernel(b0, b1, b2, b3, b4, place, ref, grad, portions, extra, mismatch, packed, slabs):
     gx = lax.axis_index("gx")
-    copy = pltpu.make_async_copy(place, spots, sem)
-    copy.start()
-    for i, source in zip((*KINDS, 4), (b0, b1, b2, b3, b4)):
-        bricks[i] = source[...]
-    copy.wait()
     flat = (EDGE * EDGE, NY)
     lane = lanes(flat)
     at_x_rim = lax.rem(lax.broadcasted_iota(jnp.int32, flat, 0), EDGE) == EDGE - 1
     at_y_rim = lax.rem(lane, EDGE) == EDGE - 1
+    came = jnp.concatenate([block[...].reshape(flat) for block in (b0, b1, b2, b3, b4)], axis=1)
+    table = (5 * NY, NY)
+    fetched = []
+    for half in range(2):
+        spots = [jnp.broadcast_to(place[ez : ez + 1, :], table) for ez in (2 * half, 2 * half + 1)]
+        moves = [(rows_of(table) == spot).astype(F32).astype(BF16) for spot in spots]
+        fetched.append(jnp.dot(came, jnp.concatenate(moves, axis=1), preferred_element_type=F32))
     for ez in range(EZ):
-        codes = [spots[0, ez * EYD + b] for b in range(EYD)]
-        found = [bricks[lax.shift_right_logical(code, 3)].reshape(flat) for code in codes]
-        blended = gather_columns(tables.at[ez], found, [jnp.bitwise_and(code, 7) for code in codes], range(EYD))
+        blended = fetched[ez // 2][:, ez % 2 * NY : (ez % 2 + 1) * NY]
         portion = portions[ez]
         ty, tx, tz = portion[2:3, :], portion[1:2, :], portion[0:1, :]
         shifted = jnp.where(at_y_rim, blended, pltpu.roll(blended, NY - 1, 1))
@@ -390,11 +396,7 @@
         in_specs=[vmem] * 10,
         out_specs=(vmem, vmem),
         scratch_shapes=[
-            pltpu.VMEM((5, EDGE, EDGE, NY), BF16),
-            pltpu.VMEM((EZ, EYD * NY, NY), BF16),
             pltpu.VMEM((EZ * 6 * EDGE, NY), F32),
-            pltpu.SMEM((8, 128), jnp.int32),
-            pltpu.SemaphoreType.DMA,
         ],
         compiler_params=pltpu.CompilerParams(vmem_limit_bytes=LIMIT),
         cost_estimate=takes(4.0),
@@ -448,38 +450,48 @@
     last_y, first_y = in_y == EYD - 1, in_y == 0
     end_y, begin_y = last_y & (row == gy_count - 1), first_y & (row == 0)
 
+    bits = [(a, b, d) for a in range(2) for b in range(2) for d in range(2)]
+
     def turn(value, by, axis):
         size = shape[axis]
         by = by % size
         return pltpu.roll(value, by, axis) if by else value
 
     def corners(main, top):
+        main_next, top_next = turn(main, -1, 0), turn(top, -1, 0)
         found = []
-        for a in range(2):
-            z_part = main if a == 0 else jnp.where(last_z, top, turn(main, -EYD, 1))
-            for b in range(2):
-                x_part = z_part if b == 0 else jnp.where(last_x, 0.0, turn(z_part, -NEL, 1))
-                for d in range(2):
-                    if d == 0:
-                        found.append(x_part)
-                    else:
-                        wrapped = turn(turn(x_part, -1, 0), EYD - 1, 1)
-                        moved = jnp.where(last_y, wrapped, turn(x_part, -1, 1))
-                        found.append(jnp.where(end_y, 0.0, moved))
+        for a, b, d in bits:
+
+            def reached(main, top, by):
+                value = turn(main, -(EYD * a + NEL * b + by), 1)
+                return jnp.where(last_z, turn(top, -(NEL * b + by), 1), value) if a else value
+
+            value = reached(main, top, d)
+            if d:
+                wrapped = jnp.where(end_y, 0.0, reached(main_next, top_next, 1 - EYD))
+                value = jnp.where(last_y, wrapped, value)
+            found.append(jnp.where(last_x, 0.0, value) if b else value)
         return found
 
     def settle(parts):
-        z_parts = []
-        for a in range(2):
-            x_parts = []
-            for b in range(2):
-                base, extra = parts[a * 4 + b * 2], parts[a * 4 + b * 2 + 1]
-                wrapped = turn(turn(extra, 1, 0), 1 - EYD, 1)
-                moved = jnp.where(first_y, wrapped, turn(extra, 1, 1))
-                x_parts.append(base + jnp.where(begin_y, 0.0, moved))
-            z_parts.append(x_parts[0] + jnp.where(first_x, 0.0, turn(x_parts[1], NEL, 1)))
-        main = z_parts[0] + jnp.where(first_z, 0.0, turn(z_parts[1], EYD, 1))
-        return main, jnp.where(last_z, z_parts[1], 0.0)
+        main, top = None, None
+        for (a, b, d), part in zip(bits, parts):
+            before = turn(part, 1, 0) if d else None
+
+            def given(by):
+                value = turn(part, by + d, 1)
+                if d:
+                    wrapped = jnp.where(begin_y, 0.0, turn(before, by + 1 - EYD, 1))
+                    value = jnp.where(first_y, wrapped, value)
+                return jnp.where(first_x, 0.0, value) if b else value
+
+            value = given(EYD * a + NEL * b)
+            value = jnp.where(first_z, 0.0, value) if a else value
+            main = value if main is None else main + value
+            if a:
+                value = given(NEL * b)
+                top = value if top is None else top + value
+        return main, jnp.where(last_z, top, 0.0)
 
     def strided(ref, start, stride):
         found = [ref[tile, pl.ds(start, gy_count, stride=stride), :] for tile in range(tiles)]
@@ -501,7 +513,6 @@
     pair_of = {}
     for p, (c, d) in enumerate(PAIRS):
         pair_of[c, d] = pair_of[d, c] = p
-    bits = [(a, b, d) for a in range(2) for b in range(2) for d in range(2)]
 
     def curved_by(vector):
         known = [corners(main, top) for main, top in vector]

time: 50.2 us -> 49.1 us (0.978)
  Pallas kernels: 11.5 us -> 10.4 us
    pallas_call x1, Pallas kernels: 2.92 us -> 2.09 us  [warp(): pl.pallas_call(warp_kernel, out_shape=(jax.ShapeDtypeStruct((NZ, EDGE, NY...]
  transfers between devices with their start and end apart: 20 -> 20, of which waited for: 8 -> 8; matrix products, arithmetic and copies ran while one was open for 0% -> 0% of each run, Pallas kernels for 14% -> 12%
where the time goes in v6:
time: 49.1 us; the launch traced here: 48.9 us
  starting transfers between devices  22.9 us (47%)
  waiting for transfers between devices  14.6 us (30%)
  Pallas kernels  10.4 us (21%)
  between operations  0.8 us (2%)
    ppermute x19, starting transfers between devices, swap(): lax.ppermute(array, axis, [(i, j) for i, j in pairs if 0 <= j < size])  19.4 us
    ppermute x19, waiting for transfers between devices, swap(): lax.ppermute(array, axis, [(i, j) for i, j in pairs if 0 <= j < size])  13.9 us
    all_to_all x1, starting transfers between devices, body(): load = lax.all_to_all(part, ('gx', 'gy'), 0, 0)  3.51 us
    pallas_call x1, Pallas kernels, solve(): pl.pallas_call(functools.partial(solve_kernel, gx_count, gy_count), out_s...  2.33 us
    pallas_call x1, Pallas kernels, ask(): pl.pallas_call(functools.partial(ask_kernel, lax.axis_size('gx')), out_sh...  2.14 us
    pallas_call x1, Pallas kernels, warp(): pl.pallas_call(warp_kernel, out_shape=(jax.ShapeDtypeStruct((NZ, EDGE, NY...  2.09 us
    pallas_call x1, Pallas kernels, moments(): pl.pallas_call(functools.partial(moments_kernel, lax.axis_size('gy')), ou...  1.94 us
    pallas_call x1, Pallas kernels, serve(): pl.pallas_call(functools.partial(serve_kernel, lines), out_shape=(jax.Sha...  1.9 us
  transfers between devices with their start and end apart: 20, of which 8 were waited for; matrix products, arithmetic and copies ran while one was open for 0% of the time, Pallas kernels for 12%

profile of v6, /device:TPU:0, one launch (start us, length us, event | category | flops | bytes accessed | tf_op | source)
XLA Modules:
  0.0 48.9 jit_solution(9345215402300345395)
XLA Ops:
  0.6 2.1 %ask.1 = (f32[16,128]{1,0:T(8,128)}, f32[16,128]{1,0:T(8,128)}, f32[8,128]{1,0:T(8,128)}, f32[8,128]{1,0:T(8,128)}, bf16[72,16,128]{2,1,0:T(8,128)(2,1)}, /*index=5*/f32[8,128]{1,0:T(8,128)}, s32[8,128]{1,0:T(8,128)}) custom-call(s32[1,32]{1,0:T(1,128)} %bitcast.8, s32[1,32]{1,0:T(1,128)} %bitcast.9, s32[1,32]{1,0:T(1,128)} %bitcast.10, ...), custom_call_target="tpu_custom_call" | custom-call | bytes 7380000 | tf_op jit(solution)/shard_map/ask/pallas_call | solution.py:162
  2.8 0.5 %collective-permute-start = (bf16[72,16,128]{2,1,0:T(8,128)(2,1)}, bf16[72,16,128]{2,1,0:T(8,128)(2,1)S(1)}, u32[]{:S(2)}, u32[]{:S(2)}) collective-permute-start(bf16[72,16,128]{2,1,0:T(8,128)(2,1)} %get-tuple-element.36), channel_id=1, source_target_pairs={{0,8},{8,0},{16,24},{24,16},{1,9},{9,1},{17,25},{25,17},{2,10},{10... | collective-permute-start | bytes 884744 | tf_op jit(solution)/shard_map/ppermute | solution.py:619
  3.3 0.7 %collective-permute-start.1 = (bf16[72,16,128]{2,1,0:T(8,128)(2,1)}, bf16[72,16,128]{2,1,0:T(8,128)(2,1)S(1)}, u32[]{:S(2)}, u32[]{:S(2)}) collective-permute-start(bf16[72,16,128]{2,1,0:T(8,128)(2,1)} %get-tuple-element.36), channel_id=1, source_target_pairs={{8,16},{16,8},{9,17},{17,9},{10,18},{18,10},{11,19},{19,11},{12,20... | collective-permute-start | bytes 884744 | tf_op jit(solution)/shard_map/ppermute | solution.py:619
  4.0 2.6 %collective-permute-start.3 = (f32[16,128]{1,0:T(8,128)}, f32[16,128]{1,0:T(8,128)S(1)}, u32[]{:S(2)}, u32[]{:S(2)}) collective-permute-start(f32[16,128]{1,0:T(8,128)} %get-tuple-element.38), channel_id=1, source_target_pairs={{0,1},{1,0},{2,3},{3,2},{4,5},{5,4},{6,7},{7,6},{8,9},{9,8},{10,11... | collective-permute-start | bytes 24584 | tf_op jit(solution)/shard_map/ppermute | solution.py:619
  6.5 3.6 %collective-permute-start.4 = (f32[16,128]{1,0:T(8,128)}, f32[16,128]{1,0:T(8,128)S(1)}, u32[]{:S(2)}, u32[]{:S(2)}) collective-permute-start(f32[16,128]{1,0:T(8,128)} %get-tuple-element.39), channel_id=1, source_target_pairs={{0,7},{1,2},{2,1},{3,4},{4,3},{5,6},{6,5},{7,0},{8,15},{9,10},{10,... | collective-permute-start | bytes 24584 | tf_op jit(solution)/shard_map/ppermute | solution.py:619
  10.1 0.4 collective-permute-start.2
  10.6 0.1 copy.9
  10.7 2.4 %collective-permute-done.4.r1.refs_5_ = f32[16,128]{1,0:T(8,128)S(1)} collective-permute-done((f32[16,128]{1,0:T(8,128)}, f32[16,128]{1,0:T(8,128)S(1)}, u32[]{:S(2)}, u32[]{:S(2)}) %collective-permute-start.4) | collective-permute-done | bytes 8224 | tf_op jit(solution)/shard_map/ppermute | solution.py:619
  13.1 0.0 copy-start.1
  13.1 1.9 %moments.1 = (bf16[3,64,16,128]{3,2,1,0:T(8,128)(2,1)S(1)}, f32[40,128]{1,0:T(8,128)S(1)}, f32[8,128]{1,0:T(8,128)S(1)}, f32[4,8,128]{2,1,0:T(8,128)S(1)}) custom-call(f32[16,128]{1,0:T(8,128)S(1)} %collective-permute-done.3.r0.refs_4_, f32[16,128]{1,0:T(8,128)S(1)} %collective-permute-done.4.r1.refs_5_, ...), custom_call_target="tpu_custom_call" | custom-call | bytes 8118000 | tf_op jit(solution)/shard_map/moments/pallas_call | solution.py:310
  15.1 0.7 %collective-permute-done.2.refs_3_ = f32[8,128]{1,0:T(8,128)S(1)} collective-permute-done((f32[8,128]{1,0:T(8,128)}, f32[8,128]{1,0:T(8,128)S(1)}, u32[]{:S(2)}, u32[]{:S(2)}) %collective-permute-start.2) | collective-permute-done | bytes 4128 | tf_op jit(solution)/shard_map/ppermute | solution.py:619
  15.7 0.0 copy-done.2
  15.8 1.9 %serve.1 = (bf16[16,16,128]{2,1,0:T(8,128)(2,1)S(1)}, bf16[16,16,128]{2,1,0:T(8,128)(2,1)S(1)}, bf16[16,16,128]{2,1,0:T(8,128)(2,1)S(1)}, bf16[16,16,128]{2,1,0:T(8,128)(2,1)S(1)}, bf16[16,16,128]{2,1,0:T(8,128)(2,1)S(1)}) custom-call(bf16[64,16,128]{2,1,0:T(8,128)(2,1)S(1)} %copy-done.1, bf16[72,16,128]{2,1,0:T(8,128)(2,1)S(1)} %collective-permute-done.a0.refs_1_, ...), custom_call_target="tpu_custom_call" | custom-call | bytes 7380000 | tf_op jit(solution)/shard_map/serve/pallas_call | solution.py:216
  17.7 1.9 %collective-permute-done.10 = f32[1,40,128]{2,1,0:T(8,128)S(1)} collective-permute-done((f32[1,40,128]{2,1,0:T(8,128)S(1)}, f32[1,40,128]{2,1,0:T(8,128)S(1)}, u32[]{:S(2)}, u32[]{:S(2)}) %collective-permute-start.10) | collective-permute-done | bytes 20512 | tf_op jit(solution)/shard_map/ppermute | solution.py:619
  19.6 0.9 %collective-permute-start.11 = (f32[2,40,128]{2,1,0:T(8,128)S(1)}, f32[2,40,128]{2,1,0:T(8,128)S(1)}, u32[]{:S(2)}, u32[]{:S(2)}) collective-permute-start(f32[2,40,128]{2,1,0:T(8,128)S(1)} %pad_maximum_fusion.1), channel_id=1, source_target_pairs={{0,4},{1,5},{2,6},{3,7},{4,0},{5,1},{6,2},{7,3},{8,12},{9,13},{10,... | collective-permute-start | bytes 122888 | tf_op jit(solution)/shard_map/ppermute | solution.py:619
  20.5 1.7 %collective-permute-start.6 = (bf16[16,16,128]{2,1,0:T(8,128)(2,1)S(1)}, bf16[16,16,128]{2,1,0:T(8,128)(2,1)S(1)}, u32[]{:S(2)}, u32[]{:S(2)}) collective-permute-start(bf16[16,16,128]{2,1,0:T(8,128)(2,1)S(1)} %get-tuple-element.47), channel_id=1, source_target_pairs={{0,6},{1,7},{2,4},{3,5},{4,2},{5,3},{6,0},{7,1},{8,14},{9,15},{10,... | collective-permute-start | bytes 196616 | tf_op jit(solution)/shard_map/ppermute | solution.py:619
  22.1 1.0 %collective-permute-start.7 = (bf16[16,16,128]{2,1,0:T(8,128)(2,1)S(1)}, bf16[16,16,128]{2,1,0:T(8,128)(2,1)S(1)}, u32[]{:S(2)}, u32[]{:S(2)}) collective-permute-start(bf16[16,16,128]{2,1,0:T(8,128)(2,1)S(1)} %get-tuple-element.48), channel_id=1, source_target_pairs={{0,1},{1,0},{2,3},{3,2},{4,5},{5,4},{6,7},{7,6},{8,9},{9,8},{10,11... | collective-permute-start | bytes 196616 | tf_op jit(solution)/shard_map/ppermute | solution.py:619
  23.1 2.6 %collective-permute-start.8 = (bf16[16,16,128]{2,1,0:T(8,128)(2,1)S(1)}, bf16[16,16,128]{2,1,0:T(8,128)(2,1)S(1)}, u32[]{:S(2)}, u32[]{:S(2)}) collective-permute-start(bf16[16,16,128]{2,1,0:T(8,128)(2,1)S(1)} %get-tuple-element.49), channel_id=1, source_target_pairs={{0,7},{1,2},{2,1},{3,4},{4,3},{5,6},{6,5},{7,0},{8,15},{9,10},{10,... | collective-permute-start | bytes 196616 | tf_op jit(solution)/shard_map/ppermute | solution.py:619
  25.7 1.0 %collective-permute-done.11 = f32[2,40,128]{2,1,0:T(8,128)S(1)} collective-permute-done((f32[2,40,128]{2,1,0:T(8,128)S(1)}, f32[2,40,128]{2,1,0:T(8,128)S(1)}, u32[]{:S(2)}, u32[]{:S(2)}) %collective-permute-start.11) | collective-permute-done | bytes 40992 | tf_op jit(solution)/shard_map/ppermute | solution.py:619
  26.8 3.9 %collective-permute-done.8.b2 = bf16[16,16,128]{2,1,0:T(8,128)(2,1)S(1)} collective-permute-done((bf16[16,16,128]{2,1,0:T(8,128)(2,1)S(1)}, bf16[16,16,128]{2,1,0:T(8,128)(2,1)S(1)}, u32[]{:S(2)}, u32[]{:S(2)}) %collective-permute-start.8) | collective-permute-done | bytes 65568 | tf_op jit(solution)/shard_map/ppermute | solution.py:619
  30.7 0.6 %collective-permute-start.12 = (f32[4,40,128]{2,1,0:T(8,128)S(1)}, f32[4,40,128]{2,1,0:T(8,128)S(1)}, u32[]{:S(2)}, u32[]{:S(2)}) collective-permute-start(f32[4,40,128]{2,1,0:T(8,128)S(1)} %pad_maximum_fusion), channel_id=1, source_target_pairs={{0,1},{1,0},{2,3},{3,2},{4,5},{5,4},{6,7},{7,6},{8,9},{9,8},{10,11... | collective-permute-start | bytes 245768 | tf_op jit(solution)/shard_map/ppermute | solution.py:619
  31.3 2.3 %collective-permute-start.13 = (f32[4,40,128]{2,1,0:T(8,128)S(1)}, f32[4,40,128]{2,1,0:T(8,128)S(1)}, u32[]{:S(2)}, u32[]{:S(2)}) collective-permute-start(f32[4,40,128]{2,1,0:T(8,128)S(1)} %pad_maximum_fusion), channel_id=1, source_target_pairs={{0,16},{8,24},{16,0},{24,8},{1,17},{9,25},{17,1},{25,9},{2,18},{10... | collective-permute-start | bytes 245768 | tf_op jit(solution)/shard_map/ppermute | solution.py:619
  33.7 2.1 %warp.1 = (f32[64,16,128]{2,1,0:T(8,128)}, f32[32,4,128]{2,1,0:T(4,128)}) custom-call(bf16[16,16,128]{2,1,0:T(8,128)(2,1)S(1)} %collective-permute-done.6.b0, bf16[16,16,128]{2,1,0:T(8,128)(2,1)S(1)} %collective-permute-done.7.b1, bf16[16,16,128]{2,1,0:T(8,128)(2,1)S(1)} %collective-permute-done.8.b2, bf16[16,16,128]{2,1,0:T(8,128)(2,1)S(1)} %collective-permute-done.9.b3, ...), custom_call_target="tpu_custom_call" | custom-call | bytes 14760000 | tf_op jit(solution)/shard_map/warp/pallas_call | solution.py:393
  35.8 3.5 %all-to-all-start = ((f32[32,4,128]{2,1,0:T(4,128)}), f32[32,4,128]{2,1,0:T(4,128)S(1)}, u32[]{:S(2)}, u32[]{:S(2)}) async-start(f32[32,4,128]{2,1,0:T(4,128)} %get-tuple-element.65), calls=%async_computation | async-start | bytes 131072 | tf_op jit(solution)/shard_map/all_to_all | solution.py:682
  39.3 0.3 collective-permute-start.15
  39.7 1.7 %collective-permute-start.14 = (f32[4,40,128]{2,1,0:T(8,128)S(1)}, f32[4,40,128]{2,1,0:T(8,128)S(1)}, u32[]{:S(2)}, u32[]{:S(2)}) collective-permute-start(f32[4,40,128]{2,1,0:T(8,128)S(1)} %collective-permute-done.12), channel_id=1, source_target_pairs={{0,16},{8,24},{16,0},{24,8},{1,17},{9,25},{17,1},{25,9},{2,18},{10... | collective-permute-start | bytes 245768 | tf_op jit(solution)/shard_map/ppermute | solution.py:619
  41.3 0.1 collective-permute-start.16
  41.4 0.4 collective-permute-start.17
  41.9 2.7 %collective-permute-done.14 = f32[4,40,128]{2,1,0:T(8,128)S(1)} collective-permute-done((f32[4,40,128]{2,1,0:T(8,128)S(1)}, f32[4,40,128]{2,1,0:T(8,128)S(1)}, u32[]{:S(2)}, u32[]{:S(2)}) %collective-permute-start.14) | collective-permute-done | bytes 81952 | tf_op jit(solution)/shard_map/ppermute | solution.py:619
  44.7 1.2 %collective-permute-done.18 = f32[4,40,128]{2,1,0:T(8,128)S(1)} collective-permute-done((f32[4,40,128]{2,1,0:T(8,128)S(1)}, f32[4,40,128]{2,1,0:T(8,128)S(1)}, u32[]{:S(2)}, u32[]{:S(2)}) %collective-permute-start.18) | collective-permute-done | bytes 81952 | tf_op jit(solution)/shard_map/ppermute | solution.py:619
  45.9 0.7 %all-to-all-done.load = f32[32,4,128]{2,1,0:T(4,128)S(1)} async-done(((f32[32,4,128]{2,1,0:T(4,128)}), f32[32,4,128]{2,1,0:T(4,128)S(1)}, u32[]{:S(2)}, u32[]{:S(2)}) %all-to-all-start) | async-done | bytes 65568 | tf_op jit(solution)/shard_map/all_to_all | solution.py:682
  46.6 2.3 %solve.1 = f32[3,5,1,8]{3,2,1,0:T(1,128)} custom-call(f32[32,40,128]{2,1,0:T(8,128)S(1)} %constant_dynamic-update-slice_fusion.hess, f32[32,4,128]{2,1,0:T(4,128)S(1)} %all-to-all-done.load), custom_call_target="tpu_custom_call" | custom-call | bytes 12915000 | tf_op jit(solution)/shard_map/solve/pallas_call | solution.py:601
  (36 shorter events, 0.1 us)
Async XLA Ops:
  0.6 12.5 %copy-start = (bf16[64,16,128]{2,1,0:T(8,128)(2,1)S(1)}, bf16[64,16,128]{2,1,0:T(8,128)(2,1)}, u32[]{:S(2)}) copy-start(bf16[64,16,128]{2,1,0:T(8,128)(2,1)} %ref.5) | copy-start | bytes 786436
  2.8 7.8 %copy-start.5 = (f32[8,128]{1,0:T(8,128)S(1)}, f32[8,128]{1,0:T(8,128)}, u32[]{:S(2)}) copy-start(f32[8,128]{1,0:T(8,128)} %get-tuple-element.40) | copy-start | bytes 12292
  2.8 10.3 %collective-permute-start = (bf16[72,16,128]{2,1,0:T(8,128)(2,1)}, bf16[72,16,128]{2,1,0:T(8,128)(2,1)S(1)}, u32[]{:S(2)}, u32[]{:S(2)}) collective-permute-start(bf16[72,16,128]{2,1,0:T(8,128)(2,1)} %get-tuple-element.36), channel_id=1, source_target_pairs={{0,8},{8,0},{16,24},{24,16},{1,9},{9,1},{17,25},{25,17},{2,10},{10... | collective-permute-start | bytes 884744 | tf_op jit(solution)/shard_map/ppermute | solution.py:619
  3.3 9.8 %collective-permute-start.1 = (bf16[72,16,128]{2,1,0:T(8,128)(2,1)}, bf16[72,16,128]{2,1,0:T(8,128)(2,1)S(1)}, u32[]{:S(2)}, u32[]{:S(2)}) collective-permute-start(bf16[72,16,128]{2,1,0:T(8,128)(2,1)} %get-tuple-element.36), channel_id=1, source_target_pairs={{8,16},{16,8},{9,17},{17,9},{10,18},{18,10},{11,19},{19,11},{12,20... | collective-permute-start | bytes 884744 | tf_op jit(solution)/shard_map/ppermute | solution.py:619
  4.0 6.6 %collective-permute-start.3 = (f32[16,128]{1,0:T(8,128)}, f32[16,128]{1,0:T(8,128)S(1)}, u32[]{:S(2)}, u32[]{:S(2)}) collective-permute-start(f32[16,128]{1,0:T(8,128)} %get-tuple-element.38), channel_id=1, source_target_pairs={{0,1},{1,0},{2,3},{3,2},{4,5},{5,4},{6,7},{7,6},{8,9},{9,8},{10,11... | collective-permute-start | bytes 24584 | tf_op jit(solution)/shard_map/ppermute | solution.py:619
  6.5 4.0 %copy-start.4 = (s32[1,1,32,3]{2,1,3,0:T(1,128)S(1)}, s32[1,1,32,3]{2,1,3,0:T(1,128)}, u32[]{:S(2)}) copy-start(s32[1,1,32,3]{2,1,3,0:T(1,128)} %param.11) | copy-start | bytes 1156
  6.5 6.6 %collective-permute-start.4 = (f32[16,128]{1,0:T(8,128)}, f32[16,128]{1,0:T(8,128)S(1)}, u32[]{:S(2)}, u32[]{:S(2)}) collective-permute-start(f32[16,128]{1,0:T(8,128)} %get-tuple-element.39), channel_id=1, source_target_pairs={{0,7},{1,2},{2,1},{3,4},{4,3},{5,6},{6,5},{7,0},{8,15},{9,10},{10,... | collective-permute-start | bytes 24584 | tf_op jit(solution)/shard_map/ppermute | solution.py:619
  10.1 5.6 %collective-permute-start.2 = (f32[8,128]{1,0:T(8,128)}, f32[8,128]{1,0:T(8,128)S(1)}, u32[]{:S(2)}, u32[]{:S(2)}) collective-permute-start(f32[8,128]{1,0:T(8,128)} %get-tuple-element.37), channel_id=1, source_target_pairs={{0,6},{1,7},{2,4},{3,5},{4,2},{5,3},{6,0},{7,1},{8,14},{9,15},{10,... | collective-permute-start | bytes 12296 | tf_op jit(solution)/shard_map/ppermute | solution.py:619
  10.6 5.2 %collective-permute-start.5 = (f32[8,128]{1,0:T(8,128)S(1)}, f32[8,128]{1,0:T(8,128)S(1)}, u32[]{:S(2)}, u32[]{:S(2)}) collective-permute-start(f32[8,128]{1,0:T(8,128)S(1)} %copy-done.5), channel_id=1, source_target_pairs={{0,2},{1,3},{2,0},{3,1},{4,6},{5,7},{6,4},{7,5},{8,10},{9,11},{10,... | collective-permute-start | bytes 12296 | tf_op jit(solution)/shard_map/ppermute | solution.py:619
  13.1 2.6 %copy-start.1 = (bf16[64,16,128]{2,1,0:T(8,128)(2,1)S(1)}, bf16[64,16,128]{2,1,0:T(8,128)(2,1)}, u32[]{:S(2)}) copy-start(bf16[64,16,128]{2,1,0:T(8,128)(2,1)} %refs_0_.1) | copy-start | bytes 786436
  15.1 0.7 %copy-start.2 = (f32[8,128]{1,0:T(8,128)S(1)}, f32[8,128]{1,0:T(8,128)}, u32[]{:S(2)}) copy-start(f32[8,128]{1,0:T(8,128)} %get-tuple-element.46.refs_7_) | copy-start | bytes 12292
  15.7 3.8 %collective-permute-start.10 = (f32[1,40,128]{2,1,0:T(8,128)S(1)}, f32[1,40,128]{2,1,0:T(8,128)S(1)}, u32[]{:S(2)}, u32[]{:S(2)}) collective-permute-start(f32[1,40,128]{2,1,0:T(8,128)S(1)} %bitcast.6), channel_id=1, source_target_pairs={{0,2},{1,3},{2,0},{3,1},{4,6},{5,7},{6,4},{7,5},{8,10},{9,11},{10,... | collective-permute-start | bytes 61448 | tf_op jit(solution)/shard_map/ppermute | solution.py:619
  19.6 7.2 %collective-permute-start.11 = (f32[2,40,128]{2,1,0:T(8,128)S(1)}, f32[2,40,128]{2,1,0:T(8,128)S(1)}, u32[]{:S(2)}, u32[]{:S(2)}) collective-permute-start(f32[2,40,128]{2,1,0:T(8,128)S(1)} %pad_maximum_fusion.1), channel_id=1, source_target_pairs={{0,4},{1,5},{2,6},{3,7},{4,0},{5,1},{6,2},{7,3},{8,12},{9,13},{10,... | collective-permute-start | bytes 122888 | tf_op jit(solution)/shard_map/ppermute | solution.py:619
  20.5 6.3 %collective-permute-start.6 = (bf16[16,16,128]{2,1,0:T(8,128)(2,1)S(1)}, bf16[16,16,128]{2,1,0:T(8,128)(2,1)S(1)}, u32[]{:S(2)}, u32[]{:S(2)}) collective-permute-start(bf16[16,16,128]{2,1,0:T(8,128)(2,1)S(1)} %get-tuple-element.47), channel_id=1, source_target_pairs={{0,6},{1,7},{2,4},{3,5},{4,2},{5,3},{6,0},{7,1},{8,14},{9,15},{10,... | collective-permute-start | bytes 196616 | tf_op jit(solution)/shard_map/ppermute | solution.py:619
  22.1 4.7 %collective-permute-start.7 = (bf16[16,16,128]{2,1,0:T(8,128)(2,1)S(1)}, bf16[16,16,128]{2,1,0:T(8,128)(2,1)S(1)}, u32[]{:S(2)}, u32[]{:S(2)}) collective-permute-start(bf16[16,16,128]{2,1,0:T(8,128)(2,1)S(1)} %get-tuple-element.48), channel_id=1, source_target_pairs={{0,1},{1,0},{2,3},{3,2},{4,5},{5,4},{6,7},{7,6},{8,9},{9,8},{10,11... | collective-permute-start | bytes 196616 | tf_op jit(solution)/shard_map/ppermute | solution.py:619
  23.1 7.6 %collective-permute-start.8 = (bf16[16,16,128]{2,1,0:T(8,128)(2,1)S(1)}, bf16[16,16,128]{2,1,0:T(8,128)(2,1)S(1)}, u32[]{:S(2)}, u32[]{:S(2)}) collective-permute-start(bf16[16,16,128]{2,1,0:T(8,128)(2,1)S(1)} %get-tuple-element.49), channel_id=1, source_target_pairs={{0,7},{1,2},{2,1},{3,4},{4,3},{5,6},{6,5},{7,0},{8,15},{9,10},{10,... | collective-permute-start | bytes 196616 | tf_op jit(solution)/shard_map/ppermute | solution.py:619
  25.7 5.0 %collective-permute-start.9 = (bf16[16,16,128]{2,1,0:T(8,128)(2,1)S(1)}, bf16[16,16,128]{2,1,0:T(8,128)(2,1)S(1)}, u32[]{:S(2)}, u32[]{:S(2)}) collective-permute-start(bf16[16,16,128]{2,1,0:T(8,128)(2,1)S(1)} %get-tuple-element.50), channel_id=1, source_target_pairs={{0,2},{1,3},{2,0},{3,1},{4,6},{5,7},{6,4},{7,5},{8,10},{9,11},{10,... | collective-permute-start | bytes 196616 | tf_op jit(solution)/shard_map/ppermute | solution.py:619
  26.8 6.9 %copy-start.3 = (s32[8,128]{1,0:T(8,128)S(1)}, s32[8,128]{1,0:T(8,128)}, u32[]{:S(2)}) copy-start(s32[8,128]{1,0:T(8,128)} %get-tuple-element.61.place) | copy-start | bytes 12292
  30.7 8.6 %collective-permute-start.12 = (f32[4,40,128]{2,1,0:T(8,128)S(1)}, f32[4,40,128]{2,1,0:T(8,128)S(1)}, u32[]{:S(2)}, u32[]{:S(2)}) collective-permute-start(f32[4,40,128]{2,1,0:T(8,128)S(1)} %pad_maximum_fusion), channel_id=1, source_target_pairs={{0,1},{1,0},{2,3},{3,2},{4,5},{5,4},{6,7},{7,6},{8,9},{9,8},{10,11... | collective-permute-start | bytes 245768 | tf_op jit(solution)/shard_map/ppermute | solution.py:619
  31.3 8.0 %collective-permute-start.13 = (f32[4,40,128]{2,1,0:T(8,128)S(1)}, f32[4,40,128]{2,1,0:T(8,128)S(1)}, u32[]{:S(2)}, u32[]{:S(2)}) collective-permute-start(f32[4,40,128]{2,1,0:T(8,128)S(1)} %pad_maximum_fusion), channel_id=1, source_target_pairs={{0,16},{8,24},{16,0},{24,8},{1,17},{9,25},{17,1},{25,9},{2,18},{10... | collective-permute-start | bytes 245768 | tf_op jit(solution)/shard_map/ppermute | solution.py:619
  35.8 10.8 %all-to-all-start = ((f32[32,4,128]{2,1,0:T(4,128)}), f32[32,4,128]{2,1,0:T(4,128)S(1)}, u32[]{:S(2)}, u32[]{:S(2)}) async-start(f32[32,4,128]{2,1,0:T(4,128)} %get-tuple-element.65), calls=%async_computation | async-start | bytes 131072 | tf_op jit(solution)/shard_map/all_to_all | solution.py:682
  39.3 5.3 %collective-permute-start.15 = (f32[4,40,128]{2,1,0:T(8,128)S(1)}, f32[4,40,128]{2,1,0:T(8,128)S(1)}, u32[]{:S(2)}, u32[]{:S(2)}) collective-permute-start(f32[4,40,128]{2,1,0:T(8,128)S(1)} %pad_maximum_fusion), channel_id=1, source_target_pairs={{0,8},{8,0},{16,24},{24,16},{1,9},{9,1},{17,25},{25,17},{2,10},{10... | collective-permute-start | bytes 245768 | tf_op jit(solution)/shard_map/ppermute | solution.py:619
  39.7 4.9 %collective-permute-start.14 = (f32[4,40,128]{2,1,0:T(8,128)S(1)}, f32[4,40,128]{2,1,0:T(8,128)S(1)}, u32[]{:S(2)}, u32[]{:S(2)}) collective-permute-start(f32[4,40,128]{2,1,0:T(8,128)S(1)} %collective-permute-done.12), channel_id=1, source_target_pairs={{0,16},{8,24},{16,0},{24,8},{1,17},{9,25},{17,1},{25,9},{2,18},{10... | collective-permute-start | bytes 245768 | tf_op jit(solution)/shard_map/ppermute | solution.py:619
  41.3 3.3 %collective-permute-start.16 = (f32[4,40,128]{2,1,0:T(8,128)S(1)}, f32[4,40,128]{2,1,0:T(8,128)S(1)}, u32[]{:S(2)}, u32[]{:S(2)}) collective-permute-start(f32[4,40,128]{2,1,0:T(8,128)S(1)} %collective-permute-done.12), channel_id=1, source_target_pairs={{0,8},{8,0},{16,24},{24,16},{1,9},{9,1},{17,25},{25,17},{2,10},{10... | collective-permute-start | bytes 245768 | tf_op jit(solution)/shard_map/ppermute | solution.py:619
  41.4 3.3 %collective-permute-start.17 = (f32[4,40,128]{2,1,0:T(8,128)S(1)}, f32[4,40,128]{2,1,0:T(8,128)S(1)}, u32[]{:S(2)}, u32[]{:S(2)}) collective-permute-start(f32[4,40,128]{2,1,0:T(8,128)S(1)} %collective-permute-done.13), channel_id=1, source_target_pairs={{0,8},{8,0},{16,24},{24,16},{1,9},{9,1},{17,25},{25,17},{2,10},{10... | collective-permute-start | bytes 245768 | tf_op jit(solution)/shard_map/ppermute | solution.py:619
  44.6 1.3 %collective-permute-start.18 = (f32[4,40,128]{2,1,0:T(8,128)S(1)}, f32[4,40,128]{2,1,0:T(8,128)S(1)}, u32[]{:S(2)}, u32[]{:S(2)}) collective-permute-start(f32[4,40,128]{2,1,0:T(8,128)S(1)} %collective-permute-done.14), channel_id=1, source_target_pairs={{0,8},{8,0},{16,24},{24,16},{1,9},{9,1},{17,25},{25,17},{2,10},{10... | collective-permute-start | bytes 245768 | tf_op jit(solution)/shard_map/ppermute | solution.py:619

commit v7 on v6

--- a/solution.py
+++ b/solution.py
@@ -253,30 +253,37 @@
     before = jnp.where(gx_even, high1, high0)
     after = jnp.where(gx_even, low0, low1)
     lane2, row2 = lanes((EDGE, NY)), rows_of((EDGE, NY))
+
+    def slopes(z):
+        plane = ref[z].astype(F32)
+        below = ref[z - 1].astype(F32) if z > 0 else jnp.zeros((EDGE, NY), F32)
+        above = ref[z + 1].astype(F32) if z + 1 < NZ else jnp.zeros((EDGE, NY), F32)
+        rim_z = rim[z]
+        nxt = jnp.where(row2 == EDGE - 1, after[z : z + 1, :], pltpu.roll(plane, EDGE - 1, 0))
+        prv = jnp.where(row2 == 0, before[z : z + 1, :], pltpu.roll(plane, 1, 0))
+        right = jnp.where(lane2 == NY - 1, rim_z, pltpu.roll(plane, NY - 1, 1))
+        left = jnp.where(lane2 == 0, rim_z, pltpu.roll(plane, 1, 1))
+        rounded = [(value * 0.5).astype(BF16) for value in (above - below, nxt - prv, right - left)]
+        for c in range(3):
+            grad[c, z] = rounded[c]
+        return [value.astype(F32) for value in rounded]
+
     for ez in range(EZ):
-        collected = [[jnp.zeros((EDGE, NY), F32) for _ in range(3)] for _ in PAIRS]
-        for k in range(EDGE):
-            z = ez * EDGE + k
-            plane = ref[z].astype(F32)
-            below = ref[z - 1].astype(F32) if z > 0 else jnp.zeros((EDGE, NY), F32)
-            above = ref[z + 1].astype(F32) if z + 1 < NZ else jnp.zeros((EDGE, NY), F32)
-            rim_z = rim[z]
-            nxt = jnp.where(row2 == EDGE - 1, after[z : z + 1, :], pltpu.roll(plane, EDGE - 1, 0))
-            prv = jnp.where(row2 == 0, before[z : z + 1, :], pltpu.roll(plane, 1, 0))
-            right = jnp.where(lane2 == NY - 1, rim_z, pltpu.roll(plane, NY - 1, 1))
-            left = jnp.where(lane2 == 0, rim_z, pltpu.roll(plane, 1, 1))
-            rounded = [((above - below) * 0.5).astype(BF16), ((nxt - prv) * 0.5).astype(BF16), ((right - left) * 0.5).astype(BF16)]
-            for c in range(3):
-                grad[c, z] = rounded[c]
-            g = [value.astype(F32) for value in rounded]
+        sums = [[jnp.zeros((EDGE, NY), F32) for _ in range(3)] for _ in PAIRS]
+        for k in range(EDGE // 2):
+            both = [slopes(ez * EDGE + k), slopes(ez * EDGE + EDGE - 1 - k)]
+            away = float(0.5 - UPPER[k])
             for p, (c, d) in enumerate(PAIRS):
-                product = g[c] * g[d]
-                for w in range(3):
-                    collected[p][w] = collected[p][w] + float(PRODUCTS[w, k]) * product
+                low, high = (g[c] * g[d] for g in both)
+                even_part, odd_part = low + high, high - low
+                sums[p][0] = sums[p][0] + even_part
+                sums[p][1] = sums[p][1] + away * odd_part
+                sums[p][2] = sums[p][2] + (away * away) * even_part
         for p in range(len(PAIRS)):
-            for w in range(3):
+            quarter, first, second = sums[p][0] * 0.25, sums[p][1], sums[p][2]
+            for w, value in enumerate((quarter - first + second, quarter - second, quarter + first + second)):
                 start = (ez * 18 + p * 3 + w) * EDGE
-                slabs[start : start + EDGE, :] = collected[p][w]
+                slabs[start : start + EDGE, :] = value
     found = weighed(slabs[...], along_y(hat_product, (0, 1, 2)))
     across = [hat_product(w, row2) for w in range(3)]
     row8, group8 = rows_of((8, 128)), lanes((8, 128)) // NEL
@@ -348,19 +355,21 @@
         shifted = jnp.concatenate([blended[EDGE:], blended[-EDGE:]], axis=0)
         blended = (1.0 - tz) * blended + tz * shifted
         blended = blended.reshape(EDGE, EDGE, NY)
-        collected = [[jnp.zeros((EDGE, NY), F32) for _ in range(2)] for _ in range(3)]
-        for k in range(EDGE):
-            z = ez * EDGE + k
-            apart = ref[z].astype(F32) - blended[k]
-            mismatch[z] = apart
+        sums = [[jnp.zeros((EDGE, NY), F32) for _ in range(2)] for _ in range(3)]
+        for k in range(EDGE // 2):
+            planes = (ez * EDGE + k, ez * EDGE + EDGE - 1 - k)
+            aparts = [ref[z].astype(F32) - blended[z - ez * EDGE] for z in planes]
+            for z, apart in zip(planes, aparts):
+                mismatch[z] = apart
             for c in range(3):
-                term = grad[c, z].astype(F32) * apart
-                for a in range(2):
-                    collected[c][a] = collected[c][a] + float(HAT[a, k]) * term
+                low, high = (grad[c, z].astype(F32) * apart for z, apart in zip(planes, aparts))
+                sums[c][0] = sums[c][0] + (low + high)
+                sums[c][1] = sums[c][1] + float(0.5 - UPPER[k]) * (high - low)
         for c in range(3):
-            for a in range(2):
+            half, first = sums[c][0] * 0.5, sums[c][1]
+            for a, value in enumerate((half - first, half + first)):
                 start = (ez * 6 + c * 2 + a) * EDGE
-                slabs[start : start + EDGE, :] = collected[c][a]
+                slabs[start : start + EDGE, :] = value
     found = weighed_once(slabs[...], along_y(lambda group, at: hat_weight(lax.rem(group, 2), at), (0, 1, 2, 3)))
     across = hat_weight(lanes((EDGE, 128)) // (2 * NEL), rows_of((EDGE, 128)))
     row, lane = rows_of((8, 128)), lanes((8, 128))

time: 49.1 us -> 48.6 us (0.990)
  no operation moved by 1% of the time
where the time goes in v7:
time: 48.6 us; the launch traced here: 48.4 us
  starting transfers between devices  22.6 us (47%)
  waiting for transfers between devices  14.7 us (30%)
  Pallas kernels  10.1 us (21%)
  between operations  0.81 us (2%)
    ppermute x19, starting transfers between devices, swap(): lax.ppermute(array, axis, [(i, j) for i, j in pairs if 0 <= j < size])  19.3 us
    ppermute x19, waiting for transfers between devices, swap(): lax.ppermute(array, axis, [(i, j) for i, j in pairs if 0 <= j < size])  14 us
    all_to_all x1, starting transfers between devices, body(): load = lax.all_to_all(part, ('gx', 'gy'), 0, 0)  3.33 us
    pallas_call x1, Pallas kernels, solve(): pl.pallas_call(functools.partial(solve_kernel, gx_count, gy_count), out_s...  2.33 us
    pallas_call x1, Pallas kernels, ask(): pl.pallas_call(functools.partial(ask_kernel, lax.axis_size('gx')), out_sh...  2.14 us
    pallas_call x1, Pallas kernels, warp(): pl.pallas_call(warp_kernel, out_shape=(jax.ShapeDtypeStruct((NZ, EDGE, NY...  1.99 us
    pallas_call x1, Pallas kernels, serve(): pl.pallas_call(functools.partial(serve_kernel, lines), out_shape=(jax.Sha...  1.89 us
    pallas_call x1, Pallas kernels, moments(): pl.pallas_call(functools.partial(moments_kernel, lax.axis_size('gy')), ou...  1.75 us
  transfers between devices with their start and end apart: 20, of which 8 were waited for; matrix products, arithmetic and copies ran while one was open for 0% of the time, Pallas kernels for 12%

profile of v7, /device:TPU:0, one launch (start us, length us, event | category | flops | bytes accessed | tf_op | source)
XLA Modules:
  0.0 48.4 jit_solution(16070308018620864856)
XLA Ops:
  0.6 2.1 %ask.1 = (f32[16,128]{1,0:T(8,128)}, f32[16,128]{1,0:T(8,128)}, f32[8,128]{1,0:T(8,128)}, f32[8,128]{1,0:T(8,128)}, bf16[72,16,128]{2,1,0:T(8,128)(2,1)}, /*index=5*/f32[8,128]{1,0:T(8,128)}, s32[8,128]{1,0:T(8,128)}) custom-call(s32[1,32]{1,0:T(1,128)} %bitcast.8, s32[1,32]{1,0:T(1,128)} %bitcast.9, s32[1,32]{1,0:T(1,128)} %bitcast.10, ...), custom_call_target="tpu_custom_call" | custom-call | bytes 7380000 | tf_op jit(solution)/shard_map/ask/pallas_call | solution.py:162
  2.8 0.5 %collective-permute-start = (bf16[72,16,128]{2,1,0:T(8,128)(2,1)}, bf16[72,16,128]{2,1,0:T(8,128)(2,1)S(1)}, u32[]{:S(2)}, u32[]{:S(2)}) collective-permute-start(bf16[72,16,128]{2,1,0:T(8,128)(2,1)} %get-tuple-element.36), channel_id=1, source_target_pairs={{0,8},{8,0},{16,24},{24,16},{1,9},{9,1},{17,25},{25,17},{2,10},{10... | collective-permute-start | bytes 884744 | tf_op jit(solution)/shard_map/ppermute | solution.py:628
  3.3 0.7 %collective-permute-start.1 = (bf16[72,16,128]{2,1,0:T(8,128)(2,1)}, bf16[72,16,128]{2,1,0:T(8,128)(2,1)S(1)}, u32[]{:S(2)}, u32[]{:S(2)}) collective-permute-start(bf16[72,16,128]{2,1,0:T(8,128)(2,1)} %get-tuple-element.36), channel_id=1, source_target_pairs={{8,16},{16,8},{9,17},{17,9},{10,18},{18,10},{11,19},{19,11},{12,20... | collective-permute-start | bytes 884744 | tf_op jit(solution)/shard_map/ppermute | solution.py:628
  4.0 2.6 %collective-permute-start.3 = (f32[16,128]{1,0:T(8,128)}, f32[16,128]{1,0:T(8,128)S(1)}, u32[]{:S(2)}, u32[]{:S(2)}) collective-permute-start(f32[16,128]{1,0:T(8,128)} %get-tuple-element.38), channel_id=1, source_target_pairs={{0,1},{1,0},{2,3},{3,2},{4,5},{5,4},{6,7},{7,6},{8,9},{9,8},{10,11... | collective-permute-start | bytes 24584 | tf_op jit(solution)/shard_map/ppermute | solution.py:628
  6.5 3.6 %collective-permute-start.4 = (f32[16,128]{1,0:T(8,128)}, f32[16,128]{1,0:T(8,128)S(1)}, u32[]{:S(2)}, u32[]{:S(2)}) collective-permute-start(f32[16,128]{1,0:T(8,128)} %get-tuple-element.39), channel_id=1, source_target_pairs={{0,7},{1,2},{2,1},{3,4},{4,3},{5,6},{6,5},{7,0},{8,15},{9,10},{10,... | collective-permute-start | bytes 24584 | tf_op jit(solution)/shard_map/ppermute | solution.py:628
  10.1 0.4 collective-permute-start.2
  10.6 0.1 copy.9
  10.7 2.4 %collective-permute-done.4.r1.refs_5_ = f32[16,128]{1,0:T(8,128)S(1)} collective-permute-done((f32[16,128]{1,0:T(8,128)}, f32[16,128]{1,0:T(8,128)S(1)}, u32[]{:S(2)}, u32[]{:S(2)}) %collective-permute-start.4) | collective-permute-done | bytes 8224 | tf_op jit(solution)/shard_map/ppermute | solution.py:628
  13.1 0.0 copy-start.1
  13.1 1.7 %moments.1 = (bf16[3,64,16,128]{3,2,1,0:T(8,128)(2,1)S(1)}, f32[40,128]{1,0:T(8,128)S(1)}, f32[8,128]{1,0:T(8,128)S(1)}, f32[4,8,128]{2,1,0:T(8,128)S(1)}) custom-call(f32[16,128]{1,0:T(8,128)S(1)} %collective-permute-done.3.r0.refs_4_, f32[16,128]{1,0:T(8,128)S(1)} %collective-permute-done.4.r1.refs_5_, ...), custom_call_target="tpu_custom_call" | custom-call | bytes 8118000 | tf_op jit(solution)/shard_map/moments/pallas_call | solution.py:317
  14.9 0.9 %collective-permute-done.2.refs_3_ = f32[8,128]{1,0:T(8,128)S(1)} collective-permute-done((f32[8,128]{1,0:T(8,128)}, f32[8,128]{1,0:T(8,128)S(1)}, u32[]{:S(2)}, u32[]{:S(2)}) %collective-permute-start.2) | collective-permute-done | bytes 4128 | tf_op jit(solution)/shard_map/ppermute | solution.py:628
  15.8 1.9 %serve.1 = (bf16[16,16,128]{2,1,0:T(8,128)(2,1)S(1)}, bf16[16,16,128]{2,1,0:T(8,128)(2,1)S(1)}, bf16[16,16,128]{2,1,0:T(8,128)(2,1)S(1)}, bf16[16,16,128]{2,1,0:T(8,128)(2,1)S(1)}, bf16[16,16,128]{2,1,0:T(8,128)(2,1)S(1)}) custom-call(bf16[64,16,128]{2,1,0:T(8,128)(2,1)S(1)} %copy-done.1, bf16[72,16,128]{2,1,0:T(8,128)(2,1)S(1)} %collective-permute-done.a0.refs_1_, ...), custom_call_target="tpu_custom_call" | custom-call | bytes 7380000 | tf_op jit(solution)/shard_map/serve/pallas_call | solution.py:216
  17.7 1.9 %collective-permute-done.10 = f32[1,40,128]{2,1,0:T(8,128)S(1)} collective-permute-done((f32[1,40,128]{2,1,0:T(8,128)S(1)}, f32[1,40,128]{2,1,0:T(8,128)S(1)}, u32[]{:S(2)}, u32[]{:S(2)}) %collective-permute-start.10) | collective-permute-done | bytes 20512 | tf_op jit(solution)/shard_map/ppermute | solution.py:628
  19.6 0.7 %collective-permute-start.11 = (f32[2,40,128]{2,1,0:T(8,128)S(1)}, f32[2,40,128]{2,1,0:T(8,128)S(1)}, u32[]{:S(2)}, u32[]{:S(2)}) collective-permute-start(f32[2,40,128]{2,1,0:T(8,128)S(1)} %pad_maximum_fusion.1), channel_id=1, source_target_pairs={{0,4},{1,5},{2,6},{3,7},{4,0},{5,1},{6,2},{7,3},{8,12},{9,13},{10,... | collective-permute-start | bytes 122888 | tf_op jit(solution)/shard_map/ppermute | solution.py:628
  20.3 1.9 %collective-permute-start.6 = (bf16[16,16,128]{2,1,0:T(8,128)(2,1)S(1)}, bf16[16,16,128]{2,1,0:T(8,128)(2,1)S(1)}, u32[]{:S(2)}, u32[]{:S(2)}) collective-permute-start(bf16[16,16,128]{2,1,0:T(8,128)(2,1)S(1)} %get-tuple-element.47), channel_id=1, source_target_pairs={{0,6},{1,7},{2,4},{3,5},{4,2},{5,3},{6,0},{7,1},{8,14},{9,15},{10,... | collective-permute-start | bytes 196616 | tf_op jit(solution)/shard_map/ppermute | solution.py:628
  22.1 0.8 %collective-permute-start.7 = (bf16[16,16,128]{2,1,0:T(8,128)(2,1)S(1)}, bf16[16,16,128]{2,1,0:T(8,128)(2,1)S(1)}, u32[]{:S(2)}, u32[]{:S(2)}) collective-permute-start(bf16[16,16,128]{2,1,0:T(8,128)(2,1)S(1)} %get-tuple-element.48), channel_id=1, source_target_pairs={{0,1},{1,0},{2,3},{3,2},{4,5},{5,4},{6,7},{7,6},{8,9},{9,8},{10,11... | collective-permute-start | bytes 196616 | tf_op jit(solution)/shard_map/ppermute | solution.py:628
  22.9 2.6 %collective-permute-start.8 = (bf16[16,16,128]{2,1,0:T(8,128)(2,1)S(1)}, bf16[16,16,128]{2,1,0:T(8,128)(2,1)S(1)}, u32[]{:S(2)}, u32[]{:S(2)}) collective-permute-start(bf16[16,16,128]{2,1,0:T(8,128)(2,1)S(1)} %get-tuple-element.49), channel_id=1, source_target_pairs={{0,7},{1,2},{2,1},{3,4},{4,3},{5,6},{6,5},{7,0},{8,15},{9,10},{10,... | collective-permute-start | bytes 196616 | tf_op jit(solution)/shard_map/ppermute | solution.py:628
  25.5 0.1 collective-permute-start.9
  25.6 1.1 %collective-permute-done.11 = f32[2,40,128]{2,1,0:T(8,128)S(1)} collective-permute-done((f32[2,40,128]{2,1,0:T(8,128)S(1)}, f32[2,40,128]{2,1,0:T(8,128)S(1)}, u32[]{:S(2)}, u32[]{:S(2)}) %collective-permute-start.11) | collective-permute-done | bytes 40992 | tf_op jit(solution)/shard_map/ppermute | solution.py:628
  26.8 3.7 %collective-permute-done.8.b2 = bf16[16,16,128]{2,1,0:T(8,128)(2,1)S(1)} collective-permute-done((bf16[16,16,128]{2,1,0:T(8,128)(2,1)S(1)}, bf16[16,16,128]{2,1,0:T(8,128)(2,1)S(1)}, u32[]{:S(2)}, u32[]{:S(2)}) %collective-permute-start.8) | collective-permute-done | bytes 65568 | tf_op jit(solution)/shard_map/ppermute | solution.py:628
  30.5 0.6 %collective-permute-start.12 = (f32[4,40,128]{2,1,0:T(8,128)S(1)}, f32[4,40,128]{2,1,0:T(8,128)S(1)}, u32[]{:S(2)}, u32[]{:S(2)}) collective-permute-start(f32[4,40,128]{2,1,0:T(8,128)S(1)} %pad_maximum_fusion), channel_id=1, source_target_pairs={{0,1},{1,0},{2,3},{3,2},{4,5},{5,4},{6,7},{7,6},{8,9},{9,8},{10,11... | collective-permute-start | bytes 245768 | tf_op jit(solution)/shard_map/ppermute | solution.py:628
  31.2 2.3 %collective-permute-start.13 = (f32[4,40,128]{2,1,0:T(8,128)S(1)}, f32[4,40,128]{2,1,0:T(8,128)S(1)}, u32[]{:S(2)}, u32[]{:S(2)}) collective-permute-start(f32[4,40,128]{2,1,0:T(8,128)S(1)} %pad_maximum_fusion), channel_id=1, source_target_pairs={{0,16},{8,24},{16,0},{24,8},{1,17},{9,25},{17,1},{25,9},{2,18},{10... | collective-permute-start | bytes 245768 | tf_op jit(solution)/shard_map/ppermute | solution.py:628
  33.5 2.0 %warp.1 = (f32[64,16,128]{2,1,0:T(8,128)}, f32[32,4,128]{2,1,0:T(4,128)}) custom-call(bf16[16,16,128]{2,1,0:T(8,128)(2,1)S(1)} %collective-permute-done.6.b0, bf16[16,16,128]{2,1,0:T(8,128)(2,1)S(1)} %collective-permute-done.7.b1, bf16[16,16,128]{2,1,0:T(8,128)(2,1)S(1)} %collective-permute-done.8.b2, bf16[16,16,128]{2,1,0:T(8,128)(2,1)S(1)} %collective-permute-done.9.b3, ...), custom_call_target="tpu_custom_call" | custom-call | bytes 14760000 | tf_op jit(solution)/shard_map/warp/pallas_call | solution.py:402
  35.5 3.3 %all-to-all-start = ((f32[32,4,128]{2,1,0:T(4,128)}), f32[32,4,128]{2,1,0:T(4,128)S(1)}, u32[]{:S(2)}, u32[]{:S(2)}) async-start(f32[32,4,128]{2,1,0:T(4,128)} %get-tuple-element.65), calls=%async_computation | async-start | bytes 131072 | tf_op jit(solution)/shard_map/all_to_all | solution.py:691
  38.9 0.3 collective-permute-start.15
  39.2 1.7 %collective-permute-start.14 = (f32[4,40,128]{2,1,0:T(8,128)S(1)}, f32[4,40,128]{2,1,0:T(8,128)S(1)}, u32[]{:S(2)}, u32[]{:S(2)}) collective-permute-start(f32[4,40,128]{2,1,0:T(8,128)S(1)} %collective-permute-done.12), channel_id=1, source_target_pairs={{0,16},{8,24},{16,0},{24,8},{1,17},{9,25},{17,1},{25,9},{2,18},{10... | collective-permute-start | bytes 245768 | tf_op jit(solution)/shard_map/ppermute | solution.py:628
  40.9 0.1 collective-permute-start.16
  40.9 0.4 collective-permute-start.17
  41.4 2.7 %collective-permute-done.14 = f32[4,40,128]{2,1,0:T(8,128)S(1)} collective-permute-done((f32[4,40,128]{2,1,0:T(8,128)S(1)}, f32[4,40,128]{2,1,0:T(8,128)S(1)}, u32[]{:S(2)}, u32[]{:S(2)}) %collective-permute-start.14) | collective-permute-done | bytes 81952 | tf_op jit(solution)/shard_map/ppermute | solution.py:628
  44.2 1.2 %collective-permute-done.18 = f32[4,40,128]{2,1,0:T(8,128)S(1)} collective-permute-done((f32[4,40,128]{2,1,0:T(8,128)S(1)}, f32[4,40,128]{2,1,0:T(8,128)S(1)}, u32[]{:S(2)}, u32[]{:S(2)}) %collective-permute-start.18) | collective-permute-done | bytes 81952 | tf_op jit(solution)/shard_map/ppermute | solution.py:628
  45.4 0.7 %all-to-all-done.load = f32[32,4,128]{2,1,0:T(4,128)S(1)} async-done(((f32[32,4,128]{2,1,0:T(4,128)}), f32[32,4,128]{2,1,0:T(4,128)S(1)}, u32[]{:S(2)}, u32[]{:S(2)}) %all-to-all-start) | async-done | bytes 65568 | tf_op jit(solution)/shard_map/all_to_all | solution.py:691
  46.1 2.3 %solve.1 = f32[3,5,1,8]{3,2,1,0:T(1,128)} custom-call(f32[32,40,128]{2,1,0:T(8,128)S(1)} %constant_dynamic-update-slice_fusion.hess, f32[32,4,128]{2,1,0:T(4,128)S(1)} %all-to-all-done.load), custom_call_target="tpu_custom_call" | custom-call | bytes 12915000 | tf_op jit(solution)/shard_map/solve/pallas_call | solution.py:610
  (36 shorter events, 0.1 us)
Async XLA Ops:
  0.6 12.5 %copy-start = (bf16[64,16,128]{2,1,0:T(8,128)(2,1)S(1)}, bf16[64,16,128]{2,1,0:T(8,128)(2,1)}, u32[]{:S(2)}) copy-start(bf16[64,16,128]{2,1,0:T(8,128)(2,1)} %ref.5) | copy-start | bytes 786436
  2.8 7.8 %copy-start.5 = (f32[8,128]{1,0:T(8,128)S(1)}, f32[8,128]{1,0:T(8,128)}, u32[]{:S(2)}) copy-start(f32[8,128]{1,0:T(8,128)} %get-tuple-element.40) | copy-start | bytes 12292
  2.8 10.3 %collective-permute-start = (bf16[72,16,128]{2,1,0:T(8,128)(2,1)}, bf16[72,16,128]{2,1,0:T(8,128)(2,1)S(1)}, u32[]{:S(2)}, u32[]{:S(2)}) collective-permute-start(bf16[72,16,128]{2,1,0:T(8,128)(2,1)} %get-tuple-element.36), channel_id=1, source_target_pairs={{0,8},{8,0},{16,24},{24,16},{1,9},{9,1},{17,25},{25,17},{2,10},{10... | collective-permute-start | bytes 884744 | tf_op jit(solution)/shard_map/ppermute | solution.py:628
  3.3 9.8 %collective-permute-start.1 = (bf16[72,16,128]{2,1,0:T(8,128)(2,1)}, bf16[72,16,128]{2,1,0:T(8,128)(2,1)S(1)}, u32[]{:S(2)}, u32[]{:S(2)}) collective-permute-start(bf16[72,16,128]{2,1,0:T(8,128)(2,1)} %get-tuple-element.36), channel_id=1, source_target_pairs={{8,16},{16,8},{9,17},{17,9},{10,18},{18,10},{11,19},{19,11},{12,20... | collective-permute-start | bytes 884744 | tf_op jit(solution)/shard_map/ppermute | solution.py:628
  4.0 6.6 %collective-permute-start.3 = (f32[16,128]{1,0:T(8,128)}, f32[16,128]{1,0:T(8,128)S(1)}, u32[]{:S(2)}, u32[]{:S(2)}) collective-permute-start(f32[16,128]{1,0:T(8,128)} %get-tuple-element.38), channel_id=1, source_target_pairs={{0,1},{1,0},{2,3},{3,2},{4,5},{5,4},{6,7},{7,6},{8,9},{9,8},{10,11... | collective-permute-start | bytes 24584 | tf_op jit(solution)/shard_map/ppermute | solution.py:628
  6.5 4.0 %copy-start.4 = (s32[1,1,32,3]{2,1,3,0:T(1,128)S(1)}, s32[1,1,32,3]{2,1,3,0:T(1,128)}, u32[]{:S(2)}) copy-start(s32[1,1,32,3]{2,1,3,0:T(1,128)} %param.11) | copy-start | bytes 1156
  6.5 6.6 %collective-permute-start.4 = (f32[16,128]{1,0:T(8,128)}, f32[16,128]{1,0:T(8,128)S(1)}, u32[]{:S(2)}, u32[]{:S(2)}) collective-permute-start(f32[16,128]{1,0:T(8,128)} %get-tuple-element.39), channel_id=1, source_target_pairs={{0,7},{1,2},{2,1},{3,4},{4,3},{5,6},{6,5},{7,0},{8,15},{9,10},{10,... | collective-permute-start | bytes 24584 | tf_op jit(solution)/shard_map/ppermute | solution.py:628
  10.1 5.6 %collective-permute-start.2 = (f32[8,128]{1,0:T(8,128)}, f32[8,128]{1,0:T(8,128)S(1)}, u32[]{:S(2)}, u32[]{:S(2)}) collective-permute-start(f32[8,128]{1,0:T(8,128)} %get-tuple-element.37), channel_id=1, source_target_pairs={{0,6},{1,7},{2,4},{3,5},{4,2},{5,3},{6,0},{7,1},{8,14},{9,15},{10,... | collective-permute-start | bytes 12296 | tf_op jit(solution)/shard_map/ppermute | solution.py:628
  10.6 5.2 %collective-permute-start.5 = (f32[8,128]{1,0:T(8,128)S(1)}, f32[8,128]{1,0:T(8,128)S(1)}, u32[]{:S(2)}, u32[]{:S(2)}) collective-permute-start(f32[8,128]{1,0:T(8,128)S(1)} %copy-done.5), channel_id=1, source_target_pairs={{0,2},{1,3},{2,0},{3,1},{4,6},{5,7},{6,4},{7,5},{8,10},{9,11},{10,... | collective-permute-start | bytes 12296 | tf_op jit(solution)/shard_map/ppermute | solution.py:628
  13.1 2.6 %copy-start.1 = (bf16[64,16,128]{2,1,0:T(8,128)(2,1)S(1)}, bf16[64,16,128]{2,1,0:T(8,128)(2,1)}, u32[]{:S(2)}) copy-start(bf16[64,16,128]{2,1,0:T(8,128)(2,1)} %refs_0_.1) | copy-start | bytes 786436
  14.9 0.9 %copy-start.2 = (f32[8,128]{1,0:T(8,128)S(1)}, f32[8,128]{1,0:T(8,128)}, u32[]{:S(2)}) copy-start(f32[8,128]{1,0:T(8,128)} %get-tuple-element.46.refs_7_) | copy-start | bytes 12292
  15.7 3.8 %collective-permute-start.10 = (f32[1,40,128]{2,1,0:T(8,128)S(1)}, f32[1,40,128]{2,1,0:T(8,128)S(1)}, u32[]{:S(2)}, u32[]{:S(2)}) collective-permute-start(f32[1,40,128]{2,1,0:T(8,128)S(1)} %bitcast.6), channel_id=1, source_target_pairs={{0,2},{1,3},{2,0},{3,1},{4,6},{5,7},{6,4},{7,5},{8,10},{9,11},{10,... | collective-permute-start | bytes 61448 | tf_op jit(solution)/shard_map/ppermute | solution.py:628
  19.6 7.2 %collective-permute-start.11 = (f32[2,40,128]{2,1,0:T(8,128)S(1)}, f32[2,40,128]{2,1,0:T(8,128)S(1)}, u32[]{:S(2)}, u32[]{:S(2)}) collective-permute-start(f32[2,40,128]{2,1,0:T(8,128)S(1)} %pad_maximum_fusion.1), channel_id=1, source_target_pairs={{0,4},{1,5},{2,6},{3,7},{4,0},{5,1},{6,2},{7,3},{8,12},{9,13},{10,... | collective-permute-start | bytes 122888 | tf_op jit(solution)/shard_map/ppermute | solution.py:628
  20.3 6.5 %collective-permute-start.6 = (bf16[16,16,128]{2,1,0:T(8,128)(2,1)S(1)}, bf16[16,16,128]{2,1,0:T(8,128)(2,1)S(1)}, u32[]{:S(2)}, u32[]{:S(2)}) collective-permute-start(bf16[16,16,128]{2,1,0:T(8,128)(2,1)S(1)} %get-tuple-element.47), channel_id=1, source_target_pairs={{0,6},{1,7},{2,4},{3,5},{4,2},{5,3},{6,0},{7,1},{8,14},{9,15},{10,... | collective-permute-start | bytes 196616 | tf_op jit(solution)/shard_map/ppermute | solution.py:628
  22.1 4.7 %collective-permute-start.7 = (bf16[16,16,128]{2,1,0:T(8,128)(2,1)S(1)}, bf16[16,16,128]{2,1,0:T(8,128)(2,1)S(1)}, u32[]{:S(2)}, u32[]{:S(2)}) collective-permute-start(bf16[16,16,128]{2,1,0:T(8,128)(2,1)S(1)} %get-tuple-element.48), channel_id=1, source_target_pairs={{0,1},{1,0},{2,3},{3,2},{4,5},{5,4},{6,7},{7,6},{8,9},{9,8},{10,11... | collective-permute-start | bytes 196616 | tf_op jit(solution)/shard_map/ppermute | solution.py:628
  22.9 7.6 %collective-permute-start.8 = (bf16[16,16,128]{2,1,0:T(8,128)(2,1)S(1)}, bf16[16,16,128]{2,1,0:T(8,128)(2,1)S(1)}, u32[]{:S(2)}, u32[]{:S(2)}) collective-permute-start(bf16[16,16,128]{2,1,0:T(8,128)(2,1)S(1)} %get-tuple-element.49), channel_id=1, source_target_pairs={{0,7},{1,2},{2,1},{3,4},{4,3},{5,6},{6,5},{7,0},{8,15},{9,10},{10,... | collective-permute-start | bytes 196616 | tf_op jit(solution)/shard_map/ppermute | solution.py:628
  25.5 5.0 %collective-permute-start.9 = (bf16[16,16,128]{2,1,0:T(8,128)(2,1)S(1)}, bf16[16,16,128]{2,1,0:T(8,128)(2,1)S(1)}, u32[]{:S(2)}, u32[]{:S(2)}) collective-permute-start(bf16[16,16,128]{2,1,0:T(8,128)(2,1)S(1)} %get-tuple-element.50), channel_id=1, source_target_pairs={{0,2},{1,3},{2,0},{3,1},{4,6},{5,7},{6,4},{7,5},{8,10},{9,11},{10,... | collective-permute-start | bytes 196616 | tf_op jit(solution)/shard_map/ppermute | solution.py:628
  26.8 6.7 %copy-start.3 = (s32[8,128]{1,0:T(8,128)S(1)}, s32[8,128]{1,0:T(8,128)}, u32[]{:S(2)}) copy-start(s32[8,128]{1,0:T(8,128)} %get-tuple-element.61.place) | copy-start | bytes 12292
  30.5 8.3 %collective-permute-start.12 = (f32[4,40,128]{2,1,0:T(8,128)S(1)}, f32[4,40,128]{2,1,0:T(8,128)S(1)}, u32[]{:S(2)}, u32[]{:S(2)}) collective-permute-start(f32[4,40,128]{2,1,0:T(8,128)S(1)} %pad_maximum_fusion), channel_id=1, source_target_pairs={{0,1},{1,0},{2,3},{3,2},{4,5},{5,4},{6,7},{7,6},{8,9},{9,8},{10,11... | collective-permute-start | bytes 245768 | tf_op jit(solution)/shard_map/ppermute | solution.py:628
  31.2 7.7 %collective-permute-start.13 = (f32[4,40,128]{2,1,0:T(8,128)S(1)}, f32[4,40,128]{2,1,0:T(8,128)S(1)}, u32[]{:S(2)}, u32[]{:S(2)}) collective-permute-start(f32[4,40,128]{2,1,0:T(8,128)S(1)} %pad_maximum_fusion), channel_id=1, source_target_pairs={{0,16},{8,24},{16,0},{24,8},{1,17},{9,25},{17,1},{25,9},{2,18},{10... | collective-permute-start | bytes 245768 | tf_op jit(solution)/shard_map/ppermute | solution.py:628
  35.5 10.6 %all-to-all-start = ((f32[32,4,128]{2,1,0:T(4,128)}), f32[32,4,128]{2,1,0:T(4,128)S(1)}, u32[]{:S(2)}, u32[]{:S(2)}) async-start(f32[32,4,128]{2,1,0:T(4,128)} %get-tuple-element.65), calls=%async_computation | async-start | bytes 131072 | tf_op jit(solution)/shard_map/all_to_all | solution.py:691
  38.9 5.3 %collective-permute-start.15 = (f32[4,40,128]{2,1,0:T(8,128)S(1)}, f32[4,40,128]{2,1,0:T(8,128)S(1)}, u32[]{:S(2)}, u32[]{:S(2)}) collective-permute-start(f32[4,40,128]{2,1,0:T(8,128)S(1)} %pad_maximum_fusion), channel_id=1, source_target_pairs={{0,8},{8,0},{16,24},{24,16},{1,9},{9,1},{17,25},{25,17},{2,10},{10... | collective-permute-start | bytes 245768 | tf_op jit(solution)/shard_map/ppermute | solution.py:628
  39.2 4.9 %collective-permute-start.14 = (f32[4,40,128]{2,1,0:T(8,128)S(1)}, f32[4,40,128]{2,1,0:T(8,128)S(1)}, u32[]{:S(2)}, u32[]{:S(2)}) collective-permute-start(f32[4,40,128]{2,1,0:T(8,128)S(1)} %collective-permute-done.12), channel_id=1, source_target_pairs={{0,16},{8,24},{16,0},{24,8},{1,17},{9,25},{17,1},{25,9},{2,18},{10... | collective-permute-start | bytes 245768 | tf_op jit(solution)/shard_map/ppermute | solution.py:628
  40.9 3.3 %collective-permute-start.16 = (f32[4,40,128]{2,1,0:T(8,128)S(1)}, f32[4,40,128]{2,1,0:T(8,128)S(1)}, u32[]{:S(2)}, u32[]{:S(2)}) collective-permute-start(f32[4,40,128]{2,1,0:T(8,128)S(1)} %collective-permute-done.12), channel_id=1, source_target_pairs={{0,8},{8,0},{16,24},{24,16},{1,9},{9,1},{17,25},{25,17},{2,10},{10... | collective-permute-start | bytes 245768 | tf_op jit(solution)/shard_map/ppermute | solution.py:628
  40.9 3.3 %collective-permute-start.17 = (f32[4,40,128]{2,1,0:T(8,128)S(1)}, f32[4,40,128]{2,1,0:T(8,128)S(1)}, u32[]{:S(2)}, u32[]{:S(2)}) collective-permute-start(f32[4,40,128]{2,1,0:T(8,128)S(1)} %collective-permute-done.13), channel_id=1, source_target_pairs={{0,8},{8,0},{16,24},{24,16},{1,9},{9,1},{17,25},{25,17},{2,10},{10... | collective-permute-start | bytes 245768 | tf_op jit(solution)/shard_map/ppermute | solution.py:628
  44.1 1.3 %collective-permute-start.18 = (f32[4,40,128]{2,1,0:T(8,128)S(1)}, f32[4,40,128]{2,1,0:T(8,128)S(1)}, u32[]{:S(2)}, u32[]{:S(2)}) collective-permute-start(f32[4,40,128]{2,1,0:T(8,128)S(1)} %collective-permute-done.14), channel_id=1, source_target_pairs={{0,8},{8,0},{16,24},{24,16},{1,9},{9,1},{17,25},{25,17},{2,10},{10... | collective-permute-start | bytes 245768 | tf_op jit(solution)/shard_map/ppermute | solution.py:628

commit v8 on v7

--- a/solution.py
+++ b/solution.py
@@ -545,8 +545,11 @@
         for c in range(3):
             main, top = settle(sums[c])
             result.append((main + LAMBDA * vector[c][0], top + LAMBDA * vector[c][1]))
-        bent = sum(known[c][n] * sums[c][n] for c in range(3) for n in range(8))
-        return result, total(bent) + LAMBDA * inner(vector, vector)
+        terms = [known[c][n] * sums[c][n] for c in range(3) for n in range(8)]
+        terms += [LAMBDA * (part * part) for pair in vector for part in pair]
+        while len(terms) > 1:
+            terms = [sum(terms[i : i + 2]) for i in range(0, len(terms), 2)]
+        return result, total(terms[0])
 
     def total(value):
         return jnp.sum(jnp.sum(value, axis=0, keepdims=True), axis=1, keepdims=True)

time: 48.6 us -> 48.6 us (level)
  no operation moved by 1% of the time
where the time goes in v8:
time: 48.6 us; the launch traced here: 48.4 us
  starting transfers between devices  22.6 us (47%)
  waiting for transfers between devices  14.7 us (30%)
  Pallas kernels  10.1 us (21%)
  between operations  0.81 us (2%)
    ppermute x19, starting transfers between devices, swap(): lax.ppermute(array, axis, [(i, j) for i, j in pairs if 0 <= j < size])  19.3 us
    ppermute x19, waiting for transfers between devices, swap(): lax.ppermute(array, axis, [(i, j) for i, j in pairs if 0 <= j < size])  14 us
    all_to_all x1, starting transfers between devices, body(): load = lax.all_to_all(part, ('gx', 'gy'), 0, 0)  3.32 us
    pallas_call x1, Pallas kernels, solve(): pl.pallas_call(functools.partial(solve_kernel, gx_count, gy_count), out_s...  2.29 us
    pallas_call x1, Pallas kernels, ask(): pl.pallas_call(functools.partial(ask_kernel, lax.axis_size('gx')), out_sh...  2.14 us
    pallas_call x1, Pallas kernels, warp(): pl.pallas_call(warp_kernel, out_shape=(jax.ShapeDtypeStruct((NZ, EDGE, NY...  1.99 us
    pallas_call x1, Pallas kernels, serve(): pl.pallas_call(functools.partial(serve_kernel, lines), out_shape=(jax.Sha...  1.9 us
    pallas_call x1, Pallas kernels, moments(): pl.pallas_call(functools.partial(moments_kernel, lax.axis_size('gy')), ou...  1.75 us
  transfers between devices with their start and end apart: 20, of which 8 were waited for; matrix products, arithmetic and copies ran while one was open for 0% of the time, Pallas kernels for 12%

profile of v8, /device:TPU:0, one launch (start us, length us, event | category | flops | bytes accessed | tf_op | source)
XLA Modules:
  0.0 48.4 jit_solution(6737437392993275014)
XLA Ops:
  0.6 2.1 %ask.1 = (f32[16,128]{1,0:T(8,128)}, f32[16,128]{1,0:T(8,128)}, f32[8,128]{1,0:T(8,128)}, f32[8,128]{1,0:T(8,128)}, bf16[72,16,128]{2,1,0:T(8,128)(2,1)}, /*index=5*/f32[8,128]{1,0:T(8,128)}, s32[8,128]{1,0:T(8,128)}) custom-call(s32[1,32]{1,0:T(1,128)} %bitcast.8, s32[1,32]{1,0:T(1,128)} %bitcast.9, s32[1,32]{1,0:T(1,128)} %bitcast.10, ...), custom_call_target="tpu_custom_call" | custom-call | bytes 7380000 | tf_op jit(solution)/shard_map/ask/pallas_call | solution.py:162
  2.8 0.5 %collective-permute-start = (bf16[72,16,128]{2,1,0:T(8,128)(2,1)}, bf16[72,16,128]{2,1,0:T(8,128)(2,1)S(1)}, u32[]{:S(2)}, u32[]{:S(2)}) collective-permute-start(bf16[72,16,128]{2,1,0:T(8,128)(2,1)} %get-tuple-element.36), channel_id=1, source_target_pairs={{0,8},{8,0},{16,24},{24,16},{1,9},{9,1},{17,25},{25,17},{2,10},{10... | collective-permute-start | bytes 884744 | tf_op jit(solution)/shard_map/ppermute | solution.py:631
  3.3 0.7 %collective-permute-start.1 = (bf16[72,16,128]{2,1,0:T(8,128)(2,1)}, bf16[72,16,128]{2,1,0:T(8,128)(2,1)S(1)}, u32[]{:S(2)}, u32[]{:S(2)}) collective-permute-start(bf16[72,16,128]{2,1,0:T(8,128)(2,1)} %get-tuple-element.36), channel_id=1, source_target_pairs={{8,16},{16,8},{9,17},{17,9},{10,18},{18,10},{11,19},{19,11},{12,20... | collective-permute-start | bytes 884744 | tf_op jit(solution)/shard_map/ppermute | solution.py:631
  4.0 2.6 %collective-permute-start.3 = (f32[16,128]{1,0:T(8,128)}, f32[16,128]{1,0:T(8,128)S(1)}, u32[]{:S(2)}, u32[]{:S(2)}) collective-permute-start(f32[16,128]{1,0:T(8,128)} %get-tuple-element.38), channel_id=1, source_target_pairs={{0,1},{1,0},{2,3},{3,2},{4,5},{5,4},{6,7},{7,6},{8,9},{9,8},{10,11... | collective-permute-start | bytes 24584 | tf_op jit(solution)/shard_map/ppermute | solution.py:631
  6.5 3.6 %collective-permute-start.4 = (f32[16,128]{1,0:T(8,128)}, f32[16,128]{1,0:T(8,128)S(1)}, u32[]{:S(2)}, u32[]{:S(2)}) collective-permute-start(f32[16,128]{1,0:T(8,128)} %get-tuple-element.39), channel_id=1, source_target_pairs={{0,7},{1,2},{2,1},{3,4},{4,3},{5,6},{6,5},{7,0},{8,15},{9,10},{10,... | collective-permute-start | bytes 24584 | tf_op jit(solution)/shard_map/ppermute | solution.py:631
  10.1 0.4 collective-permute-start.2
  10.6 0.1 copy.9
  10.7 2.4 %collective-permute-done.4.r1.refs_5_ = f32[16,128]{1,0:T(8,128)S(1)} collective-permute-done((f32[16,128]{1,0:T(8,128)}, f32[16,128]{1,0:T(8,128)S(1)}, u32[]{:S(2)}, u32[]{:S(2)}) %collective-permute-start.4) | collective-permute-done | bytes 8224 | tf_op jit(solution)/shard_map/ppermute | solution.py:631
  13.1 0.0 copy-start.1
  13.1 1.7 %moments.1 = (bf16[3,64,16,128]{3,2,1,0:T(8,128)(2,1)S(1)}, f32[40,128]{1,0:T(8,128)S(1)}, f32[8,128]{1,0:T(8,128)S(1)}, f32[4,8,128]{2,1,0:T(8,128)S(1)}) custom-call(f32[16,128]{1,0:T(8,128)S(1)} %collective-permute-done.3.r0.refs_4_, f32[16,128]{1,0:T(8,128)S(1)} %collective-permute-done.4.r1.refs_5_, ...), custom_call_target="tpu_custom_call" | custom-call | bytes 8118000 | tf_op jit(solution)/shard_map/moments/pallas_call | solution.py:317
  14.9 0.9 %collective-permute-done.2.refs_3_ = f32[8,128]{1,0:T(8,128)S(1)} collective-permute-done((f32[8,128]{1,0:T(8,128)}, f32[8,128]{1,0:T(8,128)S(1)}, u32[]{:S(2)}, u32[]{:S(2)}) %collective-permute-start.2) | collective-permute-done | bytes 4128 | tf_op jit(solution)/shard_map/ppermute | solution.py:631
  15.8 1.9 %serve.1 = (bf16[16,16,128]{2,1,0:T(8,128)(2,1)S(1)}, bf16[16,16,128]{2,1,0:T(8,128)(2,1)S(1)}, bf16[16,16,128]{2,1,0:T(8,128)(2,1)S(1)}, bf16[16,16,128]{2,1,0:T(8,128)(2,1)S(1)}, bf16[16,16,128]{2,1,0:T(8,128)(2,1)S(1)}) custom-call(bf16[64,16,128]{2,1,0:T(8,128)(2,1)S(1)} %copy-done.1, bf16[72,16,128]{2,1,0:T(8,128)(2,1)S(1)} %collective-permute-done.a0.refs_1_, ...), custom_call_target="tpu_custom_call" | custom-call | bytes 7380000 | tf_op jit(solution)/shard_map/serve/pallas_call | solution.py:216
  17.7 1.9 %collective-permute-done.10 = f32[1,40,128]{2,1,0:T(8,128)S(1)} collective-permute-done((f32[1,40,128]{2,1,0:T(8,128)S(1)}, f32[1,40,128]{2,1,0:T(8,128)S(1)}, u32[]{:S(2)}, u32[]{:S(2)}) %collective-permute-start.10) | collective-permute-done | bytes 20512 | tf_op jit(solution)/shard_map/ppermute | solution.py:631
  19.6 0.7 %collective-permute-start.11 = (f32[2,40,128]{2,1,0:T(8,128)S(1)}, f32[2,40,128]{2,1,0:T(8,128)S(1)}, u32[]{:S(2)}, u32[]{:S(2)}) collective-permute-start(f32[2,40,128]{2,1,0:T(8,128)S(1)} %pad_maximum_fusion.1), channel_id=1, source_target_pairs={{0,4},{1,5},{2,6},{3,7},{4,0},{5,1},{6,2},{7,3},{8,12},{9,13},{10,... | collective-permute-start | bytes 122888 | tf_op jit(solution)/shard_map/ppermute | solution.py:631
  20.3 1.9 %collective-permute-start.6 = (bf16[16,16,128]{2,1,0:T(8,128)(2,1)S(1)}, bf16[16,16,128]{2,1,0:T(8,128)(2,1)S(1)}, u32[]{:S(2)}, u32[]{:S(2)}) collective-permute-start(bf16[16,16,128]{2,1,0:T(8,128)(2,1)S(1)} %get-tuple-element.47), channel_id=1, source_target_pairs={{0,6},{1,7},{2,4},{3,5},{4,2},{5,3},{6,0},{7,1},{8,14},{9,15},{10,... | collective-permute-start | bytes 196616 | tf_op jit(solution)/shard_map/ppermute | solution.py:631
  22.1 0.8 %collective-permute-start.7 = (bf16[16,16,128]{2,1,0:T(8,128)(2,1)S(1)}, bf16[16,16,128]{2,1,0:T(8,128)(2,1)S(1)}, u32[]{:S(2)}, u32[]{:S(2)}) collective-permute-start(bf16[16,16,128]{2,1,0:T(8,128)(2,1)S(1)} %get-tuple-element.48), channel_id=1, source_target_pairs={{0,1},{1,0},{2,3},{3,2},{4,5},{5,4},{6,7},{7,6},{8,9},{9,8},{10,11... | collective-permute-start | bytes 196616 | tf_op jit(solution)/shard_map/ppermute | solution.py:631
  22.9 2.6 %collective-permute-start.8 = (bf16[16,16,128]{2,1,0:T(8,128)(2,1)S(1)}, bf16[16,16,128]{2,1,0:T(8,128)(2,1)S(1)}, u32[]{:S(2)}, u32[]{:S(2)}) collective-permute-start(bf16[16,16,128]{2,1,0:T(8,128)(2,1)S(1)} %get-tuple-element.49), channel_id=1, source_target_pairs={{0,7},{1,2},{2,1},{3,4},{4,3},{5,6},{6,5},{7,0},{8,15},{9,10},{10,... | collective-permute-start | bytes 196616 | tf_op jit(solution)/shard_map/ppermute | solution.py:631
  25.5 0.1 collective-permute-start.9
  25.6 1.2 %collective-permute-done.11 = f32[2,40,128]{2,1,0:T(8,128)S(1)} collective-permute-done((f32[2,40,128]{2,1,0:T(8,128)S(1)}, f32[2,40,128]{2,1,0:T(8,128)S(1)}, u32[]{:S(2)}, u32[]{:S(2)}) %collective-permute-start.11) | collective-permute-done | bytes 40992 | tf_op jit(solution)/shard_map/ppermute | solution.py:631
  26.8 3.7 %collective-permute-done.8.b2 = bf16[16,16,128]{2,1,0:T(8,128)(2,1)S(1)} collective-permute-done((bf16[16,16,128]{2,1,0:T(8,128)(2,1)S(1)}, bf16[16,16,128]{2,1,0:T(8,128)(2,1)S(1)}, u32[]{:S(2)}, u32[]{:S(2)}) %collective-permute-start.8) | collective-permute-done | bytes 65568 | tf_op jit(solution)/shard_map/ppermute | solution.py:631
  30.5 0.6 %collective-permute-start.12 = (f32[4,40,128]{2,1,0:T(8,128)S(1)}, f32[4,40,128]{2,1,0:T(8,128)S(1)}, u32[]{:S(2)}, u32[]{:S(2)}) collective-permute-start(f32[4,40,128]{2,1,0:T(8,128)S(1)} %pad_maximum_fusion), channel_id=1, source_target_pairs={{0,1},{1,0},{2,3},{3,2},{4,5},{5,4},{6,7},{7,6},{8,9},{9,8},{10,11... | collective-permute-start | bytes 245768 | tf_op jit(solution)/shard_map/ppermute | solution.py:631
  31.2 2.3 %collective-permute-start.13 = (f32[4,40,128]{2,1,0:T(8,128)S(1)}, f32[4,40,128]{2,1,0:T(8,128)S(1)}, u32[]{:S(2)}, u32[]{:S(2)}) collective-permute-start(f32[4,40,128]{2,1,0:T(8,128)S(1)} %pad_maximum_fusion), channel_id=1, source_target_pairs={{0,16},{8,24},{16,0},{24,8},{1,17},{9,25},{17,1},{25,9},{2,18},{10... | collective-permute-start | bytes 245768 | tf_op jit(solution)/shard_map/ppermute | solution.py:631
  33.5 2.0 %warp.1 = (f32[64,16,128]{2,1,0:T(8,128)}, f32[32,4,128]{2,1,0:T(4,128)}) custom-call(bf16[16,16,128]{2,1,0:T(8,128)(2,1)S(1)} %collective-permute-done.6.b0, bf16[16,16,128]{2,1,0:T(8,128)(2,1)S(1)} %collective-permute-done.7.b1, bf16[16,16,128]{2,1,0:T(8,128)(2,1)S(1)} %collective-permute-done.8.b2, bf16[16,16,128]{2,1,0:T(8,128)(2,1)S(1)} %collective-permute-done.9.b3, ...), custom_call_target="tpu_custom_call" | custom-call | bytes 14760000 | tf_op jit(solution)/shard_map/warp/pallas_call | solution.py:402
  35.5 3.3 %all-to-all-start = ((f32[32,4,128]{2,1,0:T(4,128)}), f32[32,4,128]{2,1,0:T(4,128)S(1)}, u32[]{:S(2)}, u32[]{:S(2)}) async-start(f32[32,4,128]{2,1,0:T(4,128)} %get-tuple-element.65), calls=%async_computation | async-start | bytes 131072 | tf_op jit(solution)/shard_map/all_to_all | solution.py:694
  38.9 0.3 collective-permute-start.15
  39.2 1.7 %collective-permute-start.14 = (f32[4,40,128]{2,1,0:T(8,128)S(1)}, f32[4,40,128]{2,1,0:T(8,128)S(1)}, u32[]{:S(2)}, u32[]{:S(2)}) collective-permute-start(f32[4,40,128]{2,1,0:T(8,128)S(1)} %collective-permute-done.12), channel_id=1, source_target_pairs={{0,16},{8,24},{16,0},{24,8},{1,17},{9,25},{17,1},{25,9},{2,18},{10... | collective-permute-start | bytes 245768 | tf_op jit(solution)/shard_map/ppermute | solution.py:631
  40.9 0.1 collective-permute-start.16
  40.9 0.4 collective-permute-start.17
  41.4 2.7 %collective-permute-done.14 = f32[4,40,128]{2,1,0:T(8,128)S(1)} collective-permute-done((f32[4,40,128]{2,1,0:T(8,128)S(1)}, f32[4,40,128]{2,1,0:T(8,128)S(1)}, u32[]{:S(2)}, u32[]{:S(2)}) %collective-permute-start.14) | collective-permute-done | bytes 81952 | tf_op jit(solution)/shard_map/ppermute | solution.py:631
  44.2 1.2 %collective-permute-done.18 = f32[4,40,128]{2,1,0:T(8,128)S(1)} collective-permute-done((f32[4,40,128]{2,1,0:T(8,128)S(1)}, f32[4,40,128]{2,1,0:T(8,128)S(1)}, u32[]{:S(2)}, u32[]{:S(2)}) %collective-permute-start.18) | collective-permute-done | bytes 81952 | tf_op jit(solution)/shard_map/ppermute | solution.py:631
  45.4 0.7 %all-to-all-done.load = f32[32,4,128]{2,1,0:T(4,128)S(1)} async-done(((f32[32,4,128]{2,1,0:T(4,128)}), f32[32,4,128]{2,1,0:T(4,128)S(1)}, u32[]{:S(2)}, u32[]{:S(2)}) %all-to-all-start) | async-done | bytes 65568 | tf_op jit(solution)/shard_map/all_to_all | solution.py:694
  46.1 2.3 %solve.1 = f32[3,5,1,8]{3,2,1,0:T(1,128)} custom-call(f32[32,40,128]{2,1,0:T(8,128)S(1)} %constant_dynamic-update-slice_fusion.hess, f32[32,4,128]{2,1,0:T(4,128)S(1)} %all-to-all-done.load), custom_call_target="tpu_custom_call" | custom-call | bytes 12915000 | tf_op jit(solution)/shard_map/solve/pallas_call | solution.py:613
  (36 shorter events, 0.1 us)
Async XLA Ops:
  0.6 12.5 %copy-start = (bf16[64,16,128]{2,1,0:T(8,128)(2,1)S(1)}, bf16[64,16,128]{2,1,0:T(8,128)(2,1)}, u32[]{:S(2)}) copy-start(bf16[64,16,128]{2,1,0:T(8,128)(2,1)} %ref.5) | copy-start | bytes 786436
  2.8 7.8 %copy-start.5 = (f32[8,128]{1,0:T(8,128)S(1)}, f32[8,128]{1,0:T(8,128)}, u32[]{:S(2)}) copy-start(f32[8,128]{1,0:T(8,128)} %get-tuple-element.40) | copy-start | bytes 12292
  2.8 10.3 %collective-permute-start = (bf16[72,16,128]{2,1,0:T(8,128)(2,1)}, bf16[72,16,128]{2,1,0:T(8,128)(2,1)S(1)}, u32[]{:S(2)}, u32[]{:S(2)}) collective-permute-start(bf16[72,16,128]{2,1,0:T(8,128)(2,1)} %get-tuple-element.36), channel_id=1, source_target_pairs={{0,8},{8,0},{16,24},{24,16},{1,9},{9,1},{17,25},{25,17},{2,10},{10... | collective-permute-start | bytes 884744 | tf_op jit(solution)/shard_map/ppermute | solution.py:631
  3.3 9.8 %collective-permute-start.1 = (bf16[72,16,128]{2,1,0:T(8,128)(2,1)}, bf16[72,16,128]{2,1,0:T(8,128)(2,1)S(1)}, u32[]{:S(2)}, u32[]{:S(2)}) collective-permute-start(bf16[72,16,128]{2,1,0:T(8,128)(2,1)} %get-tuple-element.36), channel_id=1, source_target_pairs={{8,16},{16,8},{9,17},{17,9},{10,18},{18,10},{11,19},{19,11},{12,20... | collective-permute-start | bytes 884744 | tf_op jit(solution)/shard_map/ppermute | solution.py:631
  4.0 6.6 %collective-permute-start.3 = (f32[16,128]{1,0:T(8,128)}, f32[16,128]{1,0:T(8,128)S(1)}, u32[]{:S(2)}, u32[]{:S(2)}) collective-permute-start(f32[16,128]{1,0:T(8,128)} %get-tuple-element.38), channel_id=1, source_target_pairs={{0,1},{1,0},{2,3},{3,2},{4,5},{5,4},{6,7},{7,6},{8,9},{9,8},{10,11... | collective-permute-start | bytes 24584 | tf_op jit(solution)/shard_map/ppermute | solution.py:631
  6.5 4.0 %copy-start.4 = (s32[1,1,32,3]{2,1,3,0:T(1,128)S(1)}, s32[1,1,32,3]{2,1,3,0:T(1,128)}, u32[]{:S(2)}) copy-start(s32[1,1,32,3]{2,1,3,0:T(1,128)} %param.11) | copy-start | bytes 1156
  6.5 6.6 %collective-permute-start.4 = (f32[16,128]{1,0:T(8,128)}, f32[16,128]{1,0:T(8,128)S(1)}, u32[]{:S(2)}, u32[]{:S(2)}) collective-permute-start(f32[16,128]{1,0:T(8,128)} %get-tuple-element.39), channel_id=1, source_target_pairs={{0,7},{1,2},{2,1},{3,4},{4,3},{5,6},{6,5},{7,0},{8,15},{9,10},{10,... | collective-permute-start | bytes 24584 | tf_op jit(solution)/shard_map/ppermute | solution.py:631
  10.1 5.6 %collective-permute-start.2 = (f32[8,128]{1,0:T(8,128)}, f32[8,128]{1,0:T(8,128)S(1)}, u32[]{:S(2)}, u32[]{:S(2)}) collective-permute-start(f32[8,128]{1,0:T(8,128)} %get-tuple-element.37), channel_id=1, source_target_pairs={{0,6},{1,7},{2,4},{3,5},{4,2},{5,3},{6,0},{7,1},{8,14},{9,15},{10,... | collective-permute-start | bytes 12296 | tf_op jit(solution)/shard_map/ppermute | solution.py:631
  10.6 5.2 %collective-permute-start.5 = (f32[8,128]{1,0:T(8,128)S(1)}, f32[8,128]{1,0:T(8,128)S(1)}, u32[]{:S(2)}, u32[]{:S(2)}) collective-permute-start(f32[8,128]{1,0:T(8,128)S(1)} %copy-done.5), channel_id=1, source_target_pairs={{0,2},{1,3},{2,0},{3,1},{4,6},{5,7},{6,4},{7,5},{8,10},{9,11},{10,... | collective-permute-start | bytes 12296 | tf_op jit(solution)/shard_map/ppermute | solution.py:631
  13.1 2.6 %copy-start.1 = (bf16[64,16,128]{2,1,0:T(8,128)(2,1)S(1)}, bf16[64,16,128]{2,1,0:T(8,128)(2,1)}, u32[]{:S(2)}) copy-start(bf16[64,16,128]{2,1,0:T(8,128)(2,1)} %refs_0_.1) | copy-start | bytes 786436
  14.9 0.9 %copy-start.2 = (f32[8,128]{1,0:T(8,128)S(1)}, f32[8,128]{1,0:T(8,128)}, u32[]{:S(2)}) copy-start(f32[8,128]{1,0:T(8,128)} %get-tuple-element.46.refs_7_) | copy-start | bytes 12292
  15.7 3.8 %collective-permute-start.10 = (f32[1,40,128]{2,1,0:T(8,128)S(1)}, f32[1,40,128]{2,1,0:T(8,128)S(1)}, u32[]{:S(2)}, u32[]{:S(2)}) collective-permute-start(f32[1,40,128]{2,1,0:T(8,128)S(1)} %bitcast.6), channel_id=1, source_target_pairs={{0,2},{1,3},{2,0},{3,1},{4,6},{5,7},{6,4},{7,5},{8,10},{9,11},{10,... | collective-permute-start | bytes 61448 | tf_op jit(solution)/shard_map/ppermute | solution.py:631
  19.6 7.2 %collective-permute-start.11 = (f32[2,40,128]{2,1,0:T(8,128)S(1)}, f32[2,40,128]{2,1,0:T(8,128)S(1)}, u32[]{:S(2)}, u32[]{:S(2)}) collective-permute-start(f32[2,40,128]{2,1,0:T(8,128)S(1)} %pad_maximum_fusion.1), channel_id=1, source_target_pairs={{0,4},{1,5},{2,6},{3,7},{4,0},{5,1},{6,2},{7,3},{8,12},{9,13},{10,... | collective-permute-start | bytes 122888 | tf_op jit(solution)/shard_map/ppermute | solution.py:631
  20.3 6.5 %collective-permute-start.6 = (bf16[16,16,128]{2,1,0:T(8,128)(2,1)S(1)}, bf16[16,16,128]{2,1,0:T(8,128)(2,1)S(1)}, u32[]{:S(2)}, u32[]{:S(2)}) collective-permute-start(bf16[16,16,128]{2,1,0:T(8,128)(2,1)S(1)} %get-tuple-element.47), channel_id=1, source_target_pairs={{0,6},{1,7},{2,4},{3,5},{4,2},{5,3},{6,0},{7,1},{8,14},{9,15},{10,... | collective-permute-start | bytes 196616 | tf_op jit(solution)/shard_map/ppermute | solution.py:631
  22.1 4.7 %collective-permute-start.7 = (bf16[16,16,128]{2,1,0:T(8,128)(2,1)S(1)}, bf16[16,16,128]{2,1,0:T(8,128)(2,1)S(1)}, u32[]{:S(2)}, u32[]{:S(2)}) collective-permute-start(bf16[16,16,128]{2,1,0:T(8,128)(2,1)S(1)} %get-tuple-element.48), channel_id=1, source_target_pairs={{0,1},{1,0},{2,3},{3,2},{4,5},{5,4},{6,7},{7,6},{8,9},{9,8},{10,11... | collective-permute-start | bytes 196616 | tf_op jit(solution)/shard_map/ppermute | solution.py:631
  22.9 7.6 %collective-permute-start.8 = (bf16[16,16,128]{2,1,0:T(8,128)(2,1)S(1)}, bf16[16,16,128]{2,1,0:T(8,128)(2,1)S(1)}, u32[]{:S(2)}, u32[]{:S(2)}) collective-permute-start(bf16[16,16,128]{2,1,0:T(8,128)(2,1)S(1)} %get-tuple-element.49), channel_id=1, source_target_pairs={{0,7},{1,2},{2,1},{3,4},{4,3},{5,6},{6,5},{7,0},{8,15},{9,10},{10,... | collective-permute-start | bytes 196616 | tf_op jit(solution)/shard_map/ppermute | solution.py:631
  25.5 5.0 %collective-permute-start.9 = (bf16[16,16,128]{2,1,0:T(8,128)(2,1)S(1)}, bf16[16,16,128]{2,1,0:T(8,128)(2,1)S(1)}, u32[]{:S(2)}, u32[]{:S(2)}) collective-permute-start(bf16[16,16,128]{2,1,0:T(8,128)(2,1)S(1)} %get-tuple-element.50), channel_id=1, source_target_pairs={{0,2},{1,3},{2,0},{3,1},{4,6},{5,7},{6,4},{7,5},{8,10},{9,11},{10,... | collective-permute-start | bytes 196616 | tf_op jit(solution)/shard_map/ppermute | solution.py:631
  26.8 6.7 %copy-start.3 = (s32[8,128]{1,0:T(8,128)S(1)}, s32[8,128]{1,0:T(8,128)}, u32[]{:S(2)}) copy-start(s32[8,128]{1,0:T(8,128)} %get-tuple-element.61.place) | copy-start | bytes 12292
  30.5 8.3 %collective-permute-start.12 = (f32[4,40,128]{2,1,0:T(8,128)S(1)}, f32[4,40,128]{2,1,0:T(8,128)S(1)}, u32[]{:S(2)}, u32[]{:S(2)}) collective-permute-start(f32[4,40,128]{2,1,0:T(8,128)S(1)} %pad_maximum_fusion), channel_id=1, source_target_pairs={{0,1},{1,0},{2,3},{3,2},{4,5},{5,4},{6,7},{7,6},{8,9},{9,8},{10,11... | collective-permute-start | bytes 245768 | tf_op jit(solution)/shard_map/ppermute | solution.py:631
  31.2 7.7 %collective-permute-start.13 = (f32[4,40,128]{2,1,0:T(8,128)S(1)}, f32[4,40,128]{2,1,0:T(8,128)S(1)}, u32[]{:S(2)}, u32[]{:S(2)}) collective-permute-start(f32[4,40,128]{2,1,0:T(8,128)S(1)} %pad_maximum_fusion), channel_id=1, source_target_pairs={{0,16},{8,24},{16,0},{24,8},{1,17},{9,25},{17,1},{25,9},{2,18},{10... | collective-permute-start | bytes 245768 | tf_op jit(solution)/shard_map/ppermute | solution.py:631
  35.5 10.6 %all-to-all-start = ((f32[32,4,128]{2,1,0:T(4,128)}), f32[32,4,128]{2,1,0:T(4,128)S(1)}, u32[]{:S(2)}, u32[]{:S(2)}) async-start(f32[32,4,128]{2,1,0:T(4,128)} %get-tuple-element.65), calls=%async_computation | async-start | bytes 131072 | tf_op jit(solution)/shard_map/all_to_all | solution.py:694
  38.9 5.3 %collective-permute-start.15 = (f32[4,40,128]{2,1,0:T(8,128)S(1)}, f32[4,40,128]{2,1,0:T(8,128)S(1)}, u32[]{:S(2)}, u32[]{:S(2)}) collective-permute-start(f32[4,40,128]{2,1,0:T(8,128)S(1)} %pad_maximum_fusion), channel_id=1, source_target_pairs={{0,8},{8,0},{16,24},{24,16},{1,9},{9,1},{17,25},{25,17},{2,10},{10... | collective-permute-start | bytes 245768 | tf_op jit(solution)/shard_map/ppermute | solution.py:631
  39.2 4.9 %collective-permute-start.14 = (f32[4,40,128]{2,1,0:T(8,128)S(1)}, f32[4,40,128]{2,1,0:T(8,128)S(1)}, u32[]{:S(2)}, u32[]{:S(2)}) collective-permute-start(f32[4,40,128]{2,1,0:T(8,128)S(1)} %collective-permute-done.12), channel_id=1, source_target_pairs={{0,16},{8,24},{16,0},{24,8},{1,17},{9,25},{17,1},{25,9},{2,18},{10... | collective-permute-start | bytes 245768 | tf_op jit(solution)/shard_map/ppermute | solution.py:631
  40.9 3.3 %collective-permute-start.16 = (f32[4,40,128]{2,1,0:T(8,128)S(1)}, f32[4,40,128]{2,1,0:T(8,128)S(1)}, u32[]{:S(2)}, u32[]{:S(2)}) collective-permute-start(f32[4,40,128]{2,1,0:T(8,128)S(1)} %collective-permute-done.12), channel_id=1, source_target_pairs={{0,8},{8,0},{16,24},{24,16},{1,9},{9,1},{17,25},{25,17},{2,10},{10... | collective-permute-start | bytes 245768 | tf_op jit(solution)/shard_map/ppermute | solution.py:631
  40.9 3.3 %collective-permute-start.17 = (f32[4,40,128]{2,1,0:T(8,128)S(1)}, f32[4,40,128]{2,1,0:T(8,128)S(1)}, u32[]{:S(2)}, u32[]{:S(2)}) collective-permute-start(f32[4,40,128]{2,1,0:T(8,128)S(1)} %collective-permute-done.13), channel_id=1, source_target_pairs={{0,8},{8,0},{16,24},{24,16},{1,9},{9,1},{17,25},{25,17},{2,10},{10... | collective-permute-start | bytes 245768 | tf_op jit(solution)/shard_map/ppermute | solution.py:631
  44.1 1.3 %collective-permute-start.18 = (f32[4,40,128]{2,1,0:T(8,128)S(1)}, f32[4,40,128]{2,1,0:T(8,128)S(1)}, u32[]{:S(2)}, u32[]{:S(2)}) collective-permute-start(f32[4,40,128]{2,1,0:T(8,128)S(1)} %collective-permute-done.14), channel_id=1, source_target_pairs={{0,8},{8,0},{16,24},{24,16},{1,9},{9,1},{17,25},{25,17},{2,10},{10... | collective-permute-start | bytes 245768 | tf_op jit(solution)/shard_map/ppermute | solution.py:631
